TPU v7x, 32 devices: a whole 2x2x4 slice. The times are simulated.
32 devices in a mesh: rows: 16 (over z, x, core), seq: 2 (over y).
Axes of the slice: x: 2, y: 2, z: 4, core: 2. Of those that a mesh axis runs over, the one named last changes fastest.
Arguments:
- target_states: bfloat16 [16, 1024, 512], P('rows', 'seq'), may hold values from -6 to 6
- source_states: bfloat16 [16, 336, 512], P('rows', 'seq'), may hold values from -6 to 6
- target_segments: int32 [16, 1024], P('rows'), may hold values from 0 to 8, as said below
- source_segments: int32 [16, 336], P('rows'), may hold values from 0 to 9, as said below
- output_grad: bfloat16 [16, 1024, 512], P('rows', 'seq'), may hold values from -6 to 6
- self_project: bfloat16 [512, 1536], P(('rows', 'seq')), may hold values from -0.25 to 0.25
- self_output: bfloat16 [512, 512], P(('rows', 'seq')), may hold values from -1 to 1
- cross_query: bfloat16 [512, 512], P(('rows', 'seq')), may hold values from -0.25 to 0.25
- cross_keyval: bfloat16 [512, 1024], P(('rows', 'seq')), may hold values from -0.25 to 0.25
- cross_output: bfloat16 [512, 512], P(('rows', 'seq')), may hold values from -1 to 1
- hidden_up: bfloat16 [512, 2048], P(('rows', 'seq')), may hold values from -0.25 to 0.25
- hidden_bias: bfloat16 [2048], P(('rows', 'seq')), may hold values from -3 to 3
- hidden_down: bfloat16 [2048, 512], P(('rows', 'seq')), may hold values from -0.25 to 0.25
- output_bias: bfloat16 [512], P(('rows', 'seq')), may hold values from -3 to 3
- first_gain: bfloat16 [512], P(('rows', 'seq')), may hold values from 0.25 to 1.75
- first_shift: bfloat16 [512], P(('rows', 'seq')), may hold values from -3 to 3
- second_gain: bfloat16 [512], P(('rows', 'seq')), may hold values from 0.25 to 1.75
- second_shift: bfloat16 [512], P(('rows', 'seq')), may hold values from -3 to 3
- third_gain: bfloat16 [512], P(('rows', 'seq')), may hold values from 0.25 to 1.75
- third_shift: bfloat16 [512], P(('rows', 'seq')), may hold values from -3 to 3
Outputs:
- layer_output: bfloat16 [16, 1024, 512], P('rows', 'seq')
- grad_target: float32 [16, 1024, 512], P('rows', 'seq')
- grad_source: float32 [16, 336, 512], P('rows', 'seq')
- grad_self_project: float32 [512, 1536], P(('rows', 'seq'))
- grad_self_output: float32 [512, 512], P(('rows', 'seq'))
- grad_cross_query: float32 [512, 512], P(('rows', 'seq'))
- grad_cross_keyval: float32 [512, 1024], P(('rows', 'seq'))
- grad_cross_output: float32 [512, 512], P(('rows', 'seq'))
- grad_hidden_up: float32 [512, 2048], P(('rows', 'seq'))
- grad_hidden_bias: float32 [2048], P(('rows', 'seq'))
- grad_hidden_down: float32 [2048, 512], P(('rows', 'seq'))
- grad_output_bias: float32 [512], P(('rows', 'seq'))
- grad_first_gain: float32 [512], P(('rows', 'seq'))
- grad_first_shift: float32 [512], P(('rows', 'seq'))
- grad_second_gain: float32 [512], P(('rows', 'seq'))
- grad_second_shift: float32 [512], P(('rows', 'seq'))
- grad_third_gain: float32 [512], P(('rows', 'seq'))
- grad_third_shift: float32 [512], P(('rows', 'seq'))
Inputs may be any that keep to these rules, and one draw needn't show every extreme that they name: `target_segments`: in each row the numbers 0 to 8 rise along the positions, each used. Sentences 0 to 3 and 5 to 8 each hold 64 to 127 positions; sentence 4 begins within the first 512 positions and ends within the last 512. `source_segments`: in each row the numbers 0 to 9 rise along the positions, each used; each sentence's source positions are roughly in proportion to its target positions, and 9 marks padding at the end of the row.
All inputs are finite; a program needn't handle non-finite values.
Results may differ from a plain program's by a relative error of at most 0.024.
Values may be sent and summed in bfloat16 or wider, within the bound.
No kernel may reach another device: no remote copies, remote signals or barrier semaphores. Data moves between devices by JAX's collectives and lax.ppermute only.
A program may use at most 256 MiB of HBM per device.

v0:
```python
import jax
import jax.numpy as jnp
from jax import lax
from jax.sharding import PartitionSpec as P

HEADS = 8
HD = 64


def layer_norm(value, gain, shift):
    row_mean = jnp.mean(value, -1, keepdims=True)
    centered = value - row_mean
    variance = jnp.mean(centered * centered, -1, keepdims=True)
    inverse = lax.rsqrt(variance + 1e-05)
    normed = centered * inverse
    return (normed * gain + shift, normed, inverse)


def norm_back(upstream, normed, inverse, gain):
    scaled = upstream * gain
    first_mean = jnp.mean(scaled, -1, keepdims=True)
    second_mean = jnp.mean(scaled * normed, -1, keepdims=True)
    grad_input = inverse * (scaled - first_mean - normed * second_mean)
    return (grad_input, jnp.sum(upstream * normed, 0), jnp.sum(upstream, 0))


def matmul(left, right):
    return jnp.dot(left, right, preferred_element_type=jnp.float32)


def transposed(left, right):
    return lax.dot_general(
        left, right, (((0,), (0,)), ((), ())), preferred_element_type=jnp.float32
    )


def against(left, right):
    return lax.dot_general(
        left, right, (((1,), (1,)), ((), ())), preferred_element_type=jnp.float32
    )


def head_split(value):
    return value.reshape(value.shape[0], HEADS, HD)


def head_join(value):
    return value.reshape(value.shape[0], HEADS * HD)


def scores_of(queries, key_rows, query_seg, key_seg):
    raw_scores = jnp.einsum(
        "qhd,khd->hqk", queries, key_rows, preferred_element_type=jnp.float32
    ) * HD ** (-0.5)
    same_seg = (query_seg[:, None] == key_seg[None, :])[None]
    return (raw_scores, same_seg)


def block_weights(queries, key_rows, query_seg, key_seg, log_total):
    raw_scores, same_seg = scores_of(queries, key_rows, query_seg, key_seg)
    return jnp.where(same_seg, jnp.exp(raw_scores - log_total[..., None]), 0.0)


def log_totals(queries, key_blocks, seg_blocks, query_seg):

    def log_advance(carry, inputs_now):
        row_max, row_total = carry
        key_rows, key_seg = inputs_now
        raw_scores, same_seg = scores_of(queries, key_rows, query_seg, key_seg)
        masked = jnp.where(same_seg, raw_scores, -1000000000.0)
        new_max = jnp.maximum(row_max, jnp.max(masked, -1))
        shifted = jnp.where(same_seg, jnp.exp(masked - new_max[..., None]), 0.0)
        return ((new_max, row_total * jnp.exp(row_max - new_max) + jnp.sum(shifted, -1)), None)

    start = (
        jnp.full((HEADS, queries.shape[0]), -1000000000.0, jnp.float32),
        jnp.zeros((HEADS, queries.shape[0]), jnp.float32),
    )
    (row_max, row_total), unused = lax.scan(log_advance, start, (key_blocks, seg_blocks))
    return row_max + jnp.log(row_total)


def weighted_sum(queries, key_blocks, value_blocks, seg_blocks, query_seg, log_total):

    def weighted_advance(carry, inputs_now):
        key_rows, value_rows, key_seg = inputs_now
        weights = block_weights(queries, key_rows, query_seg, key_seg, log_total).astype(
            jnp.bfloat16
        )
        return (
            carry
            + jnp.einsum("hqk,khd->qhd", weights, value_rows, preferred_element_type=jnp.float32),
            None,
        )

    total, unused = lax.scan(
        weighted_advance,
        jnp.zeros(queries.shape, jnp.float32),
        (key_blocks, value_blocks, seg_blocks),
    )
    return total


def grad_dots(queries, grad_heads, key_blocks, value_blocks, seg_blocks, query_seg, log_total):

    def grad_advance(carry, inputs_now):
        key_rows, value_rows, key_seg = inputs_now
        weights = block_weights(queries, key_rows, query_seg, key_seg, log_total)
        grad_weights = jnp.einsum(
            "qhd,khd->hqk", grad_heads, value_rows, preferred_element_type=jnp.float32
        )
        return (carry + jnp.sum(weights * grad_weights, -1), None)

    start = jnp.zeros((HEADS, queries.shape[0]), jnp.float32)
    total, unused = lax.scan(grad_advance, start, (key_blocks, value_blocks, seg_blocks))
    return total


def query_grads(
    queries, grad_heads, key_blocks, value_blocks, seg_blocks, query_seg, log_total, row_dots
):
    score_scale = HD ** (-0.5)

    def query_advance(carry, inputs_now):
        key_rows, value_rows, key_seg = inputs_now
        weights = block_weights(queries, key_rows, query_seg, key_seg, log_total)
        grad_weights = jnp.einsum(
            "qhd,khd->hqk", grad_heads, value_rows, preferred_element_type=jnp.float32
        )
        grad_scores = (weights * (grad_weights - row_dots[..., None])).astype(jnp.bfloat16)
        carry = (
            carry
            + jnp.einsum("hqk,khd->qhd", grad_scores, key_rows, preferred_element_type=jnp.float32)
            * score_scale
        )
        grad_keys = (
            jnp.einsum("hqk,qhd->khd", grad_scores, queries, preferred_element_type=jnp.float32)
            * score_scale
        )
        grad_values = jnp.einsum(
            "hqk,qhd->khd",
            weights.astype(jnp.bfloat16),
            grad_heads,
            preferred_element_type=jnp.float32,
        )
        return (carry, jnp.concatenate([head_join(grad_keys), head_join(grad_values)], 1))

    return lax.scan(
        query_advance, jnp.zeros(queries.shape, jnp.float32), (key_blocks, value_blocks, seg_blocks)
    )


def per_device(
    target_states,
    source_states,
    target_segments,
    source_segments,
    output_grad,
    self_project,
    self_output,
    cross_query,
    cross_keyval,
    cross_output,
    hidden_up,
    hidden_bias,
    hidden_down,
    output_bias,
    first_gain,
    first_shift,
    second_gain,
    second_shift,
    third_gain,
    third_shift,
):
    (
        full_project,
        full_output,
        full_query,
        full_keyval,
        full_crossout,
        full_up,
        full_upbias,
        full_down,
        full_downbias,
        gain_one,
        shift_one,
        gain_two,
        shift_two,
        gain_three,
        shift_three,
    ) = (
        lax.all_gather(self_project, ("rows", "seq"), axis=0, tiled=True),
        lax.all_gather(self_output, ("rows", "seq"), axis=0, tiled=True),
        lax.all_gather(cross_query, ("rows", "seq"), axis=0, tiled=True),
        lax.all_gather(cross_keyval, ("rows", "seq"), axis=0, tiled=True),
        lax.all_gather(cross_output, ("rows", "seq"), axis=0, tiled=True),
        lax.all_gather(hidden_up, ("rows", "seq"), axis=0, tiled=True),
        lax.all_gather(hidden_bias, ("rows", "seq"), axis=0, tiled=True),
        lax.all_gather(hidden_down, ("rows", "seq"), axis=0, tiled=True),
        lax.all_gather(output_bias, ("rows", "seq"), axis=0, tiled=True),
        lax.all_gather(first_gain, ("rows", "seq"), axis=0, tiled=True),
        lax.all_gather(first_shift, ("rows", "seq"), axis=0, tiled=True),
        lax.all_gather(second_gain, ("rows", "seq"), axis=0, tiled=True),
        lax.all_gather(second_shift, ("rows", "seq"), axis=0, tiled=True),
        lax.all_gather(third_gain, ("rows", "seq"), axis=0, tiled=True),
        lax.all_gather(third_shift, ("rows", "seq"), axis=0, tiled=True),
    )
    gain_one = gain_one.astype(jnp.float32)
    gain_two = gain_two.astype(jnp.float32)
    gain_three = gain_three.astype(jnp.float32)
    score_scale = HD ** (-0.5)
    states = target_states[0].astype(jnp.float32)
    local_rows = states.shape[0]
    model_width = states.shape[1]
    seq_count = lax.axis_size("seq")
    row_segments = target_segments[0]
    seq_length = row_segments.shape[0]
    own_segments = lax.dynamic_slice_in_dim(
        row_segments, lax.axis_index("seq") * local_rows, local_rows
    )
    block_rows = max(1, min(seq_count, 512 // local_rows)) * local_rows
    block_count = seq_length // block_rows
    seg_blocks = row_segments.reshape(block_count, block_rows)
    normed_value, normed_one, inverse_one = layer_norm(
        states, gain_one, shift_one.astype(jnp.float32)
    )
    lowered_one = normed_value.astype(jnp.bfloat16)
    projected = matmul(lowered_one, full_project).astype(jnp.bfloat16)
    query_flat = projected[:, :model_width]
    key_local = projected[:, model_width : 2 * model_width]
    value_local = projected[:, 2 * model_width :]
    queries = head_split(query_flat)
    key_all, value_all = (
        lax.all_gather(key_local, "seq", axis=0, tiled=True),
        lax.all_gather(value_local, "seq", axis=0, tiled=True),
    )
    key_blocks = key_all.reshape(block_count, block_rows, HEADS, HD)
    value_blocks = value_all.reshape(block_count, block_rows, HEADS, HD)
    log_total = log_totals(queries, key_blocks, seg_blocks, own_segments)
    self_mixed = head_join(
        weighted_sum(queries, key_blocks, value_blocks, seg_blocks, own_segments, log_total)
    ).astype(jnp.bfloat16)
    after_self = states + matmul(self_mixed, full_output)
    normed_value, normed_two, inverse_two = layer_norm(
        after_self, gain_two, shift_two.astype(jnp.float32)
    )
    lowered_two = normed_value.astype(jnp.bfloat16)
    cross_asked = matmul(lowered_two, full_query).astype(jnp.bfloat16)
    source_low = source_states[0]
    source_all = lax.all_gather(source_low, "seq", axis=0, tiled=True)
    key_value = matmul(source_all, full_keyval).astype(jnp.bfloat16)
    cross_key_heads = head_split(key_value[:, :model_width])
    cross_value_heads = head_split(key_value[:, model_width:])
    asked_heads = head_split(cross_asked)
    raw_scores, same_seg = scores_of(asked_heads, cross_key_heads, own_segments, source_segments[0])
    cross_probs = jax.nn.softmax(jnp.where(same_seg, raw_scores, -1000000000.0), axis=-1)
    cross_mixed = head_join(
        jnp.einsum(
            "hqk,khd->qhd",
            cross_probs.astype(jnp.bfloat16),
            cross_value_heads,
            preferred_element_type=jnp.float32,
        )
    ).astype(jnp.bfloat16)
    after_cross = after_self + matmul(cross_mixed, full_crossout)
    normed_value, normed_three, inverse_three = layer_norm(
        after_cross, gain_three, shift_three.astype(jnp.float32)
    )
    lowered_three = normed_value.astype(jnp.bfloat16)
    hidden = matmul(lowered_three, full_up) + full_upbias.astype(jnp.float32)
    activated = jax.nn.gelu(hidden).astype(jnp.bfloat16)
    layer_out = after_cross + matmul(activated, full_down) + full_downbias.astype(jnp.float32)
    grad_low = output_grad[0]
    out_grad = grad_low.astype(jnp.float32)
    grad_down = transposed(activated, grad_low)
    grad_downbias = jnp.sum(out_grad, 0)
    grad_act = against(grad_low, full_down)
    grad_hidden = jax.vjp(jax.nn.gelu, hidden)[1](grad_act)[0].astype(jnp.bfloat16)
    grad_upbias = jnp.sum(grad_hidden.astype(jnp.float32), 0)
    grad_up = transposed(lowered_three, grad_hidden)
    dx_three, grad_gain_three, grad_shift_three = norm_back(
        against(grad_hidden, full_up), normed_three, inverse_three, gain_three
    )
    grad_cross = out_grad + dx_three
    grad_cross_low = grad_cross.astype(jnp.bfloat16)
    grad_crossout = transposed(cross_mixed, grad_cross_low)
    grad_cross_heads = head_split(against(grad_cross_low, full_crossout).astype(jnp.bfloat16))
    grad_weights = jnp.einsum(
        "qhd,khd->hqk", grad_cross_heads, cross_value_heads, preferred_element_type=jnp.float32
    )
    grad_scores = (
        cross_probs * (grad_weights - jnp.sum(cross_probs * grad_weights, -1, keepdims=True))
    ).astype(jnp.bfloat16)
    grad_asked = head_join(
        jnp.einsum("hqk,khd->qhd", grad_scores, cross_key_heads, preferred_element_type=jnp.float32)
        * score_scale
    ).astype(jnp.bfloat16)
    grad_cross_keys = (
        jnp.einsum("hqk,qhd->khd", grad_scores, asked_heads, preferred_element_type=jnp.float32)
        * score_scale
    )
    grad_cross_values = jnp.einsum(
        "hqk,qhd->khd",
        cross_probs.astype(jnp.bfloat16),
        grad_cross_heads,
        preferred_element_type=jnp.float32,
    )
    pair_terms = jnp.concatenate([head_join(grad_cross_keys), head_join(grad_cross_values)], 1)
    pair_grad = lax.psum_scatter(
        pair_terms.astype(jnp.bfloat16), "seq", scatter_dimension=0, tiled=True
    )
    grad_keyval = transposed(source_low, pair_grad)
    grad_source = against(pair_grad, full_keyval)
    grad_query = transposed(lowered_two, grad_asked)
    dx_two, grad_gain_two, grad_shift_two = norm_back(
        against(grad_asked, full_query), normed_two, inverse_two, gain_two
    )
    grad_self = grad_cross + dx_two
    grad_self_low = grad_self.astype(jnp.bfloat16)
    grad_output = transposed(self_mixed, grad_self_low)
    grad_mixed = against(grad_self_low, full_output).astype(jnp.bfloat16)
    grad_heads = head_split(grad_mixed)
    row_dots = grad_dots(
        queries, grad_heads, key_blocks, value_blocks, seg_blocks, own_segments, log_total
    )
    grad_queries, key_terms = query_grads(
        queries, grad_heads, key_blocks, value_blocks, seg_blocks, own_segments, log_total, row_dots
    )
    summed = lax.psum_scatter(
        key_terms.reshape(seq_length, 2 * model_width).astype(jnp.bfloat16),
        "seq",
        scatter_dimension=0,
        tiled=True,
    )
    grad_projected = jnp.concatenate([head_join(grad_queries).astype(jnp.bfloat16), summed], 1)
    grad_project = transposed(lowered_one, grad_projected)
    dx_one, grad_gain_one, grad_shift_one = norm_back(
        against(grad_projected, full_project), normed_one, inverse_one, gain_one
    )
    grad_target = grad_self + dx_one
    shards = (
        lax.psum_scatter(grad_project, ("rows", "seq"), scatter_dimension=0, tiled=True),
        lax.psum_scatter(grad_output, ("rows", "seq"), scatter_dimension=0, tiled=True),
        lax.psum_scatter(grad_query, ("rows", "seq"), scatter_dimension=0, tiled=True),
        lax.psum_scatter(grad_keyval, ("rows", "seq"), scatter_dimension=0, tiled=True),
        lax.psum_scatter(grad_crossout, ("rows", "seq"), scatter_dimension=0, tiled=True),
        lax.psum_scatter(grad_up, ("rows", "seq"), scatter_dimension=0, tiled=True),
        lax.psum_scatter(grad_upbias, ("rows", "seq"), scatter_dimension=0, tiled=True),
        lax.psum_scatter(grad_down, ("rows", "seq"), scatter_dimension=0, tiled=True),
        lax.psum_scatter(grad_downbias, ("rows", "seq"), scatter_dimension=0, tiled=True),
        lax.psum_scatter(grad_gain_one, ("rows", "seq"), scatter_dimension=0, tiled=True),
        lax.psum_scatter(grad_shift_one, ("rows", "seq"), scatter_dimension=0, tiled=True),
        lax.psum_scatter(grad_gain_two, ("rows", "seq"), scatter_dimension=0, tiled=True),
        lax.psum_scatter(grad_shift_two, ("rows", "seq"), scatter_dimension=0, tiled=True),
        lax.psum_scatter(grad_gain_three, ("rows", "seq"), scatter_dimension=0, tiled=True),
        lax.psum_scatter(grad_shift_three, ("rows", "seq"), scatter_dimension=0, tiled=True),
    )
    return (layer_out.astype(jnp.bfloat16)[None], grad_target[None], grad_source[None]) + tuple(
        shards
    )


def solution(mesh):
    in_specs = (
        P("rows", "seq", None),
        P("rows", "seq", None),
        P("rows", None),
        P("rows", None),
        P("rows", "seq", None),
        P(("rows", "seq"), None),
        P(("rows", "seq"), None),
        P(("rows", "seq"), None),
        P(("rows", "seq"), None),
        P(("rows", "seq"), None),
        P(("rows", "seq"), None),
        P(("rows", "seq")),
        P(("rows", "seq"), None),
        P(("rows", "seq")),
        P(("rows", "seq")),
        P(("rows", "seq")),
        P(("rows", "seq")),
        P(("rows", "seq")),
        P(("rows", "seq")),
        P(("rows", "seq")),
    )
    out_specs = (
        P("rows", "seq", None),
        P("rows", "seq", None),
        P("rows", "seq", None),
        P(("rows", "seq"), None),
        P(("rows", "seq"), None),
        P(("rows", "seq"), None),
        P(("rows", "seq"), None),
        P(("rows", "seq"), None),
        P(("rows", "seq"), None),
        P(("rows", "seq")),
        P(("rows", "seq"), None),
        P(("rows", "seq")),
        P(("rows", "seq")),
        P(("rows", "seq")),
        P(("rows", "seq")),
        P(("rows", "seq")),
        P(("rows", "seq")),
        P(("rows", "seq")),
    )
    return jax.shard_map(
        per_device, mesh=mesh, in_specs=in_specs, out_specs=out_specs, check_vma=False
    )
```

profile of v0, /device:TPU:0, one launch (start us, length us, event | category | flops | bytes accessed | tf_op | source)
XLA Modules:
  0.0 1403.9 jit_solution(13623278830762067236)
XLA Ops:
  15.5 42.2 %all-reduce.17 = (bf16[512]{0:T(512)(128)(2,1)S(1)}, bf16[512]{0:T(512)(128)(2,1)S(1)}, bf16[512]{0:T(512)(128)(2,1)S(1)}, bf16[512]{0:T(512)(128)(2,1)S(1)}, bf...) all-reduce(bf16[512]{0:T(512)(128)(2,1)S(1)} %dynamic-update-slice., ...), channel_id=1, replica_groups=mesh['rows'=16,'seq'=2] {'rows','seq'}, use_global_device_ids=true, to_apply=%add.1 | all-reduce | flops 5632 | bytes 22528
  59.3 9.4 all-gather.8.cloned.1.call-done
  68.8 2.5 convolution_convert_fusion
  78.0 7.5 all-gather
  85.5 73.8 %all_gather.59 = bf16[512,512]{1,0:T(8,128)(2,1)} all-gather(bf16[16,512]{1,0:T(8,128)(2,1)S(1)} %copy-done.49), channel_id=1, replica_groups=mesh['rows'=16,'seq'=2] {'rows','seq'}, dimensions={0}, use_global_device_ids=true | all-gather | bytes 540672 | tf_op jit(solution)/shard_map/all_gather | solution.py:193
  159.3 72.3 %all_gather.64 = bf16[512,512]{1,0:T(8,128)(2,1)} all-gather(bf16[16,512]{1,0:T(8,128)(2,1)S(1)} %copy-done.50), channel_id=1, replica_groups=mesh['rows'=16,'seq'=2] {'rows','seq'}, dimensions={0}, use_global_device_ids=true | all-gather | bytes 540672 | tf_op jit(solution)/shard_map/all_gather | solution.py:194
  231.7 73.5 %all_gather.65 = bf16[512,512]{1,0:T(8,128)(2,1)} all-gather(bf16[16,512]{1,0:T(8,128)(2,1)S(1)} %copy-done.51), channel_id=1, replica_groups=mesh['rows'=16,'seq'=2] {'rows','seq'}, dimensions={0}, use_global_device_ids=true | all-gather | bytes 540672 | tf_op jit(solution)/shard_map/all_gather | solution.py:196
  307.0 1.7 convolution_convert_fusion.1
  310.2 3.9 reshape.338
  314.1 3.3 copy.136
  317.4 3.9 reshape.339
  321.3 2.5 copy.137
  323.9 7.7 while.48
  325.6 2.0 select_reduce_fusion.2
  329.5 2.0 select_reduce_fusion.2
  331.6 10.2 while.49
  331.8 4.5 fusion.214
  336.5 4.9 fusion.214
  343.2 1.7 fusion.127
  345.9 6.3 fusion.128
  352.2 3.4 fusion.75
  357.8 5.3 fusion.123
  363.2 7.3 convert_reduce_fusion
  370.4 2.9 fusion.132
  373.3 2.5 copy.142
  375.8 2.5 multiply_reduce_fusion.1
  378.4 2.7 convert_reduce_fusion.1
  382.5 3.9 fusion.79
  387.4 1.6 multiply_convert_fusion
  391.6 2.3 copy.162
  393.9 2.5 fusion.131
  396.5 2.6 copy.143
  399.1 1.7 multiply_reduce_fusion.2
  400.8 1.9 multiply_add_fusion
  404.1 9.4 while.50
  405.7 3.1 fusion.220
  410.4 3.1 fusion.220
  413.5 27.5 %while.51 = (s32[]{:T(128)}, f32[512,8,64]{0,2,1:T(8,128)}, bf16[2,512,1024]{2,1,0:T(8,128)(2,1)}, bf16[2,512,8,64]{1,3,2,0:T(8,128)(2,1)S(1)}, s32[512]{0:T(512...) while((s32[]{:T(128)}, f32[512,8,64]{0,2,1:T(8,128)}, ...), condition=%wide.region_23.24_spmd.clone, body=%wide.region_22.23_spmd.clone.sunk | while | flops 1366818816 | bytes 55894204 | solution.py:148
  415.1 1.8 fusion.234
  416.8 3.0 fusion.232
  421.2 1.9 fusion.233
  428.2 1.7 fusion.234
  430.0 2.9 fusion.232
  434.3 3.1 fusion.233
  441.1 3.0 fusion.112
  448.8 1.9 copy.164
  451.0 6.5 fusion.102
  458.8 5.0 fusion.122
  466.3 3.1 reduce-scatter.14.cloned.1.call-done
  469.4 4.1 fusion.98
  473.5 5.8 fusion.88
  479.3 2.0 copy.154
  481.4 2.5 convolution_bitcast_fusion.1
  483.8 3.7 fusion.130
  487.6 1.6 copy.150
  489.6 39.8 %all-reduce.16 = (f32[2048]{0:T(1024)S(1)}, f32[512]{0:T(512)S(1)}, f32[512]{0:T(512)S(1)}, f32[512]{0:T(512)S(1)}, f32[512]{0:T(512)S(1)}, /*index=5*/f32[512]{0:T(512)S(1)}, f32[512]{0:T(512)S(1)}, f32[512]{0:T(512)S(1)}) all-reduce(f32[2048]{0:T(1024)S(1)} %copy-done.59, ...), channel_id=11, replica_groups=mesh['rows'=16,'seq'=2] {'rows','seq'}, use_global_device_ids=true, to_apply=%region_35.36.clone | all-reduce | flops 5632 | bytes 45056
  534.8 2.5 copy.155
  538.0 69.2 %reduce-scatter.22.cloned.1.call-done = f32[16,512]{1,0:T(8,128)} async-done(((f32[512,512]{1,0:T(8,128)}), f32[16,512]{1,0:T(8,128)}) %reduce-scatter.22.cloned.1.call-update) | async-done | bytes 32784 | tf_op jit(solution)/shard_map/reduce_scatter | solution.py:346
  607.1 133.6 %reduce-scatter.20.cloned.1.call-done = f32[16,512]{1,0:T(8,128)} async-done(((f32[512,512]{1,0:T(8,128)}), f32[16,512]{1,0:T(8,128)}) %reduce-scatter.20.cloned.1.call-update) | async-done | bytes 32784 | tf_op jit(solution)/shard_map/reduce_scatter | solution.py:344
  740.7 133.7 %reduce-scatter.18.cloned.1.call-done = f32[16,512]{1,0:T(8,128)} async-done(((f32[512,512]{1,0:T(8,128)}), f32[16,512]{1,0:T(8,128)}) %reduce-scatter.18.cloned.1.call-update) | async-done | bytes 32784 | tf_op jit(solution)/shard_map/reduce_scatter | solution.py:343
  874.4 135.4 %reduce-scatter.30.cloned.1.call-done = f32[16,1024]{1,0:T(8,128)} async-done(((f32[512,1024]{1,0:T(8,128)}), f32[16,1024]{1,0:T(8,128)}) %reduce-scatter.30.cloned.1.call-update) | async-done | bytes 65552
  1009.8 141.2 %reduce-scatter.26.cloned.1.call-done = f32[64,512]{1,0:T(8,128)} async-done(((f32[2048,512]{1,0:T(8,128)}), f32[64,512]{1,0:T(8,128)}) %reduce-scatter.26.cloned.1.call-update) | async-done | bytes 131088 | tf_op jit(solution)/shard_map/reduce_scatter | solution.py:349
  1151.0 141.0 %reduce-scatter.24.cloned.1.call-done = f32[16,2048]{1,0:T(8,128)} async-done(((f32[512,2048]{1,0:T(8,128)}), f32[16,2048]{1,0:T(8,128)}) %reduce-scatter.24.cloned.1.call-update) | async-done | bytes 131088 | tf_op jit(solution)/shard_map/reduce_scatter | solution.py:347
  1292.0 105.1 %reduce-scatter.16.cloned.1.call-done = f32[16,1536]{1,0:T(8,128)} async-done(((f32[512,1536]{1,0:T(8,128)}), f32[16,1536]{1,0:T(8,128)}) %reduce-scatter.16.cloned.1.call-update) | async-done | bytes 98320 | tf_op jit(solution)/shard_map/reduce_scatter | solution.py:342
  (298 shorter events, 65.8 us)
Async XLA Ops:
  7.2 61.6 %all-gather.8.cloned.1.call-start = ((), (), s32[]{:S(2)}) async-start(), calls=%async_computation.9 | async-start | bytes 1622016 | tf_op jit(solution)/shard_map/all_gather | solution.py:192
  7.9 299.1 %all-gather.14.cloned.1.call-start = ((), (), s32[]{:S(2)}) async-start(), calls=%async_computation.12 | async-start | bytes 1081344 | tf_op jit(solution)/shard_map/all_gather | solution.py:195
  8.7 301.5 %all-gather.10.cloned.1.call-start = ((), (), s32[]{:S(2)}) async-start(), calls=%async_computation.10 | async-start | bytes 1572864 | tf_op jit(solution)/shard_map/all_gather | solution.py:235
  57.7 13.6 copy-start.61
  57.8 13.6 copy-start.44
  59.0 284.2 %copy-start.4 = (bf16[1,512,512]{1,2,0:T(8,128)(2,1)}, bf16[1,512,512]{1,2,0:T(8,128)(2,1)S(1)}, u32[]{:S(2)}) copy-start(bf16[1,512,512]{1,2,0:T(8,128)(2,1)S(1)} %copy.131) | copy-start | bytes 1572868
  59.2 12.2 copy-start.38
  59.3 13.2 copy-start.46
  71.4 6.7 copy-start.22
  71.4 14.1 %copy-start.49 = (bf16[16,512]{1,0:T(8,128)(2,1)S(1)}, bf16[16,512]{1,0:T(8,128)(2,1)}, u32[]{:S(2)}) copy-start(bf16[16,512]{1,0:T(8,128)(2,1)} %param.34) | copy-start | bytes 49156
  71.4 87.9 %copy-start.50 = (bf16[16,512]{1,0:T(8,128)(2,1)S(1)}, bf16[16,512]{1,0:T(8,128)(2,1)}, u32[]{:S(2)}) copy-start(bf16[16,512]{1,0:T(8,128)(2,1)} %param.35) | copy-start | bytes 49156
  71.4 160.3 %copy-start.51 = (bf16[16,512]{1,0:T(8,128)(2,1)S(1)}, bf16[16,512]{1,0:T(8,128)(2,1)}, u32[]{:S(2)}) copy-start(bf16[16,512]{1,0:T(8,128)(2,1)} %param.37) | copy-start | bytes 49156
  71.4 233.7 %copy-start.26 = (bf16[1,512,512]{2,1,0:T(8,128)(2,1)S(1)}, bf16[1,512,512]{2,1,0:T(8,128)(2,1)}, u32[]{:S(2)}) copy-start(bf16[1,512,512]{2,1,0:T(8,128)(2,1)} %param.32) | copy-start | bytes 1572868
  72.6 244.9 %all-gather.12.cloned.1.call-start = ((), (), s32[]{:S(2)}) async-start(), calls=%async_computation.11 | async-start | bytes 1572864 | tf_op jit(solution)/shard_map/all_gather | solution.py:234
  73.2 284.6 %all-gather.16.cloned.1.call-start = ((), (), s32[]{:S(2)}) async-start(), calls=%async_computation.13 | async-start | bytes 2162688 | tf_op jit(solution)/shard_map/all_gather | solution.py:197
  73.7 289.4 %all-gather.18.cloned.1.call-start = ((), (), s32[]{:S(2)}) async-start(), calls=%async_computation.14 | async-start | bytes 2162688 | tf_op jit(solution)/shard_map/all_gather | solution.py:199
  74.3 373.0 %reduce-scatter.28.cloned.1.call-start = ((), (), s32[]{:S(2)}) async-start(), calls=%async_computation.22 | async-start | bytes 1032192
  76.3 302.1 %copy-start.32 = (f32[512]{0:T(512)}, f32[512]{0:T(512)S(1)}, u32[]{:S(2)}) copy-start(f32[512]{0:T(512)S(1)} %convert_element_type.145) | copy-start | bytes 6148
  341.8 3.4 copy-start.15
  341.8 3.4 copy-start.40
  341.8 3.4 copy-start.55
  345.0 55.8 %copy-start = (f32[512,512]{0,1:T(8,128)}, f32[512,512]{0,1:T(8,128)S(1)}, u32[]{:S(2)}) copy-start(f32[512,512]{0,1:T(8,128)S(1)} %get-tuple-element.643) | copy-start | bytes 3145732
  345.0 7.2 copy-start.36
  345.9 6.3 copy-start.24
  352.2 3.4 copy-start.14
  356.1 22.3 %copy-start.30 = (f32[512]{0:T(512)}, f32[512]{0:T(512)S(1)}, u32[]{:S(2)}) copy-start(f32[512]{0:T(512)S(1)} %broadcast_multiply_fusion.6) | copy-start | bytes 6148
  363.2 7.3 copy-start.18
  375.8 6.7 copy-start.48
  382.0 4.4 slice-start
  382.5 3.9 slice-start.1
  382.5 3.9 copy-start.29
  390.5 10.2 copy-start.9
  390.5 8.5 copy-start.37
  390.6 8.5 copy-start.41
  390.6 8.5 copy-start.43
  393.9 75.5 %reduce-scatter.14.cloned.1.call-start = ((), (), s32[]{:S(2)}) async-start(), calls=%async_computation.15 | async-start | bytes 3145728 | tf_op jit(solution)/shard_map/reduce_scatter | solution.py:329
  399.0 4.6 copy-start.13
  399.1 5.1 copy-start.28
  399.1 5.1 copy-start.53
  441.0 3.2 copy-start.10
  441.0 3.2 copy-start.56
  441.0 4.8 copy-start.7
  441.0 4.8 copy-start.12
  441.0 166.1 %reduce-scatter.22.cloned.1.call-start = ((), (), s32[]{:S(2)}) async-start(), calls=%async_computation.19 | async-start | bytes 1081344 | tf_op jit(solution)/shard_map/reduce_scatter | solution.py:346
  444.1 3.3 copy-start.23
  444.1 296.6 %reduce-scatter.20.cloned.1.call-start = ((), (), s32[]{:S(2)}) async-start(), calls=%async_computation.18 | async-start | bytes 1081344 | tf_op jit(solution)/shard_map/reduce_scatter | solution.py:344
  445.7 428.7 %reduce-scatter.18.cloned.1.call-start = ((), (), s32[]{:S(2)}) async-start(), calls=%async_computation.17 | async-start | bytes 1081344 | tf_op jit(solution)/shard_map/reduce_scatter | solution.py:343
  447.3 3.7 copy-start.58
  447.3 562.5 %reduce-scatter.30.cloned.1.call-start = ((), (), s32[]{:S(2)}) async-start(), calls=%async_computation.23 | async-start | bytes 2162688
  450.7 700.3 %reduce-scatter.26.cloned.1.call-start = ((), (), s32[]{:S(2)}) async-start(), calls=%async_computation.21 | async-start | bytes 4325376 | tf_op jit(solution)/shard_map/reduce_scatter | solution.py:349
  457.5 834.5 %reduce-scatter.24.cloned.1.call-start = ((), (), s32[]{:S(2)}) async-start(), calls=%async_computation.20 | async-start | bytes 4325376 | tf_op jit(solution)/shard_map/reduce_scatter | solution.py:347
  463.8 5.6 copy-start.5
  463.8 5.6 copy-start.39
  463.8 5.6 copy-start.45
  463.8 5.6 copy-start.47
  463.8 5.6 copy-start.62
  463.8 933.3 %reduce-scatter.16.cloned.1.call-start = ((), (), s32[]{:S(2)}) async-start(), calls=%async_computation.16 | async-start | bytes 3244032 | tf_op jit(solution)/shard_map/reduce_scatter | solution.py:342
  466.3 7.2 copy-start.65
  473.5 7.8 copy-start.19
  473.5 10.3 copy-start.27
  483.8 5.7 copy-start.57
  483.8 5.7 copy-start.59
  483.8 5.7 copy-start.60
  483.8 5.7 copy-start.63
  (21 other events, 34.8 us)
Sparse Core Ops, SparseCore 0:
  10.9 57.8 all-gather.7
  71.7 53.1 all-gather.13
  126.4 22.1 all-gather.9
  150.6 23.0 all-gather.11
  176.6 56.9 all-gather.15
  236.6 56.5 all-gather.17
  394.0 12.6 reduce-scatter.27
  441.1 28.1 reduce-scatter.13
  472.3 134.7 reduce-scatter.21
  609.8 130.8 reduce-scatter.19
  743.6 130.7 reduce-scatter.17
  877.1 132.6 reduce-scatter.29
  1012.8 138.2 reduce-scatter.25
  1153.8 138.1 reduce-scatter.23
  1298.8 98.2 reduce-scatter.15
where the time goes:
time: 1410 us; the launch traced here: 1400 us
  waiting for transfers between devices  875 us (62%)
  blocking collectives  309 us (22%)
  matrix products  118 us (8%)
  local copies, waits for them, and re-layouts  56.4 us (4%)
  other arithmetic  29 us (2%)
  between operations  15.2 us (1%)
    reduce_scatter x1, waiting for transfers between devices, per_device(): lax.psum_scatter(grad_down, ('rows', 'seq'), scatter_dimension=0, tiled=T...  141 us
    reduce_scatter x1, waiting for transfers between devices, per_device(): lax.psum_scatter(grad_up, ('rows', 'seq'), scatter_dimension=0, tiled=True)  141 us
    unnamed x17, waiting for transfers between devices  139 us
    reduce_scatter x1, waiting for transfers between devices, per_device(): lax.psum_scatter(grad_output, ('rows', 'seq'), scatter_dimension=0, tiled...  134 us
    reduce_scatter x1, waiting for transfers between devices, per_device(): lax.psum_scatter(grad_query, ('rows', 'seq'), scatter_dimension=0, tiled=...  134 us
    reduce_scatter x1, waiting for transfers between devices, per_device(): lax.psum_scatter(grad_project, ('rows', 'seq'), scatter_dimension=0, tile...  105 us
    unnamed x2, blocking collectives  82 us
    all_gather x1, blocking collectives, per_device(): lax.all_gather(self_output, ('rows', 'seq'), axis=0, tiled=True)  73.8 us
  transfers between devices with their start and end apart: 15, of which 9 were waited for; matrix products, arithmetic and copies ran while one was open for 12% of the time, Pallas kernels for 0%

commit v1 on v0

--- a/solution.py
+++ b/solution.py
@@ -150,7 +150,86 @@
     )
 
 
-def per_device(
+BLOCK = 16
+AXES = ("rows", "seq")
+
+
+def device_pairs(flip):
+    return [(device, device ^ flip) for device in range(32)]
+
+
+def exchange(value, flip):
+    return lax.ppermute(value, AXES, device_pairs(flip))
+
+
+def device_index():
+    return lax.axis_index("rows") * 2 + lax.axis_index("seq")
+
+
+FLIP_Y, FLIP_CORE, FLIP_X, FLIP_Z = 1, 2, 4, 8
+
+
+def gather_pair(left, right):
+    width = left.shape[1]
+    both = jnp.concatenate([left, right], 1)
+    both = jnp.concatenate([both] + [exchange(both, FLIP_Z * i) for i in (1, 2, 3)], 0)
+    out = []
+    for value, first, second in (
+        (both[:, :width], FLIP_X, FLIP_Y), (both[:, width:], FLIP_Y, FLIP_X)
+    ):
+        value = jnp.concatenate([value, exchange(value, first)], 0)
+        other = exchange(value, second)
+        order = [f + i * FLIP_Z for f in (0, first) for i in range(4)]
+        order = order + [o + second for o in order]
+        order = order + [o + FLIP_CORE for o in order]
+        out.append(((value, other, exchange(value, FLIP_CORE), exchange(other, FLIP_CORE)), order))
+    return out
+
+
+def swapped(blocks):
+    value = blocks.reshape((2,) * 5 + blocks.shape[1:])
+    for axis in range(5):
+        bit = (device_index() >> (4 - axis)) & 1
+        value = jnp.where(bit == 1, jnp.flip(value, axis), value)
+    return value.reshape(blocks.shape)
+
+
+def natural(got):
+    pieces, order = got
+    whole = jnp.concatenate(pieces, 0).reshape(32, BLOCK, -1)
+    whole = jnp.concatenate([whole[order.index(i)][None] for i in range(32)], 0)
+    return swapped(whole).reshape(32 * BLOCK, -1)
+
+
+def relative(value):
+    return swapped(value.astype(jnp.bfloat16).reshape(32, BLOCK, -1))
+
+
+def scatter_pair(left, right):
+    out = []
+    for value, first, second in ((left, FLIP_Y, FLIP_X), (right, FLIP_X, FLIP_Y)):
+        parts = {i: value[i] for i in range(32)}
+        for flip in (FLIP_CORE, first, second):
+            kept = [i for i in sorted(parts) if not i & flip]
+            sent = jnp.concatenate([parts[i | flip] for i in kept], 0)
+            came = exchange(sent, flip)
+            parts = {
+                i: (
+                    parts[i].astype(jnp.float32)
+                    + came[n * BLOCK : (n + 1) * BLOCK].astype(jnp.float32)
+                ).astype(jnp.bfloat16)
+                for n, i in enumerate(kept)
+            }
+        out.append(parts)
+    width = left.shape[2]
+    total = jnp.concatenate([out[0][0], out[1][0]], 1).astype(jnp.float32)
+    for i in (1, 2, 3):
+        sent = jnp.concatenate([out[0][FLIP_Z * i], out[1][FLIP_Z * i]], 1)
+        total = total + exchange(sent, FLIP_Z * i).astype(jnp.float32)
+    return total[:, :width], total[:, width:]
+
+
+def general_device(
     target_states,
     source_states,
     target_segments,
@@ -360,7 +439,208 @@
     )
 
 
-def solution(mesh):
+def fast_device(
+    target_states,
+    source_states,
+    target_segments,
+    source_segments,
+    output_grad,
+    self_project,
+    self_output,
+    cross_query,
+    cross_keyval,
+    cross_output,
+    hidden_up,
+    hidden_bias,
+    hidden_down,
+    output_bias,
+    first_gain,
+    first_shift,
+    second_gain,
+    second_shift,
+    third_gain,
+    third_shift,
+):
+    vectors = (
+        output_bias, first_gain, first_shift, second_gain, second_shift, third_gain, third_shift
+    )
+    pad = jnp.zeros((BLOCK, 128 - len(vectors) - 4), jnp.bfloat16)
+    vector_block = jnp.concatenate(
+        [vector[:, None] for vector in vectors] + [hidden_bias.reshape(4, BLOCK).T, pad], 1
+    )
+    down_block = jnp.concatenate([hidden_down[i * BLOCK : (i + 1) * BLOCK] for i in range(4)], 1)
+    left_one = self_project[:, :768]
+    right_one = jnp.concatenate([self_project[:, 768:], vector_block], 1)
+    left_two = jnp.concatenate([self_output, cross_query, cross_keyval, cross_output, hidden_up[:, :768]], 1)
+    right_two = jnp.concatenate([hidden_up[:, 768:], down_block], 1)
+    got_one = gather_pair(left_one, right_one)
+    got_two = gather_pair(left_two, right_two)
+    left_one, right_one = [natural(v) for v in got_one]
+    left_two, right_two = [natural(v) for v in got_two]
+    full_project = jnp.concatenate([left_one, right_one[:, :768]], 1)
+    vector_rows = right_one[:, 768:768 + 128].T
+    full_downbias, gain_one, shift_one, gain_two, shift_two, gain_three, shift_three = vector_rows[:7]
+    full_upbias = vector_rows[7:11].reshape(4, 32, BLOCK).transpose(1, 0, 2).reshape(-1)
+    full_output, full_query, full_keyval, full_crossout = (
+        left_two[:, :512], left_two[:, 512:1024], left_two[:, 1024:2048], left_two[:, 2048:2560]
+    )
+    full_up = jnp.concatenate([left_two[:, 2560:], right_two[:, :1280]], 1)
+    full_down = right_two[:, 1280:].reshape(32, BLOCK, 4, 512).transpose(0, 2, 1, 3).reshape(2048, 512)
+    gain_one = gain_one.astype(jnp.float32)
+    gain_two = gain_two.astype(jnp.float32)
+    gain_three = gain_three.astype(jnp.float32)
+    score_scale = HD ** (-0.5)
+    states = target_states[0].astype(jnp.float32)
+    local_rows = states.shape[0]
+    model_width = states.shape[1]
+    seq_count = lax.axis_size("seq")
+    row_segments = target_segments[0]
+    seq_length = row_segments.shape[0]
+    own_segments = lax.dynamic_slice_in_dim(
+        row_segments, lax.axis_index("seq") * local_rows, local_rows
+    )
+    block_rows = max(1, min(seq_count, 512 // local_rows)) * local_rows
+    block_count = seq_length // block_rows
+    seg_blocks = row_segments.reshape(block_count, block_rows)
+    normed_value, normed_one, inverse_one = layer_norm(
+        states, gain_one, shift_one.astype(jnp.float32)
+    )
+    lowered_one = normed_value.astype(jnp.bfloat16)
+    projected = matmul(lowered_one, full_project).astype(jnp.bfloat16)
+    query_flat = projected[:, :model_width]
+    key_local = projected[:, model_width : 2 * model_width]
+    value_local = projected[:, 2 * model_width :]
+    queries = head_split(query_flat)
+    key_all, value_all = (
+        lax.all_gather(key_local, "seq", axis=0, tiled=True),
+        lax.all_gather(value_local, "seq", axis=0, tiled=True),
+    )
+    key_blocks = key_all.reshape(block_count, block_rows, HEADS, HD)
+    value_blocks = value_all.reshape(block_count, block_rows, HEADS, HD)
+    log_total = log_totals(queries, key_blocks, seg_blocks, own_segments)
+    self_mixed = head_join(
+        weighted_sum(queries, key_blocks, value_blocks, seg_blocks, own_segments, log_total)
+    ).astype(jnp.bfloat16)
+    after_self = states + matmul(self_mixed, full_output)
+    normed_value, normed_two, inverse_two = layer_norm(
+        after_self, gain_two, shift_two.astype(jnp.float32)
+    )
+    lowered_two = normed_value.astype(jnp.bfloat16)
+    cross_asked = matmul(lowered_two, full_query).astype(jnp.bfloat16)
+    source_low = source_states[0]
+    source_all = lax.all_gather(source_low, "seq", axis=0, tiled=True)
+    key_value = matmul(source_all, full_keyval).astype(jnp.bfloat16)
+    cross_key_heads = head_split(key_value[:, :model_width])
+    cross_value_heads = head_split(key_value[:, model_width:])
+    asked_heads = head_split(cross_asked)
+    raw_scores, same_seg = scores_of(asked_heads, cross_key_heads, own_segments, source_segments[0])
+    cross_probs = jax.nn.softmax(jnp.where(same_seg, raw_scores, -1000000000.0), axis=-1)
+    cross_mixed = head_join(
+        jnp.einsum(
+            "hqk,khd->qhd",
+            cross_probs.astype(jnp.bfloat16),
+            cross_value_heads,
+            preferred_element_type=jnp.float32,
+        )
+    ).astype(jnp.bfloat16)
+    after_cross = after_self + matmul(cross_mixed, full_crossout)
+    normed_value, normed_three, inverse_three = layer_norm(
+        after_cross, gain_three, shift_three.astype(jnp.float32)
+    )
+    lowered_three = normed_value.astype(jnp.bfloat16)
+    hidden = matmul(lowered_three, full_up) + full_upbias.astype(jnp.float32)
+    activated = jax.nn.gelu(hidden).astype(jnp.bfloat16)
+    layer_out = after_cross + matmul(activated, full_down) + full_downbias.astype(jnp.float32)
+    grad_low = output_grad[0]
+    out_grad = grad_low.astype(jnp.float32)
+    grad_down = transposed(activated, grad_low)
+    grad_downbias = jnp.sum(out_grad, 0)
+    grad_act = against(grad_low, full_down)
+    grad_hidden = jax.vjp(jax.nn.gelu, hidden)[1](grad_act)[0].astype(jnp.bfloat16)
+    grad_upbias = jnp.sum(grad_hidden.astype(jnp.float32), 0)
+    grad_up = transposed(lowered_three, grad_hidden)
+    dx_three, grad_gain_three, grad_shift_three = norm_back(
+        against(grad_hidden, full_up), normed_three, inverse_three, gain_three
+    )
+    grad_cross = out_grad + dx_three
+    grad_cross_low = grad_cross.astype(jnp.bfloat16)
+    grad_crossout = transposed(cross_mixed, grad_cross_low)
+    grad_cross_heads = head_split(against(grad_cross_low, full_crossout).astype(jnp.bfloat16))
+    grad_weights = jnp.einsum(
+        "qhd,khd->hqk", grad_cross_heads, cross_value_heads, preferred_element_type=jnp.float32
+    )
+    grad_scores = (
+        cross_probs * (grad_weights - jnp.sum(cross_probs * grad_weights, -1, keepdims=True))
+    ).astype(jnp.bfloat16)
+    grad_asked = head_join(
+        jnp.einsum("hqk,khd->qhd", grad_scores, cross_key_heads, preferred_element_type=jnp.float32)
+        * score_scale
+    ).astype(jnp.bfloat16)
+    grad_cross_keys = (
+        jnp.einsum("hqk,qhd->khd", grad_scores, asked_heads, preferred_element_type=jnp.float32)
+        * score_scale
+    )
+    grad_cross_values = jnp.einsum(
+        "hqk,qhd->khd",
+        cross_probs.astype(jnp.bfloat16),
+        grad_cross_heads,
+        preferred_element_type=jnp.float32,
+    )
+    pair_terms = jnp.concatenate([head_join(grad_cross_keys), head_join(grad_cross_values)], 1)
+    pair_grad = lax.psum_scatter(
+        pair_terms.astype(jnp.bfloat16), "seq", scatter_dimension=0, tiled=True
+    )
+    grad_keyval = transposed(source_low, pair_grad)
+    grad_source = against(pair_grad, full_keyval)
+    grad_query = transposed(lowered_two, grad_asked)
+    dx_two, grad_gain_two, grad_shift_two = norm_back(
+        against(grad_asked, full_query), normed_two, inverse_two, gain_two
+    )
+    grad_self = grad_cross + dx_two
+    grad_self_low = grad_self.astype(jnp.bfloat16)
+    grad_output = transposed(self_mixed, grad_self_low)
+    grad_mixed = against(grad_self_low, full_output).astype(jnp.bfloat16)
+    grad_heads = head_split(grad_mixed)
+    row_dots = grad_dots(
+        queries, grad_heads, key_blocks, value_blocks, seg_blocks, own_segments, log_total
+    )
+    grad_queries, key_terms = query_grads(
+        queries, grad_heads, key_blocks, value_blocks, seg_blocks, own_segments, log_total, row_dots
+    )
+    summed = lax.psum_scatter(
+        key_terms.reshape(seq_length, 2 * model_width).astype(jnp.bfloat16),
+        "seq",
+        scatter_dimension=0,
+        tiled=True,
+    )
+    grad_projected = jnp.concatenate([head_join(grad_queries).astype(jnp.bfloat16), summed], 1)
+    grad_project = transposed(lowered_one, grad_projected)
+    dx_one, grad_gain_one, grad_shift_one = norm_back(
+        against(grad_projected, full_project), normed_one, inverse_one, gain_one
+    )
+    grad_target = grad_self + dx_one
+    vector_sums = jnp.stack(
+        [grad_downbias, grad_gain_one, grad_shift_one, grad_gain_two, grad_shift_two,
+         grad_gain_three, grad_shift_three], 1)
+    bias_sums = grad_upbias.reshape(32, 4, BLOCK).transpose(0, 2, 1).reshape(512, 4)
+    vector_sums = jnp.concatenate([vector_sums, bias_sums, jnp.zeros((512, 117), jnp.float32)], 1)
+    down_sums = grad_down.reshape(32, 4, BLOCK, 512).transpose(0, 2, 1, 3).reshape(512, 2048)
+    left_two = relative(grad_up)
+    right_two = relative(down_sums)
+    own_up, own_down = scatter_pair(left_two, right_two)
+    left_one = relative(jnp.concatenate([grad_project, grad_keyval], 1))
+    right_one = relative(jnp.concatenate([grad_output, grad_query, grad_crossout, vector_sums], 1))
+    own_left, own_right = scatter_pair(left_one, right_one)
+    own_down = jnp.concatenate([own_down[:, i * 512:(i + 1) * 512] for i in range(4)], 0)
+    own_vectors = own_right[:, 1536:1536 + 11].T
+    shards = (
+        own_left[:, :1536], own_right[:, :512], own_right[:, 512:1024], own_left[:, 1536:],
+        own_right[:, 1024:1536], own_up, own_vectors[7:11].reshape(64), own_down,
+    ) + tuple(own_vectors[i] for i in range(7))
+    return (layer_out.astype(jnp.bfloat16)[None], grad_target[None], grad_source[None]) + shards
+
+
+def specs():
     in_specs = (
         P("rows", "seq", None),
         P("rows", "seq", None),
@@ -403,6 +683,13 @@
         P(("rows", "seq")),
         P(("rows", "seq")),
     )
+    return in_specs, out_specs
+
+
+def solution(mesh):
+    in_specs, out_specs = specs()
+    fast = mesh.shape["rows"] == 16 and mesh.shape["seq"] == 2
     return jax.shard_map(
-        per_device, mesh=mesh, in_specs=in_specs, out_specs=out_specs, check_vma=False
-    )
+        fast_device if fast else general_device,
+        mesh=mesh, in_specs=in_specs, out_specs=out_specs, check_vma=False,
+    )

time: 1410 us -> 584 us (0.41)
  waiting for transfers between devices: 875 us -> 85.8 us
  blocking collectives: 309 us -> 6.18 us
  local copies, waits for them, and re-layouts: 56.4 us -> 218 us
  other arithmetic: 29 us -> 101 us
  starting transfers between devices: 0.82 us -> 39.8 us
    reduce_scatter x7 -> x1, waiting for transfers between devices: 727 us -> 0.01 us  [fast_device(): lax.psum_scatter(key_terms.reshape(seq_length, 2 * model_width).astype(jn...]
    all_gather x4 -> x1, blocking collectives: 227 us -> 6.18 us  [fast_device(): source_all = lax.all_gather(source_low, 'seq', axis=0, tiled=True)]
    unnamed x17 -> x5, waiting for transfers between devices: 139 us -> 0.07 us
    unnamed x165 -> x355, local copies, waits for them, and re-layouts: 33.2 us -> 133 us
    ppermute x0 -> x40, waiting for transfers between devices: none -> 85.8 us  [exchange(): return lax.ppermute(value, AXES, device_pairs(flip))]
    unnamed x2 -> x0, blocking collectives: 82 us -> none
    ppermute x0 -> x40, starting transfers between devices: none -> 39.2 us  [exchange(): return lax.ppermute(value, AXES, device_pairs(flip))]
    select_n x0 -> x39, other arithmetic: none -> 38.8 us  [swapped(): value = jnp.where(bit == 1, jnp.flip(value, axis), value)]
  transfers between devices with their start and end apart: 15 -> 44, of which waited for: 9 -> 17; matrix products, arithmetic and copies ran while one was open for 12% -> 34% of each run, Pallas kernels for 0% -> 0%
where the time goes in v1:
time: 584 us; the launch traced here: 573 us
  local copies, waits for them, and re-layouts  218 us (37%)
  matrix products  105 us (18%)
  other arithmetic  101 us (17%)
  waiting for transfers between devices  85.8 us (15%)
  starting transfers between devices  39.8 us (7%)
  between operations  16.1 us (3%)
  blocking collectives  6.18 us (1%)
    unnamed x355, local copies, waits for them, and re-layouts  133 us
    ppermute x40, waiting for transfers between devices, exchange(): return lax.ppermute(value, AXES, device_pairs(flip))  85.8 us
    ppermute x40, starting transfers between devices, exchange(): return lax.ppermute(value, AXES, device_pairs(flip))  39.2 us
    select_n x39, other arithmetic, swapped(): value = jnp.where(bit == 1, jnp.flip(value, axis), value)  38.8 us
    unnamed x36, other arithmetic  23.3 us
    dot_general x7, matrix products, transposed(): lax.dot_general(left, right, (((0,), (0,)), ((), ())), preferred_element_...  18.3 us
    dot_general x7, matrix products, against(): lax.dot_general(left, right, (((1,), (1,)), ((), ())), preferred_element_...  18 us
    dot_general x7, matrix products, matmul(): return jnp.dot(left, right, preferred_element_type=jnp.float32)  15.3 us
  transfers between devices with their start and end apart: 44, of which 17 were waited for; matrix products, arithmetic and copies ran while one was open for 34% of the time, Pallas kernels for 0%

profile of v1, /device:TPU:0, one launch (start us, length us, event | category | flops | bytes accessed | tf_op | source)
XLA Modules:
  0.0 573.3 jit_solution(12767388610122036157)
XLA Ops:
  14.2 5.1 collective-permute-start.2
  28.1 3.7 collective-permute-start.13
  43.5 6.2 %all-gather = bf16[1,336,512]{2,1,0:T(8,128)(2,1)} all-gather(bf16[1,168,512]{2,1,0:T(8,128)(2,1)S(1)} %copy-done.41), channel_id=2, replica_groups=mesh['rows'=16,'seq'=2] {'seq'}, dimensions={1}, use_global_device_ids=true | all-gather | bytes 516096 | tf_op jit(solution)/shard_map/all_gather | solution.py:531
  60.3 2.3 collective-permute-done.8
  100.3 7.5 %collective-permute-done.14 = bf16[64,3328]{1,0:T(8,128)(2,1)S(1)} collective-permute-done((bf16[64,3328]{1,0:T(8,128)(2,1)}, bf16[64,3328]{1,0:T(8,128)(2,1)S(1)}, u32[]{:S(2)}, u32[]{:S(2)}) %collective-permute-start.14) | collective-permute-done | bytes 426016 | tf_op jit(solution)/shard_map/ppermute | solution.py:162
  109.8 6.1 %collective-permute-done.18 = bf16[64,3328]{1,0:T(8,128)(2,1)S(1)} collective-permute-done((bf16[64,3328]{1,0:T(8,128)(2,1)}, bf16[64,3328]{1,0:T(8,128)(2,1)S(1)}, u32[]{:S(2)}, u32[]{:S(2)}) %collective-permute-start.18) | collective-permute-done | bytes 426016 | tf_op jit(solution)/shard_map/ppermute | solution.py:162
  117.7 21.7 %collective-permute-done.15 = bf16[128,3328]{1,0:T(8,128)(2,1)} collective-permute-done((bf16[128,3328]{1,0:T(8,128)(2,1)S(1)}, bf16[128,3328]{1,0:T(8,128)(2,1)}, u32[]{:S(2)}, u32[]{:S(2)}) %collective-permute-start.15) | collective-permute-done | bytes 852000 | tf_op jit(solution)/shard_map/ppermute | solution.py:162
  146.7 3.9 reshape.756
  150.6 3.3 copy.264
  153.9 3.9 reshape.757
  157.7 2.5 copy.265
  160.3 7.7 %while.48 = (s32[]{:T(128)}, f32[8,512]{1,0:T(8,128)S(1)}, f32[8,512]{1,0:T(8,128)S(1)}, s32[512]{0:T(512)S(1)}, s32[2,512]{1,0:T(2,128)S(1)}, /*index=5*/bf16[2...) while((s32[]{:T(128)}, f32[8,512]{1,0:T(8,128)S(1)}, ...), condition=%wide.region_5.6_spmd.clone, body=%wide.region_2.5_spmd.clone.sunk | while | flops 285495296 | bytes 18833528 | solution.py:79
  168.0 10.3 %while.49 = (s32[]{:T(128)}, f32[512,8,64]{0,2,1:T(8,128)}, bf16[2,512,8,64]{1,3,2,0:T(8,128)(2,1)}, s32[512]{0:T(512)S(1)}, s32[2,512]{1,0:T(2,128)S(1)}, /*ind...) while((s32[]{:T(128)}, f32[512,8,64]{0,2,1:T(8,128)}, ...), condition=%wide.region_7.8_spmd.clone, body=%wide.region_6.7_spmd.clone.sunk | while | flops 546045952 | bytes 4220538 | solution.py:96
  168.2 4.5 fusion.300
  172.9 4.9 fusion.300
  178.3 2.3 convert_element_type.1387
  242.3 9.1 %reverse_select_fusion.4 = (bf16[2,2,2,2,2,16,3328]{6,5,4,3,2,1,0:T(8,128)(2,1)S(1)}, bf16[2,2,2,2,2,16,3328]{6,5,4,3,2,1,0:T(8,128)(2,1)}) fusion(bf16[2,2,2,2,2,16,3328]{6,5,4,3,2,1,0:T(8,128)(2,1)} %bitcast.1575, pred[]{:T(512)S(6)} %eq.92, bf16[2,2,2,2,2,16,3328]{6,5,4,3,2,1,0:T(8,128)(2,1)} %bitcast.115), kind=kLoop, calls=%fused_computation.79 | loop fusion | flops 3407872 | bytes 13631489 | tf_op jit(solution)/shard_map/jit(_where)/select_n | solution.py:193
  257.0 4.7 reshape.661
  261.7 3.7 copy.269
  275.5 2.5 convolution_convert_fusion.10
  278.1 6.2 %fusion.219 = (f32[8,512]{1,0:T(8,128)}, f32[8,512,336]{1,2,0:T(8,128)}) fusion(pred[512,336]{0,1:T(8,128)(4,1)} %broadcast_compare_fusion.4, bf16[512,8,64]{0,2,1:T(8,128)(2,1)} %bitcast.1593, bf16[336,8,64]{0,2,1:T(8,128)(2,1)S(1)} %bitcast.1585), kind=kOutput, calls=%fused_computation.976 | convolution fusion | flops 181666128 | bytes 6561792 | tf_op jit(solution)/shard_map/sub | solution.py:537
  284.3 3.3 fusion.92
  289.7 3.8 fusion.72
  293.5 4.6 fusion.224
  298.2 2.9 fusion.223
  301.1 2.6 convolution_convert_fusion.2
  303.8 2.6 copy.272
  306.4 2.5 multiply_reduce_fusion.1
  313.5 4.3 fusion.97
  322.1 4.5 copy.295
  326.6 2.9 convert_bitcast_fusion
  329.6 3.3 copy.297
  332.9 4.5 convert_element_type.1697
  337.3 3.0 reverse_select_fusion.19
  345.4 2.9 fusion.106
  350.4 3.0 reverse_select_fusion.24
  367.9 2.3 copy.317
  370.4 2.5 fusion.222
  372.9 2.6 copy.273
  381.0 9.4 %while.50 = (s32[]{:T(128)}, f32[8,512]{1,0:T(8,128)S(1)}, s32[512]{0:T(512)S(1)}, s32[2,512]{1,0:T(2,128)S(1)}, bf16[2,512,8,64]{1,3,2,0:T(8,128)(2,1)S(1)}, /*...) while((s32[]{:T(128)}, f32[8,512]{1,0:T(8,128)S(1)}, ...), condition=%wide.region_21.22_spmd.clone, body=%wide.region_19.21_spmd.clone.sunk | while | flops 547622912 | bytes 23683236 | solution.py:115
  382.6 3.1 fusion.306
  387.3 3.1 fusion.306
  390.4 21.4 %while.51 = (s32[]{:T(128)}, f32[512,8,64]{0,2,1:T(8,128)S(1)}, bf16[2,512,1024]{1,2,0:T(8,128)(2,1)}, bf16[2,512,8,64]{1,3,2,0:T(8,128)(2,1)S(1)}, s32[512]{0:T...) while((s32[]{:T(128)}, f32[512,8,64]{0,2,1:T(8,128)S(1)}, ...), condition=%wide.region_23.24_spmd.clone, body=%wide.region_22.23_spmd.clone.sunk | while | flops 1366818816 | bytes 68477168 | solution.py:148
  393.7 3.0 fusion.318
  404.4 3.0 fusion.318
  421.2 4.2 copy.278
  427.5 2.6 convolution_convert_fusion.8
  430.1 2.7 convolution_convert_fusion.7
  432.8 2.4 convolution_convert_fusion.9
  460.5 2.4 convolution_convert_fusion.3
  465.4 9.4 %collective-permute-done.32 = bf16[128,2048]{1,0:T(8,128)(2,1)} collective-permute-done((bf16[128,2048]{1,0:T(8,128)(2,1)}, bf16[128,2048]{1,0:T(8,128)(2,1)}, u32[]{:S(2)}, u32[]{:S(2)}) %collective-permute-start.32) | collective-permute-done | bytes 524320 | tf_op jit(solution)/shard_map/ppermute | solution.py:162
  480.2 2.3 collective-permute-done.33
  485.1 3.0 collective-permute-start.38
  488.4 2.5 convolution_bitcast_fusion
  490.9 4.3 collective-permute-done.38
  496.6 2.5 convolution_convert_fusion
  501.6 2.2 reverse_select_fusion.10
  510.4 4.6 concatenate.190
  515.1 2.4 reverse_select_fusion.29
  524.7 8.9 %collective-permute-done.26 = bf16[128,1664]{1,0:T(8,128)(2,1)S(1)} collective-permute-done((bf16[128,1664]{1,0:T(8,128)(2,1)S(1)}, bf16[128,1664]{1,0:T(8,128)(2,1)S(1)}, u32[]{:S(2)}, u32[]{:S(2)}) %collective-permute-start.26) | collective-permute-done | bytes 426016 | tf_op jit(solution)/shard_map/ppermute | solution.py:162
  534.7 6.7 %collective-permute-done.23 = bf16[128,2560]{1,0:T(8,128)(2,1)S(1)} collective-permute-done((bf16[128,2560]{1,0:T(8,128)(2,1)S(1)}, bf16[128,2560]{1,0:T(8,128)(2,1)S(1)}, u32[]{:S(2)}, u32[]{:S(2)}) %collective-permute-start.23) | collective-permute-done | bytes 655392 | tf_op jit(solution)/shard_map/ppermute | solution.py:162
  545.2 4.5 collective-permute-done.24
  556.5 2.5 copy.300
  559.0 3.9 collective-permute-done.29
  (690 shorter events, 307.8 us)
Async XLA Ops:
  7.2 36.3 %copy-start.41 = (bf16[1,168,512]{2,1,0:T(8,128)(2,1)S(1)}, bf16[1,168,512]{2,1,0:T(8,128)(2,1)}, u32[]{:S(2)}) copy-start(bf16[1,168,512]{2,1,0:T(8,128)(2,1)} %param.29) | copy-start | bytes 516100
  7.2 139.5 %all-gather.4.cloned.1.call-start = ((), (), s32[]{:S(2)}) async-start(), calls=%async_computation.2 | async-start | bytes 1572864 | tf_op jit(solution)/shard_map/all_gather | solution.py:516
  14.2 35.4 %collective-permute-start.2 = (bf16[16,1664]{1,0:T(8,128)(2,1)S(1)}, bf16[16,1664]{1,0:T(8,128)(2,1)S(1)}, u32[]{:S(2)}, u32[]{:S(2)}) collective-permute-start(bf16[16,1664]{1,0:T(8,128)(2,1)S(1)} %concatenate.159), channel_id=1, source_target_pairs={{0,24},{1,25},{2,26},{3,27},{4,28},{5,29},{6,30},{7,31},{8,16},{9,... | collective-permute-start | bytes 159752 | tf_op jit(solution)/shard_map/ppermute | solution.py:162
  19.3 31.0 %collective-permute-start.1 = (bf16[16,1664]{1,0:T(8,128)(2,1)S(1)}, bf16[16,1664]{1,0:T(8,128)(2,1)S(1)}, u32[]{:S(2)}, u32[]{:S(2)}) collective-permute-start(bf16[16,1664]{1,0:T(8,128)(2,1)S(1)} %concatenate.159), channel_id=1, source_target_pairs={{0,16},{1,17},{2,18},{3,19},{4,20},{5,21},{6,22},{7,23},{8,24},{9,... | collective-permute-start | bytes 159752 | tf_op jit(solution)/shard_map/ppermute | solution.py:162
  19.3 31.0 %collective-permute-start = (bf16[16,1664]{1,0:T(8,128)(2,1)S(1)}, bf16[16,1664]{1,0:T(8,128)(2,1)S(1)}, u32[]{:S(2)}, u32[]{:S(2)}) collective-permute-start(bf16[16,1664]{1,0:T(8,128)(2,1)S(1)} %concatenate.159), channel_id=1, source_target_pairs={{0,8},{1,9},{2,10},{3,11},{4,12},{5,13},{6,14},{7,15},{8,0},{9,1},... | collective-permute-start | bytes 159752 | tf_op jit(solution)/shard_map/ppermute | solution.py:162
  28.1 30.4 %copy-start.56 = (bf16[16,6656]{1,0:T(8,128)(2,1)}, bf16[16,6656]{1,0:T(8,128)(2,1)S(1)}, u32[]{:S(2)}) copy-start(bf16[16,6656]{1,0:T(8,128)(2,1)S(1)} %constant_dynamic-update-slice_fusion.69) | copy-start | bytes 638980
  28.1 30.4 %collective-permute-start.13 = (bf16[16,6656]{1,0:T(8,128)(2,1)S(1)}, bf16[16,6656]{1,0:T(8,128)(2,1)S(1)}, u32[]{:S(2)}, u32[]{:S(2)}) collective-permute-start(bf16[16,6656]{1,0:T(8,128)(2,1)S(1)} %constant_dynamic-update-slice_fusion.69), channel_id=1, source_target_pairs={{0,24},{1,25},{2,26},{3,27},{4,28},{5,29},{6,30},{7,31},{8,16},{9,... | collective-permute-start | bytes 638984 | tf_op jit(solution)/shard_map/ppermute | solution.py:162
  31.9 27.3 %collective-permute-start.12 = (bf16[16,6656]{1,0:T(8,128)(2,1)S(1)}, bf16[16,6656]{1,0:T(8,128)(2,1)S(1)}, u32[]{:S(2)}, u32[]{:S(2)}) collective-permute-start(bf16[16,6656]{1,0:T(8,128)(2,1)S(1)} %constant_dynamic-update-slice_fusion.69), channel_id=1, source_target_pairs={{0,16},{1,17},{2,18},{3,19},{4,20},{5,21},{6,22},{7,23},{8,24},{9,... | collective-permute-start | bytes 638984 | tf_op jit(solution)/shard_map/ppermute | solution.py:162
  41.9 230.3 %copy-start.1 = (bf16[1,512,512]{1,2,0:T(8,128)(2,1)}, bf16[1,512,512]{1,2,0:T(8,128)(2,1)S(1)}, u32[]{:S(2)}) copy-start(bf16[1,512,512]{1,2,0:T(8,128)(2,1)S(1)} %copy.250) | copy-start | bytes 1572868
  42.0 48.0 %copy-start.57 = (f32[512]{0:T(512)}, f32[512]{0:T(512)S(1)}, u32[]{:S(2)}) copy-start(f32[512]{0:T(512)S(1)} %broadcast_multiply_fusion.8) | copy-start | bytes 6148
  42.2 47.8 %copy-start.61 = (f32[512]{0:T(512)}, f32[512]{0:T(512)S(1)}, u32[]{:S(2)}) copy-start(f32[512]{0:T(512)S(1)} %add_rsqrt_fusion.2) | copy-start | bytes 6148
  49.7 9.5 %collective-permute-start.11 = (bf16[16,6656]{1,0:T(8,128)(2,1)S(1)}, bf16[16,6656]{1,0:T(8,128)(2,1)S(1)}, u32[]{:S(2)}, u32[]{:S(2)}) collective-permute-start(bf16[16,6656]{1,0:T(8,128)(2,1)S(1)} %constant_dynamic-update-slice_fusion.69), channel_id=1, source_target_pairs={{0,8},{1,9},{2,10},{3,11},{4,12},{5,13},{6,14},{7,15},{8,0},{9,1},... | collective-permute-start | bytes 638984 | tf_op jit(solution)/shard_map/ppermute | solution.py:162
  50.4 4.7 collective-permute-start.7
  52.1 4.9 collective-permute-start.3
  55.1 8.2 %collective-permute-start.9 = (bf16[128,768]{1,0:T(8,128)(2,1)S(1)}, bf16[128,768]{1,0:T(8,128)(2,1)S(1)}, u32[]{:S(2)}, u32[]{:S(2)}) collective-permute-start(bf16[128,768]{1,0:T(8,128)(2,1)S(1)} %pad_maximum_fusion.20), channel_id=1, source_target_pairs={{0,2},{1,3},{2,0},{3,1},{4,6},{5,7},{6,4},{7,5},{8,10},{9,11},{10,... | collective-permute-start | bytes 589832 | tf_op jit(solution)/shard_map/ppermute | solution.py:162
  57.0 5.7 collective-permute-start.8
  58.5 6.1 %collective-permute-start.5 = (bf16[128,896]{1,0:T(8,128)(2,1)S(1)}, bf16[128,896]{1,0:T(8,128)(2,1)S(1)}, u32[]{:S(2)}, u32[]{:S(2)}) collective-permute-start(bf16[128,896]{1,0:T(8,128)(2,1)S(1)} %pad_maximum_fusion.17), channel_id=1, source_target_pairs={{0,4},{1,5},{2,6},{3,7},{4,0},{5,1},{6,2},{7,3},{8,12},{9,13},{10,... | collective-permute-start | bytes 688136 | tf_op jit(solution)/shard_map/ppermute | solution.py:162
  59.1 26.7 %copy-start.34 = (bf16[16,6656]{1,0:T(8,128)(2,1)}, bf16[16,6656]{1,0:T(8,128)(2,1)S(1)}, u32[]{:S(2)}) copy-start(bf16[16,6656]{1,0:T(8,128)(2,1)S(1)} %collective-permute-done.12) | copy-start | bytes 638980
  59.1 5.5 collective-permute-start.4
  59.2 26.6 %copy-start.36 = (bf16[16,6656]{1,0:T(8,128)(2,1)}, bf16[16,6656]{1,0:T(8,128)(2,1)S(1)}, u32[]{:S(2)}) copy-start(bf16[16,6656]{1,0:T(8,128)(2,1)S(1)} %collective-permute-done.11) | copy-start | bytes 638980
  62.6 2.1 collective-permute-start.10
  64.7 22.4 %collective-permute-start.6 = (bf16[128,896]{1,0:T(8,128)(2,1)S(1)}, bf16[128,896]{1,0:T(8,128)(2,1)S(1)}, u32[]{:S(2)}, u32[]{:S(2)}) collective-permute-start(bf16[128,896]{1,0:T(8,128)(2,1)S(1)} %collective-permute-done.5), channel_id=1, source_target_pairs={{0,2},{1,3},{2,0},{3,1},{4,6},{5,7},{6,4},{7,5},{8,10},{9,11},{10,... | collective-permute-start | bytes 688136 | tf_op jit(solution)/shard_map/ppermute | solution.py:162
  94.3 59.5 %all-gather.6.cloned.1.call-start = ((), (), s32[]{:S(2)}) async-start(), calls=%async_computation.3 | async-start | bytes 1572864 | tf_op jit(solution)/shard_map/all_gather | solution.py:515
  95.4 12.4 %collective-permute-start.14 = (bf16[64,3328]{1,0:T(8,128)(2,1)}, bf16[64,3328]{1,0:T(8,128)(2,1)S(1)}, u32[]{:S(2)}, u32[]{:S(2)}) collective-permute-start(bf16[64,3328]{1,0:T(8,128)(2,1)} %get-tuple-element.715), channel_id=1, source_target_pairs={{0,4},{1,5},{2,6},{3,7},{4,0},{5,1},{6,2},{7,3},{8,12},{9,13},{10,... | collective-permute-start | bytes 1277960 | tf_op jit(solution)/shard_map/ppermute | solution.py:162
  97.7 18.1 %collective-permute-start.18 = (bf16[64,3328]{1,0:T(8,128)(2,1)}, bf16[64,3328]{1,0:T(8,128)(2,1)S(1)}, u32[]{:S(2)}, u32[]{:S(2)}) collective-permute-start(bf16[64,3328]{1,0:T(8,128)(2,1)} %get-tuple-element.714), channel_id=1, source_target_pairs={{0,1},{1,0},{2,3},{3,2},{4,5},{5,4},{6,7},{7,6},{8,9},{9,8},{10,11... | collective-permute-start | bytes 1277960 | tf_op jit(solution)/shard_map/ppermute | solution.py:162
  100.0 360.5 %reduce-scatter.7.cloned.1.call-start = ((), (), s32[]{:S(2)}) async-start(), calls=%async_computation.5 | async-start | bytes 1032192
  108.9 37.1 %collective-permute-start.16 = (bf16[128,3328]{1,0:T(8,128)(2,1)S(1)}, bf16[128,3328]{1,0:T(8,128)(2,1)S(1)}, u32[]{:S(2)}, u32[]{:S(2)}) collective-permute-start(bf16[128,3328]{1,0:T(8,128)(2,1)S(1)} %pad_maximum_fusion.11), channel_id=1, source_target_pairs={{0,2},{1,3},{2,0},{3,1},{4,6},{5,7},{6,4},{7,5},{8,10},{9,11},{10,... | collective-permute-start | bytes 2555912 | tf_op jit(solution)/shard_map/ppermute | solution.py:162
  109.0 30.5 %collective-permute-start.15 = (bf16[128,3328]{1,0:T(8,128)(2,1)S(1)}, bf16[128,3328]{1,0:T(8,128)(2,1)}, u32[]{:S(2)}, u32[]{:S(2)}) collective-permute-start(bf16[128,3328]{1,0:T(8,128)(2,1)S(1)} %pad_maximum_fusion.11), channel_id=1, source_target_pairs={{0,1},{1,0},{2,3},{3,2},{4,5},{5,4},{6,7},{7,6},{8,9},{9,8},{10,11... | collective-permute-start | bytes 2555912 | tf_op jit(solution)/shard_map/ppermute | solution.py:162
  116.9 22.6 %collective-permute-start.20 = (bf16[128,3328]{1,0:T(8,128)(2,1)S(1)}, bf16[128,3328]{1,0:T(8,128)(2,1)}, u32[]{:S(2)}, u32[]{:S(2)}) collective-permute-start(bf16[128,3328]{1,0:T(8,128)(2,1)S(1)} %pad_maximum_fusion.12), channel_id=1, source_target_pairs={{0,4},{1,5},{2,6},{3,7},{4,0},{5,1},{6,2},{7,3},{8,12},{9,13},{10,... | collective-permute-start | bytes 2555912 | tf_op jit(solution)/shard_map/ppermute | solution.py:162
  117.0 23.0 %collective-permute-start.19 = (bf16[128,3328]{1,0:T(8,128)(2,1)S(1)}, bf16[128,3328]{1,0:T(8,128)(2,1)S(1)}, u32[]{:S(2)}, u32[]{:S(2)}) collective-permute-start(bf16[128,3328]{1,0:T(8,128)(2,1)S(1)} %pad_maximum_fusion.12), channel_id=1, source_target_pairs={{0,2},{1,3},{2,0},{3,1},{4,6},{5,7},{6,4},{7,5},{8,10},{9,11},{10,... | collective-permute-start | bytes 2555912 | tf_op jit(solution)/shard_map/ppermute | solution.py:162
  139.5 44.2 %collective-permute-start.17 = (bf16[128,3328]{1,0:T(8,128)(2,1)}, bf16[128,3328]{1,0:T(8,128)(2,1)}, u32[]{:S(2)}, u32[]{:S(2)}) collective-permute-start(bf16[128,3328]{1,0:T(8,128)(2,1)} %collective-permute-done.15), channel_id=1, source_target_pairs={{0,2},{1,3},{2,0},{3,1},{4,6},{5,7},{6,4},{7,5},{8,10},{9,11},{10,... | collective-permute-start | bytes 2555912 | tf_op jit(solution)/shard_map/ppermute | solution.py:162
  139.5 41.1 %collective-permute-start.21 = (bf16[128,3328]{1,0:T(8,128)(2,1)}, bf16[128,3328]{1,0:T(8,128)(2,1)}, u32[]{:S(2)}, u32[]{:S(2)}) collective-permute-start(bf16[128,3328]{1,0:T(8,128)(2,1)} %collective-permute-done.20), channel_id=1, source_target_pairs={{0,2},{1,3},{2,0},{3,1},{4,6},{5,7},{6,4},{7,5},{8,10},{9,11},{10,... | collective-permute-start | bytes 2555912 | tf_op jit(solution)/shard_map/ppermute | solution.py:162
  178.3 30.9 %copy-start.67 = (f32[8,512]{1,0:T(8,128)}, f32[8,512]{1,0:T(8,128)S(1)}, u32[]{:S(2)}) copy-start(f32[8,512]{1,0:T(8,128)S(1)} %get-tuple-element.1209) | copy-start | bytes 49156
  178.3 14.5 %copy-start.33 = (bf16[128,3328]{1,0:T(8,128)(2,1)S(1)}, bf16[128,3328]{1,0:T(8,128)(2,1)}, u32[]{:S(2)}) copy-start(bf16[128,3328]{1,0:T(8,128)(2,1)} %copy-done.32) | copy-start | bytes 2555908
  178.3 23.6 %copy-start.31 = (bf16[128,3328]{1,0:T(8,128)(2,1)S(1)}, bf16[128,3328]{1,0:T(8,128)(2,1)}, u32[]{:S(2)}) copy-start(bf16[128,3328]{1,0:T(8,128)(2,1)} %copy-done.30) | copy-start | bytes 2555908
  178.3 30.1 %copy-start.35 = (bf16[16,6656]{1,0:T(8,128)(2,1)S(1)}, bf16[16,6656]{1,0:T(8,128)(2,1)}, u32[]{:S(2)}) copy-start(bf16[16,6656]{1,0:T(8,128)(2,1)} %copy-done.34) | copy-start | bytes 638980
  289.4 11.7 %copy-start.6 = (f32[512,512]{0,1:T(8,128)}, f32[512,512]{0,1:T(8,128)S(1)}, u32[]{:S(2)}) copy-start(f32[512,512]{0,1:T(8,128)S(1)} %get-tuple-element.758) | copy-start | bytes 3145732
  322.1 48.3 %copy-start.14 = (bf16[8,64,512]{2,1,0:T(8,128)(2,1)}, bf16[8,64,512]{2,1,0:T(8,128)(2,1)S(1)}, u32[]{:S(2)}) copy-start(bf16[8,64,512]{2,1,0:T(8,128)(2,1)S(1)} %fusion.91) | copy-start | bytes 1572868
  355.1 11.8 %copy-start.53 = (bf16[8,64,336]{2,1,0:T(8,128)(2,1)S(1)}, bf16[8,64,336]{2,1,0:T(8,128)(2,1)}, u32[]{:S(2)}) copy-start(bf16[8,64,336]{2,1,0:T(8,128)(2,1)} %fusion.97) | copy-start | bytes 1032196
  355.8 11.1 %copy-start.13 = (bf16[2,2,2,2,2,16,2048]{6,5,4,3,2,1,0:T(8,128)(2,1)}, bf16[2,2,2,2,2,16,2048]{6,5,4,3,2,1,0:T(8,128)(2,1)S(1)}, u32[]{:S(2)}) copy-start(bf16[2,2,2,2,2,16,2048]{6,5,4,3,2,1,0:T(8,128)(2,1)S(1)} %reverse_select_fusion.20) | copy-start | bytes 6291460
  366.9 68.4 %collective-permute-start.34 = (bf16[256,2048]{1,0:T(8,128)(2,1)}, bf16[256,2048]{1,0:T(8,128)(2,1)}, u32[]{:S(2)}, u32[]{:S(2)}) collective-permute-start(bf16[256,2048]{1,0:T(8,128)(2,1)} %constant_dynamic-update-slice_fusion.219), channel_id=1, source_target_pairs={{0,2},{1,3},{2,0},{3,1},{4,6},{5,7},{6,4},{7,5},{8,10},{9,11},{10,... | collective-permute-start | bytes 3145736 | tf_op jit(solution)/shard_map/ppermute | solution.py:162
  370.2 126.4 %reduce-scatter.5.cloned.1.call-start = ((), (), s32[]{:S(2)}) async-start(), calls=%async_computation.4 | async-start | bytes 3145728 | tf_op jit(solution)/shard_map/reduce_scatter | solution.py:610
  390.4 22.9 %copy-start.72 = (bf16[2048]{0:T(1024)(128)(2,1)S(1)}, bf16[2048]{0:T(1024)(128)(2,1)}, u32[]{:S(2)}) copy-start(bf16[2048]{0:T(1024)(128)(2,1)} %get-tuple-element.767) | copy-start | bytes 12292
  390.4 23.3 %copy-start.76 = (bf16[512]{0:T(512)(128)(2,1)S(1)}, bf16[512]{0:T(512)(128)(2,1)}, u32[]{:S(2)}) copy-start(bf16[512]{0:T(512)(128)(2,1)} %get-tuple-element.765) | copy-start | bytes 3076
  390.4 24.2 %copy-start.71 = (bf16[512]{0:T(512)(128)(2,1)S(1)}, bf16[512]{0:T(512)(128)(2,1)}, u32[]{:S(2)}) copy-start(bf16[512]{0:T(512)(128)(2,1)} %get-tuple-element.591) | copy-start | bytes 3076
  419.9 27.6 %collective-permute-start.31 = (bf16[256,2048]{1,0:T(8,128)(2,1)}, bf16[256,2048]{1,0:T(8,128)(2,1)}, u32[]{:S(2)}, u32[]{:S(2)}) collective-permute-start(bf16[256,2048]{1,0:T(8,128)(2,1)} %constant_dynamic-update-slice_fusion.195), channel_id=1, source_target_pairs={{0,2},{1,3},{2,0},{3,1},{4,6},{5,7},{6,4},{7,5},{8,10},{9,11},{10,... | collective-permute-start | bytes 3145736 | tf_op jit(solution)/shard_map/ppermute | solution.py:162
  430.1 30.4 %copy-start.42 = (bf16[1,168,512]{2,1,0:T(8,128)(2,1)S(1)}, bf16[1,168,512]{2,1,0:T(8,128)(2,1)}, u32[]{:S(2)}) copy-start(bf16[1,168,512]{2,1,0:T(8,128)(2,1)} %param.29) | copy-start | bytes 516100
  447.1 15.8 %collective-permute-start.35 = (bf16[128,2048]{1,0:T(8,128)(2,1)}, bf16[128,2048]{1,0:T(8,128)(2,1)}, u32[]{:S(2)}, u32[]{:S(2)}) collective-permute-start(bf16[128,2048]{1,0:T(8,128)(2,1)} %constant_dynamic-update-slice_fusion.235), channel_id=1, source_target_pairs={{0,4},{1,5},{2,6},{3,7},{4,0},{5,1},{6,2},{7,3},{8,12},{9,13},{10,... | collective-permute-start | bytes 1572872 | tf_op jit(solution)/shard_map/ppermute | solution.py:162
  459.6 15.1 %collective-permute-start.32 = (bf16[128,2048]{1,0:T(8,128)(2,1)}, bf16[128,2048]{1,0:T(8,128)(2,1)}, u32[]{:S(2)}, u32[]{:S(2)}) collective-permute-start(bf16[128,2048]{1,0:T(8,128)(2,1)} %constant_dynamic-update-slice_fusion.211), channel_id=1, source_target_pairs={{0,1},{1,0},{2,3},{3,2},{4,5},{5,4},{6,7},{7,6},{8,9},{9,8},{10,11... | collective-permute-start | bytes 1572872 | tf_op jit(solution)/shard_map/ppermute | solution.py:162
  462.9 25.5 %copy-start.54 = (bf16[168,1024]{1,0:T(8,128)(2,1)S(1)}, bf16[168,1024]{1,0:T(8,128)(2,1)}, u32[]{:S(2)}) copy-start(bf16[168,1024]{1,0:T(8,128)(2,1)} %reduce-scatter.7.cloned.1.call-done) | copy-start | bytes 1032196
  464.2 14.9 %collective-permute-start.36 = (bf16[64,2048]{1,0:T(8,128)(2,1)S(1)}, bf16[64,2048]{1,0:T(8,128)(2,1)S(1)}, u32[]{:S(2)}, u32[]{:S(2)}) collective-permute-start(bf16[64,2048]{1,0:T(8,128)(2,1)S(1)} %pad_maximum_fusion.16), channel_id=1, source_target_pairs={{0,1},{1,0},{2,3},{3,2},{4,5},{5,4},{6,7},{7,6},{8,9},{9,8},{10,11... | collective-permute-start | bytes 786440 | tf_op jit(solution)/shard_map/ppermute | solution.py:162
  476.1 6.4 %collective-permute-start.33 = (bf16[64,2048]{1,0:T(8,128)(2,1)S(1)}, bf16[64,2048]{1,0:T(8,128)(2,1)S(1)}, u32[]{:S(2)}, u32[]{:S(2)}) collective-permute-start(bf16[64,2048]{1,0:T(8,128)(2,1)S(1)} %pad_maximum_fusion.15), channel_id=1, source_target_pairs={{0,4},{1,5},{2,6},{3,7},{4,0},{5,1},{6,2},{7,3},{8,12},{9,13},{10,... | collective-permute-start | bytes 786440 | tf_op jit(solution)/shard_map/ppermute | solution.py:162
  483.8 7.1 %collective-permute-start.37 = (bf16[16,4096]{1,0:T(8,128)(2,1)S(1)}, bf16[16,4096]{1,0:T(8,128)(2,1)S(1)}, u32[]{:S(2)}, u32[]{:S(2)}) collective-permute-start(bf16[16,4096]{1,0:T(8,128)(2,1)S(1)} %pad_maximum_fusion.24), channel_id=1, source_target_pairs={{0,8},{1,9},{2,10},{3,11},{4,12},{5,13},{6,14},{7,15},{8,0},{9,1},... | collective-permute-start | bytes 393224 | tf_op jit(solution)/shard_map/ppermute | solution.py:162
  485.1 10.0 %collective-permute-start.38 = (bf16[16,4096]{1,0:T(8,128)(2,1)S(1)}, bf16[16,4096]{1,0:T(8,128)(2,1)S(1)}, u32[]{:S(2)}, u32[]{:S(2)}) collective-permute-start(bf16[16,4096]{1,0:T(8,128)(2,1)S(1)} %pad_maximum_fusion.25), channel_id=1, source_target_pairs={{0,16},{1,17},{2,18},{3,19},{4,20},{5,21},{6,22},{7,23},{8,24},{9,... | collective-permute-start | bytes 393224 | tf_op jit(solution)/shard_map/ppermute | solution.py:162
  488.2 7.0 %collective-permute-start.39 = (bf16[16,4096]{1,0:T(8,128)(2,1)S(1)}, bf16[16,4096]{1,0:T(8,128)(2,1)S(1)}, u32[]{:S(2)}, u32[]{:S(2)}) collective-permute-start(bf16[16,4096]{1,0:T(8,128)(2,1)S(1)} %pad_maximum_fusion.26), channel_id=1, source_target_pairs={{0,24},{1,25},{2,26},{3,27},{4,28},{5,29},{6,30},{7,31},{8,16},{9,... | collective-permute-start | bytes 393224 | tf_op jit(solution)/shard_map/ppermute | solution.py:162
  519.0 2.4 collective-permute-start.25
  520.3 3.1 collective-permute-start.22
  521.7 11.9 %collective-permute-start.26 = (bf16[128,1664]{1,0:T(8,128)(2,1)S(1)}, bf16[128,1664]{1,0:T(8,128)(2,1)S(1)}, u32[]{:S(2)}, u32[]{:S(2)}) collective-permute-start(bf16[128,1664]{1,0:T(8,128)(2,1)S(1)} %constant_dynamic-update-slice_fusion.187), channel_id=1, source_target_pairs={{0,4},{1,5},{2,6},{3,7},{4,0},{5,1},{6,2},{7,3},{8,12},{9,13},{10,... | collective-permute-start | bytes 1277960 | tf_op jit(solution)/shard_map/ppermute | solution.py:162
  523.7 17.6 %collective-permute-start.23 = (bf16[128,2560]{1,0:T(8,128)(2,1)S(1)}, bf16[128,2560]{1,0:T(8,128)(2,1)S(1)}, u32[]{:S(2)}, u32[]{:S(2)}) collective-permute-start(bf16[128,2560]{1,0:T(8,128)(2,1)S(1)} %constant_dynamic-update-slice_fusion.163), channel_id=1, source_target_pairs={{0,1},{1,0},{2,3},{3,2},{4,5},{5,4},{6,7},{7,6},{8,9},{9,8},{10,11... | collective-permute-start | bytes 1966088 | tf_op jit(solution)/shard_map/ppermute | solution.py:162
  533.7 11.4 %collective-permute-start.27 = (bf16[64,1664]{1,0:T(8,128)(2,1)S(1)}, bf16[64,1664]{1,0:T(8,128)(2,1)S(1)}, u32[]{:S(2)}, u32[]{:S(2)}) collective-permute-start(bf16[64,1664]{1,0:T(8,128)(2,1)S(1)} %pad_maximum_fusion.19), channel_id=1, source_target_pairs={{0,1},{1,0},{2,3},{3,2},{4,5},{5,4},{6,7},{7,6},{8,9},{9,8},{10,11... | collective-permute-start | bytes 638984 | tf_op jit(solution)/shard_map/ppermute | solution.py:162
  541.6 8.2 %collective-permute-start.24 = (bf16[64,2560]{1,0:T(8,128)(2,1)S(1)}, bf16[64,2560]{1,0:T(8,128)(2,1)S(1)}, u32[]{:S(2)}, u32[]{:S(2)}) collective-permute-start(bf16[64,2560]{1,0:T(8,128)(2,1)S(1)} %pad_maximum_fusion.14), channel_id=1, source_target_pairs={{0,4},{1,5},{2,6},{3,7},{4,0},{5,1},{6,2},{7,3},{8,12},{9,13},{10,... | collective-permute-start | bytes 983048 | tf_op jit(solution)/shard_map/ppermute | solution.py:162
  549.9 9.1 %collective-permute-start.28 = (bf16[16,4224]{1,0:T(8,128)(2,1)S(1)}, bf16[16,4224]{1,0:T(8,128)(2,1)S(1)}, u32[]{:S(2)}, u32[]{:S(2)}) collective-permute-start(bf16[16,4224]{1,0:T(8,128)(2,1)S(1)} %pad_maximum_fusion.21), channel_id=1, source_target_pairs={{0,8},{1,9},{2,10},{3,11},{4,12},{5,13},{6,14},{7,15},{8,0},{9,1},... | collective-permute-start | bytes 405512 | tf_op jit(solution)/shard_map/ppermute | solution.py:162
  552.0 11.0 %collective-permute-start.29 = (bf16[16,4224]{1,0:T(8,128)(2,1)S(1)}, bf16[16,4224]{1,0:T(8,128)(2,1)S(1)}, u32[]{:S(2)}, u32[]{:S(2)}) collective-permute-start(bf16[16,4224]{1,0:T(8,128)(2,1)S(1)} %pad_maximum_fusion.22), channel_id=1, source_target_pairs={{0,16},{1,17},{2,18},{3,19},{4,20},{5,21},{6,22},{7,23},{8,24},{9,... | collective-permute-start | bytes 405512 | tf_op jit(solution)/shard_map/ppermute | solution.py:162
  553.7 9.2 %collective-permute-start.30 = (bf16[16,4224]{1,0:T(8,128)(2,1)}, bf16[16,4224]{1,0:T(8,128)(2,1)S(1)}, u32[]{:S(2)}, u32[]{:S(2)}) collective-permute-start(bf16[16,4224]{1,0:T(8,128)(2,1)} %pad_maximum_fusion.23), channel_id=1, source_target_pairs={{0,24},{1,25},{2,26},{3,27},{4,28},{5,29},{6,30},{7,31},{8,16},{9,... | collective-permute-start | bytes 405512 | tf_op jit(solution)/shard_map/ppermute | solution.py:162
  (66 other events, 246.0 us)
Sparse Core Ops, SparseCore 0:
  94.4 33.5 all-gather.3
  130.1 21.0 all-gather.5
  370.3 15.9 reduce-scatter.6
  427.6 31.4 reduce-scatter.4

commit v2 on v0

--- a/solution.py
+++ b/solution.py
@@ -1,6 +1,8 @@
 import jax
 import jax.numpy as jnp
 from jax import lax
+from jax.experimental import pallas as pl
+from jax.experimental.pallas import tpu as pltpu
 from jax.sharding import PartitionSpec as P
 
 HEADS = 8
@@ -150,7 +152,7 @@
     )
 
 
-def per_device(
+def general_device(
     target_states,
     source_states,
     target_segments,
@@ -360,7 +362,664 @@
     )
 
 
-def solution(mesh):
+F32, BF16 = jnp.float32, jnp.bfloat16
+BLOCK = 16
+AXES = ("rows", "seq")
+FLIP_Y, FLIP_CORE, FLIP_X, FLIP_Z = 1, 2, 4, 8
+MODEL, FEED, OWN, WINDOW, HALF_SOURCE = 512, 2048, 512, 256, 192
+KEYS, SOURCES = OWN + WINDOW, 2 * HALF_SOURCE
+TILE = 128
+MASKED = -1000000000.0
+SCALE = HD ** (-0.5)
+
+
+def exchange(value, flip):
+    return lax.ppermute(value, AXES, [(device, device ^ flip) for device in range(32)])
+
+
+def gather_pair(both, width):
+    both = jnp.concatenate([both] + [exchange(both, FLIP_Z * i) for i in (1, 2, 3)], 0)
+    out = []
+    for value, first, second in (
+        (both[:, :width], FLIP_X, FLIP_Y), (both[:, width:], FLIP_Y, FLIP_X)
+    ):
+        value = jnp.concatenate([value, exchange(value, first)], 0)
+        other = exchange(value, second)
+        out.append([value, other, exchange(value, FLIP_CORE), exchange(other, FLIP_CORE)])
+    return out[0] + out[1]
+
+
+def scatter_steps(kept, sent, first, second):
+    came = exchange(sent, FLIP_CORE)
+    for flip in (first, second):
+        half = kept.shape[0] // 2
+        sent = kept[half:] + came[half:]
+        kept = kept[:half] + came[:half]
+        came = exchange(sent, flip)
+    return kept + came
+
+
+def scatter_pair(left, right):
+    left = scatter_steps(left[0], left[1], FLIP_Y, FLIP_X)
+    right = scatter_steps(right[0], right[1], FLIP_X, FLIP_Y)
+    both = jnp.concatenate([left, right], 1)
+    return [both[:BLOCK]] + [
+        exchange(both[BLOCK * i : BLOCK * (i + 1)], FLIP_Z * i) for i in (1, 2, 3)
+    ]
+
+
+def block_flips(first, second):
+    return [
+        (core * 2 + b, (a * 4 + z) * BLOCK, core * FLIP_CORE + b * second + a * first + z * FLIP_Z)
+        for core in (0, 1) for b in (0, 1) for a in (0, 1) for z in range(4)
+    ]
+
+
+LEFT_FLIPS, RIGHT_FLIPS = block_flips(FLIP_X, FLIP_Y), block_flips(FLIP_Y, FLIP_X)
+
+
+def nn(left, right):
+    return jnp.dot(left, right, preferred_element_type=F32)
+
+
+def load_blocks(me, flips, pieces, columns, target, target_columns, semaphore):
+    for piece, row, flip in flips:
+        place = pl.multiple_of((me ^ flip) * BLOCK, BLOCK)
+        pltpu.make_async_copy(
+            pieces[piece].at[pl.ds(row, BLOCK), columns],
+            target.at[pl.ds(place, BLOCK), target_columns],
+            semaphore,
+        ).start()
+
+
+def wait_all(target, semaphore):
+    pltpu.make_async_copy(target, target, semaphore).wait()
+
+
+def store_blocks(me, flips, source, columns, targets, target_columns, semaphore):
+    for piece, row, flip in flips:
+        place = pl.multiple_of((me ^ flip) * BLOCK, BLOCK)
+        pltpu.make_async_copy(
+            source.at[pl.ds(place, BLOCK), columns],
+            targets[piece // 2].at[pl.ds((piece % 2) * 128 + row, BLOCK), target_columns],
+            semaphore,
+        ).start()
+
+
+def normed_rows(value):
+    centered = value - jnp.mean(value, -1, keepdims=True)
+    inverse = lax.rsqrt(jnp.mean(centered * centered, -1, keepdims=True) + 1e-05)
+    return centered * inverse, inverse
+
+
+def norm_back_rows(upstream, normed, inverse, gain):
+    scaled = upstream * gain
+    first_mean = jnp.mean(scaled, -1, keepdims=True)
+    second_mean = jnp.mean(scaled * normed, -1, keepdims=True)
+    return inverse * (scaled - first_mean - normed * second_mean)
+
+
+def column_sum(value):
+    return jnp.sum(value, 0, keepdims=True)
+
+
+def own_segments_of(index, segments):
+    return jnp.where(index == 0, segments[:, :OWN], segments[:, OWN:]).astype(F32)
+
+
+def key_segments_of(index, segments):
+    near = jnp.where(index == 0, segments[:, OWN:KEYS], segments[:, OWN - WINDOW : OWN])
+    return jnp.concatenate([own_segments_of(index, segments), near.astype(F32)], 1)
+
+
+def spread(row):
+    return jnp.broadcast_to(row, (TILE, row.shape[1])).T
+
+
+def lane_half(shape, half):
+    lanes = lax.broadcasted_iota(jnp.int32, shape, 1)
+    return (lanes < HD) if half == 0 else (lanes >= HD)
+
+
+def attend(queries, keys, values, mixed, log_rows, query_seg, key_row):
+    (key_ref, key_at), (value_ref, value_at) = keys, values
+    count = key_row.shape[1]
+
+    def block(index, unused):
+        rows = pl.ds(pl.multiple_of(index * TILE, TILE), TILE)
+        same = jnp.concatenate([query_seg[rows, :]] * (count // TILE), 1) == key_row
+        bias = jnp.where(same, 0.0, MASKED)
+        lanes = lax.broadcasted_iota(jnp.int32, (TILE, TILE), 1)
+        logs = jnp.zeros((TILE, TILE), F32)
+        for pair in range(HEADS // 2):
+            at = pair * TILE
+            query = queries[rows, at : at + TILE]
+            key = key_ref[:, key_at + at : key_at + at + TILE]
+            value = value_ref[:, value_at + at : value_at + at + TILE]
+            halves = []
+            for half in range(2):
+                masked = jnp.where(lane_half(query.shape, half), query, jnp.zeros_like(query))
+                scores = against(masked, key) + bias
+                top = jnp.max(scores, -1, keepdims=True)
+                weights = jnp.exp(scores - top)
+                total = jnp.sum(weights, -1, keepdims=True)
+                halves.append(nn(weights.astype(BF16), value) * (1.0 / total))
+                logs = jnp.where(lanes == pair * 2 + half, top + jnp.log(total), logs)
+            mixed[rows, at : at + TILE] = jnp.where(
+                lane_half(halves[0].shape, 0), halves[0], halves[1]
+            ).astype(BF16)
+        log_rows[:, rows] = logs.T[:HEADS]
+        return unused
+
+    lax.fori_loop(0, OWN // TILE, block, 0)
+
+
+def head_dots(upstream, mixed):
+    head = lax.broadcasted_iota(jnp.int32, (HEADS, MODEL), 1) // HD
+    ones = (head == lax.broadcasted_iota(jnp.int32, (HEADS, MODEL), 0)).astype(F32)
+    return lax.dot_general(
+        ones, upstream.astype(F32) * mixed.astype(F32), (((1,), (1,)), ((), ())),
+        precision=lax.Precision.HIGHEST, preferred_element_type=F32,
+    )
+
+
+def attend_back(
+    queries, upstream, keys, values, log_rows, dot_rows, query_row, key_seg, query_grad, pair_grad
+):
+    (key_ref, key_at), (value_ref, value_at) = keys, values
+    query_grad[...] = jnp.zeros_like(query_grad)
+
+    def block(index, unused):
+        rows = pl.ds(pl.multiple_of(index * TILE, TILE), TILE)
+        same = jnp.concatenate([key_seg[rows, :]] * (OWN // TILE), 1) == query_row
+        bias = jnp.where(same, 0.0, MASKED)
+        for pair in range(HEADS // 2):
+            at = pair * TILE
+            query = queries[:, at : at + TILE]
+            grad = upstream[:, at : at + TILE]
+            key = key_ref[rows, key_at + at : key_at + at + TILE]
+            value = value_ref[rows, value_at + at : value_at + at + TILE]
+            total = jnp.zeros((OWN, TILE), F32)
+            key_parts, value_parts = [], []
+            for half in range(2):
+                head = pair * 2 + half
+                keep = lane_half(key.shape, half)
+                one_key = jnp.where(keep, key, jnp.zeros_like(key))
+                one_value = jnp.where(keep, value, jnp.zeros_like(value))
+                weights = jnp.exp(against(one_key, query) + (bias - log_rows[head : head + 1, :]))
+                grads = against(one_value, grad) - dot_rows[head : head + 1, :]
+                score_grad = (weights * grads).astype(BF16)
+                value_parts.append(nn(weights.astype(BF16), grad))
+                key_parts.append(nn(score_grad, query))
+                total = total + transposed(score_grad, one_key)
+            query_grad[:, at : at + TILE] += total
+            keep = lane_half(key_parts[0].shape, 0)
+            pair_grad[rows, at : at + TILE] = jnp.where(keep, *key_parts).astype(BF16)
+            pair_grad[rows, MODEL + at : MODEL + at + TILE] = jnp.where(keep, *value_parts).astype(BF16)
+        return unused
+
+    lax.fori_loop(0, key_seg.shape[0] // TILE, block, 0)
+
+
+def pack_body(
+    place, vectors, project, output, query, keyval, crossout, up, down, states,
+    one, two, three, window, semaphore
+):
+    me, side = place[0], place[1]
+    send = pltpu.make_async_copy(
+        states.at[pl.ds(pl.multiple_of((1 - side) * WINDOW, WINDOW), WINDOW), :], window, semaphore
+    )
+    send.start()
+    values = jnp.broadcast_to(vectors[...].astype(F32), (8, 256))
+    lanes = lax.broadcasted_iota(jnp.int32, (8, TILE), 1)
+    rows = lax.broadcasted_iota(jnp.int32, (8, TILE), 0)
+    packed = jnp.zeros((8, TILE), F32)
+    spot, wide = (me & 7) * 16, (me & 1) * 64
+    for row in range(7):
+        moved = pltpu.roll(values, spot + 256 - 16 * row, 1)[:, :TILE]
+        inside = jnp.logical_and(lanes >= spot, lanes < spot + 16)
+        packed = jnp.where(jnp.logical_and(rows == row, inside), moved, packed)
+    moved = pltpu.roll(values, wide + 256 - 112, 1)[:, :TILE]
+    inside = jnp.logical_and(lanes >= wide, lanes < wide + 64)
+    packed = jnp.where(jnp.logical_and(rows == 7, inside), moved, packed)
+    one[:, :1536] = project[...]
+    one[:, 1536:] = jnp.concatenate([packed, jnp.zeros((8, TILE), F32)], 0).astype(BF16)
+    two[:, :512] = output[...]
+    two[:, 512:1024] = query[...]
+    two[:, 1024:2048] = keyval[...]
+    two[:, 2048:] = crossout[...]
+    three[:, :FEED] = up[...]
+    for part in range(4):
+        three[:, FEED + part * 512 : FEED + (part + 1) * 512] = down[part * BLOCK : (part + 1) * BLOCK, :]
+    send.wait()
+
+
+def self_body(place, segments, states, window, *refs):
+    pieces, refs = refs[:8], refs[8:]
+    queries, pair, mixed, log_rows, lowered, vectors, up_bias, weight, packed, query_seg, sems = refs
+    me, side = place[0], place[1]
+    load_blocks(me, RIGHT_FLIPS, pieces[4:], slice(768, 896), packed, slice(0, 128), sems.at[0])
+    load_blocks(me, LEFT_FLIPS, pieces[:4], slice(0, 768), weight, slice(0, 768), sems.at[1])
+    load_blocks(me, RIGHT_FLIPS, pieces[4:], slice(0, 768), weight, slice(768, 1536), sems.at[2])
+    query_seg[...] = spread(own_segments_of(side, segments[...]))
+    key_row = key_segments_of(side, segments[...])
+    wait_all(packed, sems.at[0])
+    for tile in range(4):
+        total = jnp.zeros((8, TILE), F32)
+        for i in range(8):
+            total = total + packed[(tile * 8 + i) * BLOCK : (tile * 8 + i + 1) * BLOCK, :].astype(F32)[:8]
+        vectors[:, tile * TILE : (tile + 1) * TILE] = total
+    for tile in range(16):
+        total = (
+            packed[2 * tile * BLOCK : (2 * tile + 1) * BLOCK, :].astype(F32)
+            + packed[(2 * tile + 1) * BLOCK : (2 * tile + 2) * BLOCK, :].astype(F32)
+        )
+        up_bias[:, tile * TILE : (tile + 1) * TILE] = total[7:8]
+    gain, shift = vectors[1:2, :], vectors[2:3, :]
+    for i in range(KEYS // TILE):
+        rows = slice(i * TILE, (i + 1) * TILE)
+        value = states[rows, :] if i < 4 else window[(i - 4) * TILE : (i - 3) * TILE, :]
+        lowered[rows, :] = (normed_rows(value.astype(F32))[0] * gain + shift).astype(BF16)
+    wait_all(weight.at[:, :768], sems.at[1])
+    wait_all(weight.at[:, 768:], sems.at[2])
+    for i in range(KEYS // 256):
+        rows = slice(i * 256, (i + 1) * 256)
+        if i < 2:
+            queries[rows, :] = (nn(lowered[rows, :], weight[:, :512]) .astype(BF16) * SCALE).astype(BF16)
+        pair[rows, :] = nn(lowered[rows, :], weight[:, 512:]).astype(BF16)
+    attend(queries, (pair, 0), (pair, MODEL), mixed, log_rows, query_seg, key_row)
+
+
+def cross_body(place, segments, source_segments, states, own_source, other_source, self_mixed, vectors, *refs):
+    pieces, refs = refs[:8], refs[8:]
+    after_self, lowered, queries, pair, mixed, log_rows, after_cross, source, weight, query_seg, sems = refs
+    me, side = place[0], place[1]
+    load_blocks(me, LEFT_FLIPS, pieces[:4], slice(0, 1280), weight, slice(0, 1280), sems.at[0])
+    load_blocks(me, RIGHT_FLIPS, pieces[4:], slice(0, 1280), weight, slice(1280, 2560), sems.at[1])
+    query_seg[...] = spread(own_segments_of(side, segments[...]))
+    key_row = source_segments[...].astype(F32)
+    source[:HALF_SOURCE, :] = jnp.where(side == 0, own_source[...], other_source[...])
+    source[HALF_SOURCE:, :] = jnp.where(side == 0, other_source[...], own_source[...])
+    gain, shift = vectors[3:4, :], vectors[4:5, :]
+    wait_all(weight.at[:, :1280], sems.at[0])
+    wait_all(weight.at[:, 1280:], sems.at[1])
+    pair[...] = nn(source[...], weight[:, 1024:2048]).astype(BF16)
+    for i in range(2):
+        rows = slice(i * 256, (i + 1) * 256)
+        value = states[rows, :].astype(F32) + nn(self_mixed[rows, :], weight[:, :512])
+        after_self[rows, :] = value
+        lowered[rows, :] = (normed_rows(value)[0] * gain + shift).astype(BF16)
+        queries[rows, :] = (nn(lowered[rows, :], weight[:, 512:1024]).astype(BF16) * SCALE).astype(BF16)
+    attend(queries, (pair, 0), (pair, MODEL), mixed, log_rows, query_seg, key_row)
+    for i in range(2):
+        rows = slice(i * 256, (i + 1) * 256)
+        after_cross[rows, :] = after_self[rows, :] + nn(mixed[rows, :], weight[:, 2048:])
+
+
+CHUNK = 512
+
+
+def feed_body(place, after_cross, output_grad, vectors, up_bias, *refs):
+    pieces, refs = refs[:8], refs[8:]
+    (
+        layer_out, after_grad, up_keep, up_send, down_keep, down_send, sums, bias_sums,
+        up, down, lowered, flipped, total, back, up_grad, down_grad, sems,
+    ) = refs
+    me = place[0]
+    load_blocks(me, LEFT_FLIPS, pieces[:4], slice(0, FEED), up, slice(0, FEED), sems.at[0])
+    for part in range(4):
+        for piece, row, flip in RIGHT_FLIPS:
+            spot = pl.multiple_of((me ^ flip) * 64 + part * BLOCK, BLOCK)
+            pltpu.make_async_copy(
+                pieces[4 + piece].at[pl.ds(row, BLOCK), slice(part * 512, (part + 1) * 512)],
+                down.at[pl.ds(spot, BLOCK), :],
+                sems.at[1],
+            ).start()
+    gain, shift = vectors[5:6, :], vectors[6:7, :]
+    for i in range(4):
+        rows = slice(i * TILE, (i + 1) * TILE)
+        low = (normed_rows(after_cross[rows, :])[0] * gain + shift).astype(BF16)
+        lowered[rows, :] = low
+    flipped[...] = lowered[...].T
+    total[...] = jnp.zeros_like(total)
+    back[...] = jnp.zeros_like(back)
+    wait_all(up, sems.at[0])
+    wait_all(down, sems.at[1])
+
+    def chunk(index, unused):
+        at = pl.ds(pl.multiple_of(index * CHUNK, CHUNK), CHUNK)
+        hidden = nn(lowered[...], up[:, at]) + up_bias[:, at]
+        square = hidden * hidden
+        inner = 0.7978845608028654 * hidden * (1.0 + 0.044715 * square)
+        curve = jnp.tanh(inner)
+        half = 0.5 * (1.0 + curve)
+        activated = (hidden * half).astype(BF16)
+        slope = half + (0.5 * 0.7978845608028654) * hidden * (1.0 - curve * curve) * (
+            1.0 + (3 * 0.044715) * square
+        )
+        total[...] += nn(activated, down[at, :])
+        down_grad[at, :] = transposed(activated, output_grad[...]).astype(BF16)
+        grad_hidden = (against(output_grad[...], down[at, :]) * slope).astype(BF16)
+        bias_sums[:, at] = column_sum(grad_hidden.astype(F32))
+        up_grad[:, at] = nn(flipped[...], grad_hidden).astype(BF16)
+        back[...] += against(grad_hidden, up[:, at])
+        return unused
+
+    lax.fori_loop(0, FEED // CHUNK, chunk, 0)
+    store_blocks(me, LEFT_FLIPS, up_grad, slice(0, FEED), (up_keep, up_send), slice(0, FEED), sems.at[2])
+    for part in range(4):
+        for piece, row, flip in RIGHT_FLIPS:
+            spot = pl.multiple_of((me ^ flip) * 64 + part * BLOCK, BLOCK)
+            pltpu.make_async_copy(
+                down_grad.at[pl.ds(spot, BLOCK), :],
+                (down_keep, down_send)[piece // 2].at[
+                    pl.ds((piece % 2) * 128 + row, BLOCK), slice(part * 512, (part + 1) * 512)
+                ],
+                sems.at[3],
+            ).start()
+    gain_sum, shift_sum, bias_sum = (jnp.zeros((1, MODEL), F32) for _ in range(3))
+    for i in range(4):
+        rows = slice(i * TILE, (i + 1) * TILE)
+        value, grad = after_cross[rows, :], output_grad[rows, :].astype(F32)
+        layer_out[rows, :] = (value + total[rows, :] + vectors[0:1, :]).astype(BF16)
+        normed, inverse = normed_rows(value)
+        upstream = back[rows, :]
+        after_grad[rows, :] = grad + norm_back_rows(upstream, normed, inverse, gain)
+        gain_sum, shift_sum = gain_sum + column_sum(upstream * normed), shift_sum + column_sum(upstream)
+        bias_sum = bias_sum + column_sum(grad)
+    zero = jnp.zeros((1, MODEL), F32)
+    sums[...] = jnp.concatenate([bias_sum, zero, zero, zero, zero, gain_sum, shift_sum, zero], 0)
+    wait_all(up_grad, sems.at[2])
+    wait_all(down_grad, sems.at[3])
+
+
+def cross_back_body(
+    place, segments, source_segments, own_source, other_source, after_self, lowered, queries, pair,
+    mixed, log_rows, after_grad, vectors, sums, *refs
+):
+    pieces, refs = refs[:8], refs[8:]
+    (
+        self_grad, source_own, source_send, left_keep, left_send, right_keep, right_send, new_sums,
+        source, weight, upstream, query_grad, pair_grad, left_grad, right_grad, key_seg, sems,
+    ) = refs
+    me, side = place[0], place[1]
+    load_blocks(me, RIGHT_FLIPS, pieces[4:], slice(0, 1280), weight, slice(1280, 2560), sems.at[1])
+    load_blocks(me, LEFT_FLIPS, pieces[:4], slice(0, 1280), weight, slice(0, 1280), sems.at[0])
+    key_seg[...] = spread(source_segments[...].astype(F32))
+    query_row = own_segments_of(side, segments[...])
+    source[:HALF_SOURCE, :] = jnp.where(side == 0, own_source[...], other_source[...])
+    source[HALF_SOURCE:, :] = jnp.where(side == 0, other_source[...], own_source[...])
+    wait_all(weight.at[:, 1280:], sems.at[1])
+    wait_all(weight.at[:, :1280], sems.at[0])
+    grad_low = after_grad[...].astype(BF16)
+    upstream[...] = against(grad_low, weight[:, 2048:]).astype(BF16)
+    left_grad[:, :512] = transposed(mixed[...], grad_low).astype(BF16)
+    dot_rows = head_dots(upstream[...], mixed[...])
+    attend_back(
+        queries, upstream, (pair, 0), (pair, MODEL), log_rows, dot_rows, query_row, key_seg,
+        query_grad, pair_grad,
+    )
+    asked = (query_grad[...] * SCALE).astype(BF16)
+    left_grad[:, 512:] = transposed(lowered[...], asked).astype(BF16)
+    right_grad[...] = transposed(source[...], pair_grad[...]).astype(BF16)
+    store_blocks(me, LEFT_FLIPS, left_grad, slice(0, 1024), (left_keep, left_send), slice(0, 1024), sems.at[2])
+    store_blocks(me, RIGHT_FLIPS, right_grad, slice(0, 1024), (right_keep, right_send), slice(0, 1024), sems.at[3])
+    back = against(pair_grad[...], weight[:, 1024:2048])
+    first, second = back[:HALF_SOURCE], back[HALF_SOURCE:]
+    source_own[...] = jnp.where(side == 0, first, second)
+    source_send[...] = jnp.where(side == 0, second, first).astype(BF16)
+    gain = vectors[3:4, :]
+    gain_sum, shift_sum = jnp.zeros((1, MODEL), F32), jnp.zeros((1, MODEL), F32)
+    for i in range(2):
+        rows = slice(i * 256, (i + 1) * 256)
+        normed, inverse = normed_rows(after_self[rows, :])
+        up = against(asked[rows, :], weight[:, 512:1024])
+        self_grad[rows, :] = after_grad[rows, :] + norm_back_rows(up, normed, inverse, gain)
+        gain_sum, shift_sum = gain_sum + column_sum(up * normed), shift_sum + column_sum(up)
+    zero = jnp.zeros((1, MODEL), F32)
+    new_sums[...] = sums[...] + jnp.concatenate(
+        [zero, zero, zero, gain_sum, shift_sum, zero, zero, zero], 0
+    )
+    wait_all(left_grad, sems.at[2])
+    wait_all(right_grad, sems.at[3])
+
+
+def self_back_body(
+    place, segments, states, window, lowered, queries, pair, mixed, log_rows, self_grad, vectors,
+    sums, bias_sums, *refs
+):
+    pieces, more, refs = refs[:8], refs[8:12], refs[12:]
+    (
+        own_back, send_back, left_keep, left_send, right_keep, right_send,
+        weight, output, upstream, query_grad, pair_grad, left_grad, right_grad, key_seg, sems,
+    ) = refs
+    me, side = place[0], place[1]
+    load_blocks(me, LEFT_FLIPS, more, slice(0, 512), output, slice(0, 512), sems.at[4])
+    load_blocks(me, LEFT_FLIPS, pieces[:4], slice(0, 768), weight, slice(0, 768), sems.at[0])
+    load_blocks(me, RIGHT_FLIPS, pieces[4:], slice(0, 768), weight, slice(768, 1536), sems.at[1])
+    key_seg[...] = spread(key_segments_of(side, segments[...]))
+    query_row = own_segments_of(side, segments[...])
+    wait_all(output, sems.at[4])
+    grad_low = self_grad[...].astype(BF16)
+    upstream[...] = against(grad_low, output[...]).astype(BF16)
+    right_grad[:, 512:1024] = transposed(mixed[...], grad_low).astype(BF16)
+    dot_rows = head_dots(upstream[...], mixed[...])
+    attend_back(
+        queries, upstream, (pair, 0), (pair, MODEL), log_rows, dot_rows, query_row, key_seg,
+        query_grad, pair_grad,
+    )
+    wait_all(weight.at[:, :768], sems.at[0])
+    wait_all(weight.at[:, 768:], sems.at[1])
+    asked = (query_grad[...] * SCALE).astype(BF16)
+    left_grad[:, :512] = transposed(lowered[:OWN, :], asked).astype(BF16)
+    left_grad[:, 512:] = transposed(lowered[...], pair_grad[:, :512]).astype(BF16)
+    right_grad[:, :512] = transposed(lowered[...], pair_grad[:, 512:]).astype(BF16)
+    store_blocks(me, LEFT_FLIPS, left_grad, slice(0, 1024), (left_keep, left_send), slice(0, 1024), sems.at[2])
+    gain_sum, shift_sum = jnp.zeros((1, MODEL), F32), jnp.zeros((1, MODEL), F32)
+    for i in range(3):
+        rows = slice(i * 256, (i + 1) * 256)
+        back = against(pair_grad[rows, :], weight[:, 512:])
+        if i < 2:
+            back = back + against(asked[rows, :], weight[:, :512])
+            own_back[rows, :] = back
+            value = states[rows, :]
+        else:
+            send_back[...] = back.astype(BF16)
+            value = window[...]
+        normed = normed_rows(value.astype(F32))[0]
+        gain_sum, shift_sum = gain_sum + column_sum(back * normed), shift_sum + column_sum(back)
+    zero = jnp.zeros((1, MODEL), F32)
+    sums = sums[...] + jnp.concatenate([zero, gain_sum, shift_sum, zero, zero, zero, zero, zero], 0)
+    last = lax.broadcasted_iota(jnp.int32, (8, TILE), 0) == 7
+    for device in range(32):
+        tile, wide = device // 8 * TILE, device // 2 * TILE
+        value = jnp.where(last, bias_sums[:, wide : wide + TILE], sums[:, tile : tile + TILE])
+        high = value.astype(BF16).astype(F32)
+        right_grad[device * BLOCK : (device + 1) * BLOCK, 1024:] = jnp.concatenate(
+            [high, value - high], 0
+        ).astype(BF16)
+    store_blocks(me, RIGHT_FLIPS, right_grad, slice(0, 1152), (right_keep, right_send), slice(0, 1152), sems.at[3])
+    wait_all(left_grad, sems.at[2])
+    wait_all(right_grad, sems.at[3])
+
+
+def target_body(place, back, came, states, self_grad, vectors, out):
+    gain = vectors[1:2, :]
+    for i in range(4):
+        rows = slice(i * TILE, (i + 1) * TILE)
+        here = (i < 2) == (place[1] == 1)
+        extra = came[(i % 2) * TILE : (i % 2 + 1) * TILE, :].astype(F32)
+        upstream = back[rows, :] + jnp.where(here, extra, 0.0)
+        normed, inverse = normed_rows(states[rows, :].astype(F32))
+        out[rows, :] = self_grad[rows, :] + norm_back_rows(upstream, normed, inverse, gain)
+
+
+def finish_body(place, *refs):
+    feed, cross, last, outs = refs[:4], refs[4:8], refs[8:12], refs[12:]
+    project, output, query, keyval, crossout, up, down, small = outs
+    me = place[0]
+
+    def total(parts, begin, end):
+        value = parts[0][:, begin:end].astype(F32)
+        for part in parts[1:]:
+            value = value + part[:, begin:end].astype(F32)
+        return value
+
+    up[...] = total(feed, 0, FEED)
+    for part in range(4):
+        down[part * BLOCK : (part + 1) * BLOCK, :] = total(feed, FEED + part * 512, FEED + (part + 1) * 512)
+    crossout[...] = total(cross, 0, 512)
+    query[...] = total(cross, 512, 1024)
+    keyval[...] = total(cross, 1024, 2048)
+    project[...] = total(last, 0, 1536)
+    output[...] = total(last, 1536, 2048)
+    value = total(last, 2048, 2176)
+    value = value[:8] + value[8:]
+    narrow = pltpu.roll(value, (TILE - (me & 7) * 16) & 127, 1)
+    wide = pltpu.roll(value, (TILE - (me & 1) * 64) & 127, 1)
+    last_row = lax.broadcasted_iota(jnp.int32, (8, TILE), 0) == 7
+    small[...] = jnp.where(last_row, wide, narrow)
+
+
+def shape_of(*shape, dtype=BF16):
+    return jax.ShapeDtypeStruct(shape, dtype)
+
+
+VMEM_SPEC = pl.BlockSpec(memory_space=pltpu.VMEM)
+ANY_SPEC = pl.BlockSpec(memory_space=pl.ANY)
+SMEM_SPEC = pl.BlockSpec(memory_space=pltpu.SMEM)
+
+
+def call(body, name, place, inputs, pieces, outs, scratch, flops, any_outs=(), any_ins=()):
+    return pl.pallas_call(
+        body,
+        name=name,
+        out_shape=outs,
+        in_specs=[SMEM_SPEC]
+        + [ANY_SPEC if i in any_ins else VMEM_SPEC for i in range(len(inputs))]
+        + [ANY_SPEC] * len(pieces),
+        out_specs=[ANY_SPEC if i in any_outs else VMEM_SPEC for i in range(len(outs))],
+        scratch_shapes=scratch,
+        compiler_params=pltpu.CompilerParams(vmem_limit_bytes=40 * 2**20),
+        cost_estimate=pl.CostEstimate(flops=flops, bytes_accessed=4 * 2**20, transcendentals=0),
+    )(place, *inputs, *pieces)
+
+
+def fast_device(
+    target_states, source_states, target_segments, source_segments, output_grad, self_project,
+    self_output, cross_query, cross_keyval, cross_output, hidden_up, hidden_bias, hidden_down,
+    output_bias, first_gain, first_shift, second_gain, second_shift, third_gain, third_shift,
+):
+    vmem, dma = pltpu.VMEM, pltpu.SemaphoreType.DMA
+    side = lax.axis_index("seq")
+    place = jnp.stack([lax.axis_index("rows") * 2 + side, side]).astype(jnp.int32)
+    states, grad = target_states[0], output_grad[0]
+    small = jnp.concatenate([
+        output_bias, first_gain, first_shift, second_gain, second_shift, third_gain, third_shift,
+        hidden_bias, jnp.zeros((80,), BF16),
+    ]).reshape(1, 256)
+    one, two, three, near = call(
+        pack_body, "pack", place,
+        [small, self_project, self_output, cross_query, cross_keyval, cross_output, hidden_up, hidden_down, states],
+        [], [shape_of(16, 1664), shape_of(16, 2560), shape_of(16, 4096), shape_of(WINDOW, MODEL)],
+        [dma], 1000000, any_outs=(3,), any_ins=(8,),
+    )
+    window = exchange(near, FLIP_Y)
+    pieces_one = gather_pair(one, 768)
+    pieces_two = gather_pair(two, 1280)
+    pieces_three = gather_pair(three, FEED)
+    half = source_states.shape[1]
+    own_source = jnp.pad(source_states[0], ((0, HALF_SOURCE - half), (0, 0)))
+    other_source = exchange(own_source, FLIP_Y)
+    gap = jnp.full((1, HALF_SOURCE - half), -1, jnp.int32)
+    source_seg = jnp.concatenate([source_segments[:, :half], gap, source_segments[:, half:], gap], 1)
+
+    queries, pair, mixed, logs, lowered, vectors, up_bias = call(
+        self_body, "self_forward", place, [target_segments, states, window], pieces_one,
+        [
+            shape_of(OWN, MODEL), shape_of(KEYS, 2 * MODEL), shape_of(OWN, MODEL), shape_of(HEADS, OWN, dtype=F32),
+            shape_of(KEYS, MODEL), shape_of(8, MODEL, dtype=F32), shape_of(1, FEED, dtype=F32),
+        ],
+        [vmem((MODEL, 1536), BF16), vmem((MODEL, TILE), BF16), vmem((OWN, TILE), F32), dma((3,))],
+        5000000000,
+    )
+    after_self, lowered_two, queries_two, pair_two, mixed_two, logs_two, after_cross = call(
+        cross_body, "cross_forward", place,
+        [target_segments, source_seg, states, own_source, other_source, mixed, vectors], pieces_two,
+        [
+            shape_of(OWN, MODEL, dtype=F32), shape_of(OWN, MODEL), shape_of(OWN, MODEL), shape_of(SOURCES, 2 * MODEL),
+            shape_of(OWN, MODEL), shape_of(HEADS, OWN, dtype=F32), shape_of(OWN, MODEL, dtype=F32),
+        ],
+        [vmem((SOURCES, MODEL), BF16), vmem((MODEL, 2560), BF16), vmem((OWN, TILE), F32), dma((2,))],
+        5000000000,
+    )
+    layer_out, after_grad, up_keep, up_send, down_keep, down_send, sums, bias_sums = call(
+        feed_body, "feed", place, [after_cross, grad, vectors, up_bias], pieces_three,
+        [shape_of(OWN, MODEL), shape_of(OWN, MODEL, dtype=F32)] + [shape_of(256, FEED)] * 4
+        + [shape_of(8, MODEL, dtype=F32), shape_of(1, FEED, dtype=F32)],
+        [
+            vmem((MODEL, FEED), BF16), vmem((FEED, MODEL), BF16), vmem((OWN, MODEL), BF16), vmem((MODEL, OWN), BF16),
+            vmem((OWN, MODEL), F32), vmem((OWN, MODEL), F32), vmem((MODEL, FEED), BF16), vmem((FEED, MODEL), BF16),
+            dma((4,)),
+        ],
+        10000000000, any_outs=(2, 3, 4, 5),
+    )
+    feed = scatter_pair((up_keep, up_send), (down_keep, down_send))
+    self_grad, source_own, source_send, *cross_sends, sums = call(
+        cross_back_body, "cross_backward", place,
+        [
+            target_segments, source_seg, own_source, other_source, after_self, lowered_two, queries_two, pair_two,
+            mixed_two, logs_two, after_grad, vectors, sums,
+        ],
+        pieces_two,
+        [shape_of(OWN, MODEL, dtype=F32), shape_of(HALF_SOURCE, MODEL, dtype=F32), shape_of(HALF_SOURCE, MODEL)]
+        + [shape_of(256, 1024)] * 4 + [shape_of(8, MODEL, dtype=F32)],
+        [
+            vmem((SOURCES, MODEL), BF16), vmem((MODEL, 2560), BF16), vmem((OWN, MODEL), BF16), vmem((OWN, MODEL), F32),
+            vmem((SOURCES, 2 * MODEL), BF16), vmem((MODEL, 1024), BF16), vmem((MODEL, 1024), BF16),
+            vmem((SOURCES, TILE), F32), dma((4,)),
+        ],
+        8000000000, any_outs=(3, 4, 5, 6),
+    )
+    cross = scatter_pair(cross_sends[:2], cross_sends[2:])
+    source_came = exchange(source_send, FLIP_Y)
+    grad_source = source_own[:half] + source_came[:half].astype(F32)
+    own_back, send_back, *last_sends = call(
+        self_back_body, "self_backward", place,
+        [target_segments, states, window, lowered, queries, pair, mixed, logs, self_grad, vectors, sums, bias_sums],
+        pieces_one + pieces_two[:4],
+        [shape_of(OWN, MODEL, dtype=F32), shape_of(WINDOW, MODEL)] + [shape_of(256, 1024)] * 2
+        + [shape_of(256, 1152)] * 2,
+        [
+            vmem((MODEL, 1536), BF16), vmem((MODEL, MODEL), BF16), vmem((OWN, MODEL), BF16), vmem((OWN, MODEL), F32),
+            vmem((KEYS, 2 * MODEL), BF16), vmem((MODEL, 1024), BF16), vmem((MODEL, 1152), BF16),
+            vmem((KEYS, TILE), F32), dma((5,)),
+        ],
+        12000000000, any_outs=(2, 3, 4, 5),
+    )
+    last = scatter_pair(last_sends[:2], last_sends[2:])
+    (grad_target,) = call(
+        target_body, "target_grad", place, [own_back, exchange(send_back, FLIP_Y), states, self_grad, vectors], [],
+        [shape_of(OWN, MODEL, dtype=F32)], [], 1000000,
+    )
+    *grads, small = call(
+        finish_body, "finish", place, feed + cross + last, [],
+        [
+            shape_of(16, 1536, dtype=F32), shape_of(16, 512, dtype=F32), shape_of(16, 512, dtype=F32),
+            shape_of(16, 1024, dtype=F32), shape_of(16, 512, dtype=F32), shape_of(16, 2048, dtype=F32),
+            shape_of(64, 512, dtype=F32), shape_of(8, TILE, dtype=F32),
+        ],
+        [], 1000000,
+    )
+    project, output, query, keyval, crossout, up, down = grads
+    rows = [small[i, :16] for i in range(7)]
+    return (
+        layer_out[None], grad_target[None], grad_source[None], project, output, query, keyval, crossout, up,
+        small[7, :64], down, *rows,
+    )
+
+
+def specs():
     in_specs = (
         P("rows", "seq", None),
         P("rows", "seq", None),
@@ -403,6 +1062,13 @@
         P(("rows", "seq")),
         P(("rows", "seq")),
     )
+    return in_specs, out_specs
+
+
+def solution(mesh):
+    in_specs, out_specs = specs()
+    fast = mesh.shape["rows"] == 16 and mesh.shape["seq"] == 2
     return jax.shard_map(
-        per_device, mesh=mesh, in_specs=in_specs, out_specs=out_specs, check_vma=False
-    )
+        fast_device if fast else general_device,
+        mesh=mesh, in_specs=in_specs, out_specs=out_specs, check_vma=False,
+    )

time: 1410 us -> 289 us (0.20)
  waiting for transfers between devices: 875 us -> 103 us
  blocking collectives: 309 us -> 0 us
  matrix products: 118 us -> 0 us
  Pallas kernels: 0 us -> 95.4 us
  starting transfers between devices: 0.82 us -> 65.1 us
  local copies, waits for them, and re-layouts: 56.4 us -> 20.9 us
  other arithmetic: 29 us -> 1.96 us
    reduce_scatter x7 -> x0, waiting for transfers between devices: 727 us -> none  [the longest x1 141 us: per_device(): lax.psum_scatter(grad_down, ('rows', 'seq'), scatter_dimension=0, tiled=T...]
    all_gather x4 -> x0, blocking collectives: 227 us -> none  [the longest x1 73.8 us: per_device(): lax.all_gather(self_output, ('rows', 'seq'), axis=0, tiled=True)]
    unnamed x17 -> x0, waiting for transfers between devices: 139 us -> none
    dot_general x44 -> x0, matrix products: 111 us -> none  [the longest x7 22.9 us: transposed(): lax.dot_general(left, right, (((0,), (0,)), ((), ())), preferred_element_...]
    ppermute x0 -> x64, waiting for transfers between devices: none -> 103 us  [exchange(): lax.ppermute(value, AXES, [(device, device ^ flip) for device in range(32)])]
    pallas_call x0 -> x8, Pallas kernels: none -> 95.4 us  [call(): pl.pallas_call(body, name=name, out_shape=outs, in_specs=[SMEM_SPEC] + [A...]
    unnamed x2 -> x0, blocking collectives: 82 us -> none
    ppermute x0 -> x64, starting transfers between devices: none -> 65.1 us  [exchange(): lax.ppermute(value, AXES, [(device, device ^ flip) for device in range(32)])]
  transfers between devices with their start and end apart: 15 -> 64, of which waited for: 9 -> 26; matrix products, arithmetic and copies ran while one was open for 12% -> 1% of each run, Pallas kernels for 0% -> 11%
where the time goes in v2:
time: 289 us; the launch traced here: 288 us
  waiting for transfers between devices  103 us (36%)
  Pallas kernels  95.4 us (33%)
  starting transfers between devices  65.1 us (23%)
  local copies, waits for them, and re-layouts  20.9 us (7%)
    ppermute x64, waiting for transfers between devices, exchange(): lax.ppermute(value, AXES, [(device, device ^ flip) for device in range(32)])  103 us
    pallas_call x8, Pallas kernels, call(): pl.pallas_call(body, name=name, out_shape=outs, in_specs=[SMEM_SPEC] + [A...  95.4 us
    ppermute x64, starting transfers between devices, exchange(): lax.ppermute(value, AXES, [(device, device ^ flip) for device in range(32)])  65.1 us
    unnamed x53, local copies, waits for them, and re-layouts  13.3 us
  transfers between devices with their start and end apart: 64, of which 26 were waited for; matrix products, arithmetic and copies ran while one was open for 1% of the time, Pallas kernels for 11%

profile of v2, /device:TPU:0, one launch (start us, length us, event | category | flops | bytes accessed | tf_op | source)
XLA Modules:
  0.0 288.0 jit_solution(13770748472520175140)
XLA Ops:
  0.7 5.4 %concatenate.43 = bf16[256]{0:T(256)(128)(2,1)S(1)} concatenate(bf16[16]{0:T(256)(128)(2,1)} %param.33, bf16[16]{0:T(256)(128)(2,1)} %param.34, bf16[16]{0:T(256)(128)(2,1)} %param.35, bf16[16]{0:T(256)(128)(2,1)} %param.36, bf16[16]{0:T(256)(128)(2,1)} %param.37, bf16[16]{0:T(256)(128)(2,1)} %param.38, bf16[16]{0:T(256)(128)(2,1)} %param.39, bf16[64]{0:T(256)(128)(2,1)} %param.31, ...), dimensions={0} | concatenate | bytes 1024 | tf_op jit(solution)/shard_map/concatenate | solution.py:917
  6.2 1.0 copy-done
  13.3 5.1 %collective-permute-start.4 = (bf16[16,1664]{1,0:T(8,128)(2,1)S(1)}, bf16[16,1664]{1,0:T(8,128)(2,1)S(1)}, u32[]{:S(2)}, u32[]{:S(2)}) collective-permute-start(bf16[16,1664]{1,0:T(8,128)(2,1)S(1)} %get-tuple-element.67), channel_id=1, source_target_pairs={{0,24},{1,25},{2,26},{3,27},{4,28},{5,29},{6,30},{7,31},{8,16},{9,... | collective-permute-start | bytes 159752 | tf_op jit(solution)/shard_map/ppermute | solution.py:377
  19.1 3.7 %collective-permute-start.15 = (bf16[16,2560]{1,0:T(8,128)(2,1)S(1)}, bf16[16,2560]{1,0:T(8,128)(2,1)S(1)}, u32[]{:S(2)}, u32[]{:S(2)}) collective-permute-start(bf16[16,2560]{1,0:T(8,128)(2,1)S(1)} %get-tuple-element.70), channel_id=1, source_target_pairs={{0,24},{1,25},{2,26},{3,27},{4,28},{5,29},{6,30},{7,31},{8,16},{9,... | collective-permute-start | bytes 245768 | tf_op jit(solution)/shard_map/ppermute | solution.py:377
  22.8 0.9 pad.4.own_source
  24.5 3.2 %collective-permute-done.3 = bf16[16,1664]{1,0:T(8,128)(2,1)S(1)} collective-permute-done((bf16[16,1664]{1,0:T(8,128)(2,1)S(1)}, bf16[16,1664]{1,0:T(8,128)(2,1)S(1)}, u32[]{:S(2)}, u32[]{:S(2)}) %collective-permute-start.3) | collective-permute-done | bytes 53280 | tf_op jit(solution)/shard_map/ppermute | solution.py:377
  28.5 2.2 collective-permute-done.13
  30.7 1.6 collective-permute-start.24
  32.3 4.4 %collective-permute-done.14 = bf16[16,2560]{1,0:T(8,128)(2,1)S(1)} collective-permute-done((bf16[16,2560]{1,0:T(8,128)(2,1)S(1)}, bf16[16,2560]{1,0:T(8,128)(2,1)S(1)}, u32[]{:S(2)}, u32[]{:S(2)}) %collective-permute-start.14) | collective-permute-done | bytes 81952 | tf_op jit(solution)/shard_map/ppermute | solution.py:377
  36.7 1.5 collective-permute-start
  38.8 1.6 collective-permute-start.5
  40.4 1.0 collective-permute-done.25
  41.4 1.5 collective-permute-start.9
  43.6 1.6 collective-permute-start.16
  45.2 4.3 %collective-permute-done.9 = bf16[64,896]{1,0:T(8,128)(2,1)S(1)} collective-permute-done((bf16[64,896]{1,0:T(8,128)(2,1)S(1)}, bf16[64,896]{1,0:T(8,128)(2,1)S(1)}, u32[]{:S(2)}, u32[]{:S(2)}) %collective-permute-start.9) | collective-permute-done | bytes 114720 | tf_op jit(solution)/shard_map/ppermute | solution.py:377
  49.5 1.5 collective-permute-start.31
  51.1 2.0 collective-permute-done.20
  53.0 1.5 collective-permute-start.27
  54.7 1.6 collective-permute-start.6
  56.8 1.6 collective-permute-start.10
  58.6 3.4 %collective-permute-done.6.refs_1_ = bf16[128,768]{1,0:T(8,128)(2,1)S(1)} collective-permute-done((bf16[128,768]{1,0:T(8,128)(2,1)S(1)}, bf16[128,768]{1,0:T(8,128)(2,1)S(1)}, u32[]{:S(2)}, u32[]{:S(2)}) %collective-permute-start.6) | collective-permute-done | bytes 196640 | tf_op jit(solution)/shard_map/ppermute | solution.py:377
  62.0 1.5 collective-permute-start.17
  64.9 1.5 collective-permute-start.28
  66.4 1.5 collective-permute-start.32
  68.5 4.2 %collective-permute-done.17.refs_1_.refs_9_ = bf16[128,1280]{1,0:T(8,128)(2,1)S(1)} collective-permute-done((bf16[128,1280]{1,0:T(8,128)(2,1)S(1)}, bf16[128,1280]{1,0:T(8,128)(2,1)S(1)}, u32[]{:S(2)}, u32[]{:S(2)}) %collective-permute-start.17) | collective-permute-done | bytes 327712 | tf_op jit(solution)/shard_map/ppermute | solution.py:377
  73.3 13.4 %collective-permute-done.21.refs_5_ = bf16[128,1280]{1,0:T(8,128)(2,1)S(1)} collective-permute-done((bf16[128,1280]{1,0:T(8,128)(2,1)S(1)}, bf16[128,1280]{1,0:T(8,128)(2,1)S(1)}, u32[]{:S(2)}, u32[]{:S(2)}) %collective-permute-start.21) | collective-permute-done | bytes 327712 | tf_op jit(solution)/shard_map/ppermute | solution.py:377
  87.8 15.0 %self_forward.1 = (bf16[512,512]{1,0:T(8,128)(2,1)S(1)}, bf16[768,1024]{1,0:T(8,128)(2,1)S(1)}, bf16[512,512]{1,0:T(8,128)(2,1)S(1)}, f32[8,512]{1,0:T(8,128)S(1...) custom-call(s32[2]{0:T(128)S(1)} %pad_add_fusion.1.place, s32[1,1024]{1,0:T(1,128)S(1)} %copy-done.10, ...), custom_call_target="tpu_custom_call" | custom-call | flops 5000000000 | bytes 4194304 | tf_op jit(solution)/shard_map/self_forward/pallas_call | solution.py:894
  104.6 13.8 %cross_forward.1 = (f32[512,512]{1,0:T(8,128)S(1)}, bf16[512,512]{1,0:T(8,128)(2,1)S(1)}, bf16[512,512]{1,0:T(8,128)(2,1)S(1)}, bf16[384,1024]{1,0:T(8,128)(2,1)...) custom-call(s32[2]{0:T(128)S(1)} %pad_add_fusion.1.place, ...), custom_call_target="tpu_custom_call" | custom-call | flops 5000000000 | bytes 4194304 | tf_op jit(solution)/shard_map/cross_forward/pallas_call | solution.py:894
  119.3 21.4 %feed.1 = (bf16[512,512]{1,0:T(8,128)(2,1)}, f32[512,512]{1,0:T(8,128)S(1)}, bf16[256,2048]{1,0:T(8,128)(2,1)S(1)}, bf16[256,2048]{1,0:T(8,128)(2,1)S(1)}, bf16[...) custom-call(s32[2]{0:T(128)S(1)} %pad_add_fusion.1.place, ...), custom_call_target="tpu_custom_call" | custom-call | flops 10000000000 | bytes 4194304 | tf_op jit(solution)/shard_map/feed/pallas_call | solution.py:894
  140.7 1.0 copy-done.17
  141.6 1.0 copy-done.16
  142.7 1.2 copy-done.18
  143.9 16.7 %cross_backward.1 = (f32[512,512]{1,0:T(8,128)S(1)}, f32[192,512]{1,0:T(8,128)S(1)}, bf16[192,512]{1,0:T(8,128)(2,1)S(1)}, bf16[256,1024]{1,0:T(8,128)(2,1)S(1)}...) custom-call(s32[2]{0:T(128)S(1)} %pad_add_fusion.1.place, ...), custom_call_target="tpu_custom_call" | custom-call | flops 8000000000 | bytes 4194304 | tf_op jit(solution)/shard_map/cross_backward/pallas_call | solution.py:894
  160.6 1.0 copy-done.20
  161.7 24.3 %self_backward.1 = (f32[512,512]{1,0:T(8,128)S(1)}, bf16[256,512]{1,0:T(8,128)(2,1)S(1)}, bf16[256,1024]{1,0:T(8,128)(2,1)S(1)}, bf16[256,1024]{1,0:T(8,128)(2,1...) custom-call(s32[2]{0:T(128)S(1)} %pad_add_fusion.1.place, s32[1,1024]{1,0:T(1,128)S(1)} %copy-done.10, ...), custom_call_target="tpu_custom_call" | custom-call | flops 12000000000 | bytes 4194304 | tf_op jit(solution)/shard_map/self_backward/pallas_call | solution.py:894
  187.5 1.5 collective-permute-start.35
  191.0 1.0 collective-permute-start.47
  192.0 13.9 %collective-permute-done.56 = bf16[128,1024]{1,0:T(8,128)(2,1)S(1)} collective-permute-done((bf16[128,1024]{1,0:T(8,128)(2,1)S(1)}, bf16[128,1024]{1,0:T(8,128)(2,1)S(1)}, u32[]{:S(2)}, u32[]{:S(2)}) %collective-permute-start.56) | collective-permute-done | bytes 262176 | tf_op jit(solution)/shard_map/ppermute | solution.py:377
  206.0 1.5 collective-permute-start.50
  207.5 3.2 %collective-permute-done.47 = bf16[128,1024]{1,0:T(8,128)(2,1)S(1)} collective-permute-done((bf16[128,1024]{1,0:T(8,128)(2,1)S(1)}, bf16[128,1024]{1,0:T(8,128)(2,1)S(1)}, u32[]{:S(2)}, u32[]{:S(2)}) %collective-permute-start.47) | collective-permute-done | bytes 262176 | tf_op jit(solution)/shard_map/ppermute | solution.py:377
  210.7 1.5 collective-permute-start.59
  212.6 6.3 %collective-permute-done.59 = bf16[128,1152]{1,0:T(8,128)(2,1)S(1)} collective-permute-done((bf16[128,1152]{1,0:T(8,128)(2,1)S(1)}, bf16[128,1152]{1,0:T(8,128)(2,1)S(1)}, u32[]{:S(2)}, u32[]{:S(2)}) %collective-permute-start.59) | collective-permute-done | bytes 294944 | tf_op jit(solution)/shard_map/ppermute | solution.py:377
  218.9 1.5 collective-permute-start.57
  220.4 3.7 %collective-permute-done.57 = bf16[64,1024]{1,0:T(8,128)(2,1)S(1)} collective-permute-done((bf16[64,1024]{1,0:T(8,128)(2,1)S(1)}, bf16[64,1024]{1,0:T(8,128)(2,1)S(1)}, u32[]{:S(2)}, u32[]{:S(2)}) %collective-permute-start.57) | collective-permute-done | bytes 131104 | tf_op jit(solution)/shard_map/ppermute | solution.py:377
  224.1 1.5 collective-permute-start.48
  225.6 3.5 %collective-permute-done.48 = bf16[64,1024]{1,0:T(8,128)(2,1)S(1)} collective-permute-done((bf16[64,1024]{1,0:T(8,128)(2,1)S(1)}, bf16[64,1024]{1,0:T(8,128)(2,1)S(1)}, u32[]{:S(2)}, u32[]{:S(2)}) %collective-permute-start.48) | collective-permute-done | bytes 131104 | tf_op jit(solution)/shard_map/ppermute | solution.py:377
  229.6 5.2 %collective-permute-done.51 = bf16[64,1024]{1,0:T(8,128)(2,1)S(1)} collective-permute-done((bf16[64,1024]{1,0:T(8,128)(2,1)S(1)}, bf16[64,1024]{1,0:T(8,128)(2,1)S(1)}, u32[]{:S(2)}, u32[]{:S(2)}) %collective-permute-start.51) | collective-permute-done | bytes 131104 | tf_op jit(solution)/shard_map/ppermute | solution.py:377
  235.3 4.6 %collective-permute-done.60 = bf16[64,1152]{1,0:T(8,128)(2,1)S(1)} collective-permute-done((bf16[64,1152]{1,0:T(8,128)(2,1)S(1)}, bf16[64,1152]{1,0:T(8,128)(2,1)S(1)}, u32[]{:S(2)}, u32[]{:S(2)}) %collective-permute-start.60) | collective-permute-done | bytes 147488 | tf_op jit(solution)/shard_map/ppermute | solution.py:377
  239.9 5.8 %collective-permute-start.54 = (bf16[16,2048]{1,0:T(8,128)(2,1)S(1)}, bf16[16,2048]{1,0:T(8,128)(2,1)S(1)}, u32[]{:S(2)}, u32[]{:S(2)}) collective-permute-start(bf16[16,2048]{1,0:T(8,128)(2,1)S(1)} %get-tuple-element.138), channel_id=1, source_target_pairs={{0,24},{1,25},{2,26},{3,27},{4,28},{5,29},{6,30},{7,31},{8,16},{9,... | collective-permute-start | bytes 196616 | tf_op jit(solution)/shard_map/ppermute | solution.py:377
  246.5 1.3 collective-permute-start.41
  247.8 7.2 %collective-permute-done.38 = bf16[128,2048]{1,0:T(8,128)(2,1)S(1)} collective-permute-done((bf16[128,2048]{1,0:T(8,128)(2,1)S(1)}, bf16[128,2048]{1,0:T(8,128)(2,1)S(1)}, u32[]{:S(2)}, u32[]{:S(2)}) %collective-permute-start.38) | collective-permute-done | bytes 524320 | tf_op jit(solution)/shard_map/ppermute | solution.py:377
  255.1 2.7 collective-permute-done.41
  257.7 1.2 collective-permute-start.39
  259.0 5.1 %collective-permute-done.39 = bf16[64,2048]{1,0:T(8,128)(2,1)S(1)} collective-permute-done((bf16[64,2048]{1,0:T(8,128)(2,1)S(1)}, bf16[64,2048]{1,0:T(8,128)(2,1)S(1)}, u32[]{:S(2)}, u32[]{:S(2)}) %collective-permute-start.39) | collective-permute-done | bytes 262176 | tf_op jit(solution)/shard_map/ppermute | solution.py:377
  264.1 1.8 collective-permute-start.42
  265.9 4.5 %collective-permute-done.42 = bf16[64,2048]{1,0:T(8,128)(2,1)S(1)} collective-permute-done((bf16[64,2048]{1,0:T(8,128)(2,1)S(1)}, bf16[64,2048]{1,0:T(8,128)(2,1)S(1)}, u32[]{:S(2)}, u32[]{:S(2)}) %collective-permute-start.42) | collective-permute-done | bytes 262176 | tf_op jit(solution)/shard_map/ppermute | solution.py:377
  270.5 1.9 collective-permute-start.63
  272.4 1.8 collective-permute-start.61
  275.1 1.8 collective-permute-start.45
  277.7 1.8 collective-permute-start.44
  280.3 2.3 target_grad.1
  282.5 1.4 collective-permute-done.43.refs_1_
  284.0 1.6 collective-permute-done.44.refs_2_
  285.5 1.4 finish.1
  (170 shorter events, 26.3 us)
Async XLA Ops:
  13.3 15.0 %collective-permute-start.4 = (bf16[16,1664]{1,0:T(8,128)(2,1)S(1)}, bf16[16,1664]{1,0:T(8,128)(2,1)S(1)}, u32[]{:S(2)}, u32[]{:S(2)}) collective-permute-start(bf16[16,1664]{1,0:T(8,128)(2,1)S(1)} %get-tuple-element.67), channel_id=1, source_target_pairs={{0,24},{1,25},{2,26},{3,27},{4,28},{5,29},{6,30},{7,31},{8,16},{9,... | collective-permute-start | bytes 159752 | tf_op jit(solution)/shard_map/ppermute | solution.py:377
  18.4 9.3 %collective-permute-start.3 = (bf16[16,1664]{1,0:T(8,128)(2,1)S(1)}, bf16[16,1664]{1,0:T(8,128)(2,1)S(1)}, u32[]{:S(2)}, u32[]{:S(2)}) collective-permute-start(bf16[16,1664]{1,0:T(8,128)(2,1)S(1)} %get-tuple-element.67), channel_id=1, source_target_pairs={{0,16},{1,17},{2,18},{3,19},{4,20},{5,21},{6,22},{7,23},{8,24},{9,... | collective-permute-start | bytes 159752 | tf_op jit(solution)/shard_map/ppermute | solution.py:377
  18.4 5.4 %collective-permute-start.2 = (bf16[16,1664]{1,0:T(8,128)(2,1)S(1)}, bf16[16,1664]{1,0:T(8,128)(2,1)S(1)}, u32[]{:S(2)}, u32[]{:S(2)}) collective-permute-start(bf16[16,1664]{1,0:T(8,128)(2,1)S(1)} %get-tuple-element.67), channel_id=1, source_target_pairs={{0,8},{1,9},{2,10},{3,11},{4,12},{5,13},{6,14},{7,15},{8,0},{9,1},... | collective-permute-start | bytes 159752 | tf_op jit(solution)/shard_map/ppermute | solution.py:377
  19.1 19.2 %collective-permute-start.15 = (bf16[16,2560]{1,0:T(8,128)(2,1)S(1)}, bf16[16,2560]{1,0:T(8,128)(2,1)S(1)}, u32[]{:S(2)}, u32[]{:S(2)}) collective-permute-start(bf16[16,2560]{1,0:T(8,128)(2,1)S(1)} %get-tuple-element.70), channel_id=1, source_target_pairs={{0,24},{1,25},{2,26},{3,27},{4,28},{5,29},{6,30},{7,31},{8,16},{9,... | collective-permute-start | bytes 245768 | tf_op jit(solution)/shard_map/ppermute | solution.py:377
  22.8 13.9 %collective-permute-start.14 = (bf16[16,2560]{1,0:T(8,128)(2,1)S(1)}, bf16[16,2560]{1,0:T(8,128)(2,1)S(1)}, u32[]{:S(2)}, u32[]{:S(2)}) collective-permute-start(bf16[16,2560]{1,0:T(8,128)(2,1)S(1)} %get-tuple-element.70), channel_id=1, source_target_pairs={{0,16},{1,17},{2,18},{3,19},{4,20},{5,21},{6,22},{7,23},{8,24},{9,... | collective-permute-start | bytes 245768 | tf_op jit(solution)/shard_map/ppermute | solution.py:377
  23.8 6.9 %collective-permute-start.13 = (bf16[16,2560]{1,0:T(8,128)(2,1)S(1)}, bf16[16,2560]{1,0:T(8,128)(2,1)S(1)}, u32[]{:S(2)}, u32[]{:S(2)}) collective-permute-start(bf16[16,2560]{1,0:T(8,128)(2,1)S(1)} %get-tuple-element.70), channel_id=1, source_target_pairs={{0,8},{1,9},{2,10},{3,11},{4,12},{5,13},{6,14},{7,15},{8,0},{9,1},... | collective-permute-start | bytes 245768 | tf_op jit(solution)/shard_map/ppermute | solution.py:377
  27.7 15.3 %collective-permute-start.26 = (bf16[16,4096]{1,0:T(8,128)(2,1)S(1)}, bf16[16,4096]{1,0:T(8,128)(2,1)S(1)}, u32[]{:S(2)}, u32[]{:S(2)}) collective-permute-start(bf16[16,4096]{1,0:T(8,128)(2,1)S(1)} %get-tuple-element.73), channel_id=1, source_target_pairs={{0,24},{1,25},{2,26},{3,27},{4,28},{5,29},{6,30},{7,31},{8,16},{9,... | collective-permute-start | bytes 393224 | tf_op jit(solution)/shard_map/ppermute | solution.py:377
  28.3 13.1 %collective-permute-start.25 = (bf16[16,4096]{1,0:T(8,128)(2,1)S(1)}, bf16[16,4096]{1,0:T(8,128)(2,1)S(1)}, u32[]{:S(2)}, u32[]{:S(2)}) collective-permute-start(bf16[16,4096]{1,0:T(8,128)(2,1)S(1)} %get-tuple-element.73), channel_id=1, source_target_pairs={{0,16},{1,17},{2,18},{3,19},{4,20},{5,21},{6,22},{7,23},{8,24},{9,... | collective-permute-start | bytes 393224 | tf_op jit(solution)/shard_map/ppermute | solution.py:377
  30.7 8.2 %collective-permute-start.24 = (bf16[16,4096]{1,0:T(8,128)(2,1)S(1)}, bf16[16,4096]{1,0:T(8,128)(2,1)S(1)}, u32[]{:S(2)}, u32[]{:S(2)}) collective-permute-start(bf16[16,4096]{1,0:T(8,128)(2,1)S(1)} %get-tuple-element.73), channel_id=1, source_target_pairs={{0,8},{1,9},{2,10},{3,11},{4,12},{5,13},{6,14},{7,15},{8,0},{9,1},... | collective-permute-start | bytes 393224 | tf_op jit(solution)/shard_map/ppermute | solution.py:377
  36.7 18.0 %collective-permute-start = (bf16[192,512]{1,0:T(8,128)(2,1)S(1)}, bf16[192,512]{1,0:T(8,128)(2,1)S(1)}, u32[]{:S(2)}, u32[]{:S(2)}) collective-permute-start(bf16[192,512]{1,0:T(8,128)(2,1)S(1)} %pad.4.own_source), channel_id=1, source_target_pairs={{0,1},{1,0},{2,3},{3,2},{4,5},{5,4},{6,7},{7,6},{8,9},{9,8},{10,11... | collective-permute-start | bytes 589832 | tf_op jit(solution)/shard_map/ppermute | solution.py:377
  38.2 18.6 %collective-permute-start.1 = (bf16[256,512]{1,0:T(8,128)(2,1)S(1)}, bf16[256,512]{1,0:T(8,128)(2,1)S(1)}, u32[]{:S(2)}, u32[]{:S(2)}) collective-permute-start(bf16[256,512]{1,0:T(8,128)(2,1)S(1)} %get-tuple-element.66), channel_id=1, source_target_pairs={{0,1},{1,0},{2,3},{3,2},{4,5},{5,4},{6,7},{7,6},{8,9},{9,8},{10,11... | collective-permute-start | bytes 786440 | tf_op jit(solution)/shard_map/ppermute | solution.py:377
  38.8 4.8 %collective-permute-start.5 = (bf16[64,768]{1,0:T(8,128)(2,1)S(1)}, bf16[64,768]{1,0:T(8,128)(2,1)S(1)}, u32[]{:S(2)}, u32[]{:S(2)}) collective-permute-start(bf16[64,768]{1,0:T(8,128)(2,1)S(1)} %slice.312), channel_id=1, source_target_pairs={{0,4},{1,5},{2,6},{3,7},{4,0},{5,1},{6,2},{7,3},{8,12},{9,13},{10,... | collective-permute-start | bytes 294920 | tf_op jit(solution)/shard_map/ppermute | solution.py:377
  41.4 8.1 %collective-permute-start.9 = (bf16[64,896]{1,0:T(8,128)(2,1)S(1)}, bf16[64,896]{1,0:T(8,128)(2,1)S(1)}, u32[]{:S(2)}, u32[]{:S(2)}) collective-permute-start(bf16[64,896]{1,0:T(8,128)(2,1)S(1)} %slice.313), channel_id=1, source_target_pairs={{0,1},{1,0},{2,3},{3,2},{4,5},{5,4},{6,7},{7,6},{8,9},{9,8},{10,11... | collective-permute-start | bytes 344072 | tf_op jit(solution)/shard_map/ppermute | solution.py:377
  43.0 10.1 %collective-permute-start.20 = (bf16[64,1280]{1,0:T(8,128)(2,1)S(1)}, bf16[64,1280]{1,0:T(8,128)(2,1)S(1)}, u32[]{:S(2)}, u32[]{:S(2)}) collective-permute-start(bf16[64,1280]{1,0:T(8,128)(2,1)S(1)} %get-tuple-element.132), channel_id=1, source_target_pairs={{0,1},{1,0},{2,3},{3,2},{4,5},{5,4},{6,7},{7,6},{8,9},{9,8},{10,11... | collective-permute-start | bytes 491528 | tf_op jit(solution)/shard_map/ppermute | solution.py:377
  43.6 10.9 %collective-permute-start.16 = (bf16[64,1280]{1,0:T(8,128)(2,1)S(1)}, bf16[64,1280]{1,0:T(8,128)(2,1)S(1)}, u32[]{:S(2)}, u32[]{:S(2)}) collective-permute-start(bf16[64,1280]{1,0:T(8,128)(2,1)S(1)} %get-tuple-element.133), channel_id=1, source_target_pairs={{0,4},{1,5},{2,6},{3,7},{4,0},{5,1},{6,2},{7,3},{8,12},{9,13},{10,... | collective-permute-start | bytes 491528 | tf_op jit(solution)/shard_map/ppermute | solution.py:377
  49.5 7.3 %collective-permute-start.31 = (bf16[64,2048]{1,0:T(8,128)(2,1)S(1)}, bf16[64,2048]{1,0:T(8,128)(2,1)S(1)}, u32[]{:S(2)}, u32[]{:S(2)}) collective-permute-start(bf16[64,2048]{1,0:T(8,128)(2,1)S(1)} %get-tuple-element.130), channel_id=1, source_target_pairs={{0,1},{1,0},{2,3},{3,2},{4,5},{5,4},{6,7},{7,6},{8,9},{9,8},{10,11... | collective-permute-start | bytes 786440 | tf_op jit(solution)/shard_map/ppermute | solution.py:377
  53.0 10.5 %collective-permute-start.27 = (bf16[64,2048]{1,0:T(8,128)(2,1)S(1)}, bf16[64,2048]{1,0:T(8,128)(2,1)S(1)}, u32[]{:S(2)}, u32[]{:S(2)}) collective-permute-start(bf16[64,2048]{1,0:T(8,128)(2,1)S(1)} %get-tuple-element.131), channel_id=1, source_target_pairs={{0,4},{1,5},{2,6},{3,7},{4,0},{5,1},{6,2},{7,3},{8,12},{9,13},{10,... | collective-permute-start | bytes 786440 | tf_op jit(solution)/shard_map/ppermute | solution.py:377
  54.6 3.8 %collective-permute-start.7 = (bf16[128,768]{1,0:T(8,128)(2,1)S(1)}, bf16[128,768]{1,0:T(8,128)(2,1)S(1)}, u32[]{:S(2)}, u32[]{:S(2)}) collective-permute-start(bf16[128,768]{1,0:T(8,128)(2,1)S(1)} %pad_maximum_fusion.5.refs_0_), channel_id=1, source_target_pairs={{0,2},{1,3},{2,0},{3,1},{4,6},{5,7},{6,4},{7,5},{8,10},{9,11},{10,... | collective-permute-start | bytes 589832 | tf_op jit(solution)/shard_map/ppermute | solution.py:377
  54.7 7.4 %collective-permute-start.6 = (bf16[128,768]{1,0:T(8,128)(2,1)S(1)}, bf16[128,768]{1,0:T(8,128)(2,1)S(1)}, u32[]{:S(2)}, u32[]{:S(2)}) collective-permute-start(bf16[128,768]{1,0:T(8,128)(2,1)S(1)} %pad_maximum_fusion.5.refs_0_), channel_id=1, source_target_pairs={{0,1},{1,0},{2,3},{3,2},{4,5},{5,4},{6,7},{7,6},{8,9},{9,8},{10,11... | collective-permute-start | bytes 589832 | tf_op jit(solution)/shard_map/ppermute | solution.py:377
  56.8 6.8 %collective-permute-start.11 = (bf16[128,896]{1,0:T(8,128)(2,1)S(1)}, bf16[128,896]{1,0:T(8,128)(2,1)S(1)}, u32[]{:S(2)}, u32[]{:S(2)}) collective-permute-start(bf16[128,896]{1,0:T(8,128)(2,1)S(1)} %pad_maximum_fusion.4.refs_4_), channel_id=1, source_target_pairs={{0,2},{1,3},{2,0},{3,1},{4,6},{5,7},{6,4},{7,5},{8,10},{9,11},{10,... | collective-permute-start | bytes 688136 | tf_op jit(solution)/shard_map/ppermute | solution.py:377
  56.8 8.1 %collective-permute-start.10 = (bf16[128,896]{1,0:T(8,128)(2,1)S(1)}, bf16[128,896]{1,0:T(8,128)(2,1)S(1)}, u32[]{:S(2)}, u32[]{:S(2)}) collective-permute-start(bf16[128,896]{1,0:T(8,128)(2,1)S(1)} %pad_maximum_fusion.4.refs_4_), channel_id=1, source_target_pairs={{0,4},{1,5},{2,6},{3,7},{4,0},{5,1},{6,2},{7,3},{8,12},{9,13},{10,... | collective-permute-start | bytes 688136 | tf_op jit(solution)/shard_map/ppermute | solution.py:377
  58.4 9.5 %collective-permute-start.18 = (bf16[128,1280]{1,0:T(8,128)(2,1)S(1)}, bf16[128,1280]{1,0:T(8,128)(2,1)S(1)}, u32[]{:S(2)}, u32[]{:S(2)}) collective-permute-start(bf16[128,1280]{1,0:T(8,128)(2,1)S(1)} %pad_maximum_fusion.2.refs_0_.refs_8_), channel_id=1, source_target_pairs={{0,2},{1,3},{2,0},{3,1},{4,6},{5,7},{6,4},{7,5},{8,10},{9,11},{10,... | collective-permute-start | bytes 983048 | tf_op jit(solution)/shard_map/ppermute | solution.py:377
  62.0 10.6 %collective-permute-start.17 = (bf16[128,1280]{1,0:T(8,128)(2,1)S(1)}, bf16[128,1280]{1,0:T(8,128)(2,1)S(1)}, u32[]{:S(2)}, u32[]{:S(2)}) collective-permute-start(bf16[128,1280]{1,0:T(8,128)(2,1)S(1)} %pad_maximum_fusion.2.refs_0_.refs_8_), channel_id=1, source_target_pairs={{0,1},{1,0},{2,3},{3,2},{4,5},{5,4},{6,7},{7,6},{8,9},{9,8},{10,11... | collective-permute-start | bytes 983048 | tf_op jit(solution)/shard_map/ppermute | solution.py:377
  63.6 9.1 %collective-permute-start.22 = (bf16[128,1280]{1,0:T(8,128)(2,1)S(1)}, bf16[128,1280]{1,0:T(8,128)(2,1)S(1)}, u32[]{:S(2)}, u32[]{:S(2)}) collective-permute-start(bf16[128,1280]{1,0:T(8,128)(2,1)S(1)} %pad_maximum_fusion.3.refs_4_), channel_id=1, source_target_pairs={{0,2},{1,3},{2,0},{3,1},{4,6},{5,7},{6,4},{7,5},{8,10},{9,11},{10,... | collective-permute-start | bytes 983048 | tf_op jit(solution)/shard_map/ppermute | solution.py:377
  63.6 2.9 collective-permute-start.8
  64.9 22.4 %collective-permute-start.28 = (bf16[128,2048]{1,0:T(8,128)(2,1)S(1)}, bf16[128,2048]{1,0:T(8,128)(2,1)S(1)}, u32[]{:S(2)}, u32[]{:S(2)}) collective-permute-start(bf16[128,2048]{1,0:T(8,128)(2,1)S(1)} %pad_maximum_fusion.refs_0_), channel_id=1, source_target_pairs={{0,1},{1,0},{2,3},{3,2},{4,5},{5,4},{6,7},{7,6},{8,9},{9,8},{10,11... | collective-permute-start | bytes 1572872 | tf_op jit(solution)/shard_map/ppermute | solution.py:377
  66.4 21.3 %collective-permute-start.32 = (bf16[128,2048]{1,0:T(8,128)(2,1)S(1)}, bf16[128,2048]{1,0:T(8,128)(2,1)S(1)}, u32[]{:S(2)}, u32[]{:S(2)}) collective-permute-start(bf16[128,2048]{1,0:T(8,128)(2,1)S(1)} %pad_maximum_fusion.1.refs_4_), channel_id=1, source_target_pairs={{0,4},{1,5},{2,6},{3,7},{4,0},{5,1},{6,2},{7,3},{8,12},{9,13},{10,... | collective-permute-start | bytes 1572872 | tf_op jit(solution)/shard_map/ppermute | solution.py:377
  67.9 18.8 %collective-permute-start.21 = (bf16[128,1280]{1,0:T(8,128)(2,1)S(1)}, bf16[128,1280]{1,0:T(8,128)(2,1)S(1)}, u32[]{:S(2)}, u32[]{:S(2)}) collective-permute-start(bf16[128,1280]{1,0:T(8,128)(2,1)S(1)} %pad_maximum_fusion.3.refs_4_), channel_id=1, source_target_pairs={{0,4},{1,5},{2,6},{3,7},{4,0},{5,1},{6,2},{7,3},{8,12},{9,13},{10,... | collective-permute-start | bytes 983048 | tf_op jit(solution)/shard_map/ppermute | solution.py:377
  72.7 14.1 %collective-permute-start.12 = (bf16[128,896]{1,0:T(8,128)(2,1)S(1)}, bf16[128,896]{1,0:T(8,128)(2,1)S(1)}, u32[]{:S(2)}, u32[]{:S(2)}) collective-permute-start(bf16[128,896]{1,0:T(8,128)(2,1)S(1)} %collective-permute-done.10.refs_5_), channel_id=1, source_target_pairs={{0,2},{1,3},{2,0},{3,1},{4,6},{5,7},{6,4},{7,5},{8,10},{9,11},{10,... | collective-permute-start | bytes 688136 | tf_op jit(solution)/shard_map/ppermute | solution.py:377
  72.7 14.6 %collective-permute-start.19 = (bf16[128,1280]{1,0:T(8,128)(2,1)S(1)}, bf16[128,1280]{1,0:T(8,128)(2,1)S(1)}, u32[]{:S(2)}, u32[]{:S(2)}) collective-permute-start(bf16[128,1280]{1,0:T(8,128)(2,1)S(1)} %collective-permute-done.17.refs_1_.refs_9_), channel_id=1, source_target_pairs={{0,2},{1,3},{2,0},{3,1},{4,6},{5,7},{6,4},{7,5},{8,10},{9,11},{10,... | collective-permute-start | bytes 983048 | tf_op jit(solution)/shard_map/ppermute | solution.py:377
  86.7 32.5 %collective-permute-start.29 = (bf16[128,2048]{1,0:T(8,128)(2,1)S(1)}, bf16[128,2048]{1,0:T(8,128)(2,1)S(1)}, u32[]{:S(2)}, u32[]{:S(2)}) collective-permute-start(bf16[128,2048]{1,0:T(8,128)(2,1)S(1)} %pad_maximum_fusion.refs_0_), channel_id=1, source_target_pairs={{0,2},{1,3},{2,0},{3,1},{4,6},{5,7},{6,4},{7,5},{8,10},{9,11},{10,... | collective-permute-start | bytes 1572872 | tf_op jit(solution)/shard_map/ppermute | solution.py:377
  86.7 32.5 %collective-permute-start.33 = (bf16[128,2048]{1,0:T(8,128)(2,1)S(1)}, bf16[128,2048]{1,0:T(8,128)(2,1)S(1)}, u32[]{:S(2)}, u32[]{:S(2)}) collective-permute-start(bf16[128,2048]{1,0:T(8,128)(2,1)S(1)} %pad_maximum_fusion.1.refs_4_), channel_id=1, source_target_pairs={{0,2},{1,3},{2,0},{3,1},{4,6},{5,7},{6,4},{7,5},{8,10},{9,11},{10,... | collective-permute-start | bytes 1572872 | tf_op jit(solution)/shard_map/ppermute | solution.py:377
  87.2 17.3 %collective-permute-start.23 = (bf16[128,1280]{1,0:T(8,128)(2,1)S(1)}, bf16[128,1280]{1,0:T(8,128)(2,1)S(1)}, u32[]{:S(2)}, u32[]{:S(2)}) collective-permute-start(bf16[128,1280]{1,0:T(8,128)(2,1)S(1)} %collective-permute-done.21.refs_5_), channel_id=1, source_target_pairs={{0,2},{1,3},{2,0},{3,1},{4,6},{5,7},{6,4},{7,5},{8,10},{9,11},{10,... | collective-permute-start | bytes 983048 | tf_op jit(solution)/shard_map/ppermute | solution.py:377
  87.3 31.9 %collective-permute-start.30 = (bf16[128,2048]{1,0:T(8,128)(2,1)S(1)}, bf16[128,2048]{1,0:T(8,128)(2,1)S(1)}, u32[]{:S(2)}, u32[]{:S(2)}) collective-permute-start(bf16[128,2048]{1,0:T(8,128)(2,1)S(1)} %collective-permute-done.28.refs_1_), channel_id=1, source_target_pairs={{0,2},{1,3},{2,0},{3,1},{4,6},{5,7},{6,4},{7,5},{8,10},{9,11},{10,... | collective-permute-start | bytes 1572872 | tf_op jit(solution)/shard_map/ppermute | solution.py:377
  87.8 31.5 %collective-permute-start.34 = (bf16[128,2048]{1,0:T(8,128)(2,1)S(1)}, bf16[128,2048]{1,0:T(8,128)(2,1)S(1)}, u32[]{:S(2)}, u32[]{:S(2)}) collective-permute-start(bf16[128,2048]{1,0:T(8,128)(2,1)S(1)} %collective-permute-done.32.refs_5_), channel_id=1, source_target_pairs={{0,2},{1,3},{2,0},{3,1},{4,6},{5,7},{6,4},{7,5},{8,10},{9,11},{10,... | collective-permute-start | bytes 1572872 | tf_op jit(solution)/shard_map/ppermute | solution.py:377
  186.0 3.0 %collective-permute-start.55 = (bf16[256,1024]{1,0:T(8,128)(2,1)S(1)}, bf16[256,1024]{1,0:T(8,128)(2,1)S(1)}, u32[]{:S(2)}, u32[]{:S(2)}) collective-permute-start(bf16[256,1024]{1,0:T(8,128)(2,1)S(1)} %get-tuple-element.103), channel_id=1, source_target_pairs={{0,2},{1,3},{2,0},{3,1},{4,6},{5,7},{6,4},{7,5},{8,10},{9,11},{10,... | collective-permute-start | bytes 1572872 | tf_op jit(solution)/shard_map/ppermute | solution.py:377
  186.5 2.6 collective-permute-start.46
  186.5 3.2 %collective-permute-start.49 = (bf16[256,1024]{1,0:T(8,128)(2,1)S(1)}, bf16[256,1024]{1,0:T(8,128)(2,1)S(1)}, u32[]{:S(2)}, u32[]{:S(2)}) collective-permute-start(bf16[256,1024]{1,0:T(8,128)(2,1)S(1)} %get-tuple-element.101), channel_id=1, source_target_pairs={{0,2},{1,3},{2,0},{3,1},{4,6},{5,7},{6,4},{7,5},{8,10},{9,11},{10,... | collective-permute-start | bytes 1572872 | tf_op jit(solution)/shard_map/ppermute | solution.py:377
  187.0 83.5 %collective-permute-start.36 = (bf16[192,512]{1,0:T(8,128)(2,1)S(1)}, bf16[192,512]{1,0:T(8,128)(2,1)S(1)}, u32[]{:S(2)}, u32[]{:S(2)}) collective-permute-start(bf16[192,512]{1,0:T(8,128)(2,1)S(1)} %get-tuple-element.93), channel_id=1, source_target_pairs={{0,1},{1,0},{2,3},{3,2},{4,5},{5,4},{6,7},{7,6},{8,9},{9,8},{10,11... | collective-permute-start | bytes 589832 | tf_op jit(solution)/shard_map/ppermute | solution.py:377
  187.5 85.0 %collective-permute-start.35 = (bf16[256,512]{1,0:T(8,128)(2,1)S(1)}, bf16[256,512]{1,0:T(8,128)(2,1)S(1)}, u32[]{:S(2)}, u32[]{:S(2)}) collective-permute-start(bf16[256,512]{1,0:T(8,128)(2,1)S(1)} %get-tuple-element.91), channel_id=1, source_target_pairs={{0,1},{1,0},{2,3},{3,2},{4,5},{5,4},{6,7},{7,6},{8,9},{9,8},{10,11... | collective-permute-start | bytes 786440 | tf_op jit(solution)/shard_map/ppermute | solution.py:377
  189.0 2.0 collective-permute-start.58
  189.1 56.6 %collective-permute-start.37 = (bf16[256,2048]{1,0:T(8,128)(2,1)S(1)}, bf16[256,2048]{1,0:T(8,128)(2,1)S(1)}, u32[]{:S(2)}, u32[]{:S(2)}) collective-permute-start(bf16[256,2048]{1,0:T(8,128)(2,1)S(1)} %get-tuple-element.95), channel_id=1, source_target_pairs={{0,2},{1,3},{2,0},{3,1},{4,6},{5,7},{6,4},{7,5},{8,10},{9,11},{10,... | collective-permute-start | bytes 3145736 | tf_op jit(solution)/shard_map/ppermute | solution.py:377
  189.7 16.2 %collective-permute-start.56 = (bf16[128,1024]{1,0:T(8,128)(2,1)S(1)}, bf16[128,1024]{1,0:T(8,128)(2,1)S(1)}, u32[]{:S(2)}, u32[]{:S(2)}) collective-permute-start(bf16[128,1024]{1,0:T(8,128)(2,1)S(1)} %get-tuple-element.121), channel_id=1, source_target_pairs={{0,1},{1,0},{2,3},{3,2},{4,5},{5,4},{6,7},{7,6},{8,9},{9,8},{10,11... | collective-permute-start | bytes 786440 | tf_op jit(solution)/shard_map/ppermute | solution.py:377
  191.0 19.7 %collective-permute-start.47 = (bf16[128,1024]{1,0:T(8,128)(2,1)S(1)}, bf16[128,1024]{1,0:T(8,128)(2,1)S(1)}, u32[]{:S(2)}, u32[]{:S(2)}) collective-permute-start(bf16[128,1024]{1,0:T(8,128)(2,1)S(1)} %get-tuple-element.125), channel_id=1, source_target_pairs={{0,1},{1,0},{2,3},{3,2},{4,5},{5,4},{6,7},{7,6},{8,9},{9,8},{10,11... | collective-permute-start | bytes 786440 | tf_op jit(solution)/shard_map/ppermute | solution.py:377
  206.0 6.6 %collective-permute-start.50 = (bf16[128,1024]{1,0:T(8,128)(2,1)S(1)}, bf16[128,1024]{1,0:T(8,128)(2,1)S(1)}, u32[]{:S(2)}, u32[]{:S(2)}) collective-permute-start(bf16[128,1024]{1,0:T(8,128)(2,1)S(1)} %get-tuple-element.123), channel_id=1, source_target_pairs={{0,4},{1,5},{2,6},{3,7},{4,0},{5,1},{6,2},{7,3},{8,12},{9,13},{10,... | collective-permute-start | bytes 786440 | tf_op jit(solution)/shard_map/ppermute | solution.py:377
  210.7 8.2 %collective-permute-start.59 = (bf16[128,1152]{1,0:T(8,128)(2,1)S(1)}, bf16[128,1152]{1,0:T(8,128)(2,1)S(1)}, u32[]{:S(2)}, u32[]{:S(2)}) collective-permute-start(bf16[128,1152]{1,0:T(8,128)(2,1)S(1)} %get-tuple-element.119), channel_id=1, source_target_pairs={{0,4},{1,5},{2,6},{3,7},{4,0},{5,1},{6,2},{7,3},{8,12},{9,13},{10,... | collective-permute-start | bytes 884744 | tf_op jit(solution)/shard_map/ppermute | solution.py:377
  212.5 33.8 %collective-permute-start.40 = (bf16[256,2048]{1,0:T(8,128)(2,1)S(1)}, bf16[256,2048]{1,0:T(8,128)(2,1)S(1)}, u32[]{:S(2)}, u32[]{:S(2)}) collective-permute-start(bf16[256,2048]{1,0:T(8,128)(2,1)S(1)} %get-tuple-element.97), channel_id=1, source_target_pairs={{0,2},{1,3},{2,0},{3,1},{4,6},{5,7},{6,4},{7,5},{8,10},{9,11},{10,... | collective-permute-start | bytes 3145736 | tf_op jit(solution)/shard_map/ppermute | solution.py:377
  218.9 5.2 %collective-permute-start.57 = (bf16[64,1024]{1,0:T(8,128)(2,1)S(1)}, bf16[64,1024]{1,0:T(8,128)(2,1)S(1)}, u32[]{:S(2)}, u32[]{:S(2)}) collective-permute-start(bf16[64,1024]{1,0:T(8,128)(2,1)S(1)} %slice_add_fusion.18), channel_id=1, source_target_pairs={{0,4},{1,5},{2,6},{3,7},{4,0},{5,1},{6,2},{7,3},{8,12},{9,13},{10,... | collective-permute-start | bytes 393224 | tf_op jit(solution)/shard_map/ppermute | solution.py:377
  224.1 5.0 %collective-permute-start.48 = (bf16[64,1024]{1,0:T(8,128)(2,1)S(1)}, bf16[64,1024]{1,0:T(8,128)(2,1)S(1)}, u32[]{:S(2)}, u32[]{:S(2)}) collective-permute-start(bf16[64,1024]{1,0:T(8,128)(2,1)S(1)} %slice_add_fusion.22), channel_id=1, source_target_pairs={{0,4},{1,5},{2,6},{3,7},{4,0},{5,1},{6,2},{7,3},{8,12},{9,13},{10,... | collective-permute-start | bytes 393224 | tf_op jit(solution)/shard_map/ppermute | solution.py:377
  229.0 5.7 %collective-permute-start.51 = (bf16[64,1024]{1,0:T(8,128)(2,1)S(1)}, bf16[64,1024]{1,0:T(8,128)(2,1)S(1)}, u32[]{:S(2)}, u32[]{:S(2)}) collective-permute-start(bf16[64,1024]{1,0:T(8,128)(2,1)S(1)} %slice_add_fusion.20), channel_id=1, source_target_pairs={{0,1},{1,0},{2,3},{3,2},{4,5},{5,4},{6,7},{7,6},{8,9},{9,8},{10,11... | collective-permute-start | bytes 393224 | tf_op jit(solution)/shard_map/ppermute | solution.py:377
  234.7 5.1 %collective-permute-start.60 = (bf16[64,1152]{1,0:T(8,128)(2,1)S(1)}, bf16[64,1152]{1,0:T(8,128)(2,1)S(1)}, u32[]{:S(2)}, u32[]{:S(2)}) collective-permute-start(bf16[64,1152]{1,0:T(8,128)(2,1)S(1)} %slice_add_fusion.16), channel_id=1, source_target_pairs={{0,1},{1,0},{2,3},{3,2},{4,5},{5,4},{6,7},{7,6},{8,9},{9,8},{10,11... | collective-permute-start | bytes 442376 | tf_op jit(solution)/shard_map/ppermute | solution.py:377
  239.9 34.3 %collective-permute-start.54 = (bf16[16,2048]{1,0:T(8,128)(2,1)S(1)}, bf16[16,2048]{1,0:T(8,128)(2,1)S(1)}, u32[]{:S(2)}, u32[]{:S(2)}) collective-permute-start(bf16[16,2048]{1,0:T(8,128)(2,1)S(1)} %get-tuple-element.138), channel_id=1, source_target_pairs={{0,24},{1,25},{2,26},{3,27},{4,28},{5,29},{6,30},{7,31},{8,16},{9,... | collective-permute-start | bytes 196616 | tf_op jit(solution)/shard_map/ppermute | solution.py:377
  245.8 9.2 %collective-permute-start.38 = (bf16[128,2048]{1,0:T(8,128)(2,1)S(1)}, bf16[128,2048]{1,0:T(8,128)(2,1)S(1)}, u32[]{:S(2)}, u32[]{:S(2)}) collective-permute-start(bf16[128,2048]{1,0:T(8,128)(2,1)S(1)} %get-tuple-element.117), channel_id=1, source_target_pairs={{0,1},{1,0},{2,3},{3,2},{4,5},{5,4},{6,7},{7,6},{8,9},{9,8},{10,11... | collective-permute-start | bytes 1572872 | tf_op jit(solution)/shard_map/ppermute | solution.py:377
  246.5 11.3 %collective-permute-start.41 = (bf16[128,2048]{1,0:T(8,128)(2,1)S(1)}, bf16[128,2048]{1,0:T(8,128)(2,1)S(1)}, u32[]{:S(2)}, u32[]{:S(2)}) collective-permute-start(bf16[128,2048]{1,0:T(8,128)(2,1)S(1)} %get-tuple-element.115), channel_id=1, source_target_pairs={{0,4},{1,5},{2,6},{3,7},{4,0},{5,1},{6,2},{7,3},{8,12},{9,13},{10,... | collective-permute-start | bytes 1572872 | tf_op jit(solution)/shard_map/ppermute | solution.py:377
  255.0 20.1 %collective-permute-start.52 = (bf16[16,2048]{1,0:T(8,128)(2,1)S(1)}, bf16[16,2048]{1,0:T(8,128)(2,1)S(1)}, u32[]{:S(2)}, u32[]{:S(2)}) collective-permute-start(bf16[16,2048]{1,0:T(8,128)(2,1)S(1)} %get-tuple-element.140), channel_id=1, source_target_pairs={{0,8},{1,9},{2,10},{3,11},{4,12},{5,13},{6,14},{7,15},{8,0},{9,1},... | collective-permute-start | bytes 196616 | tf_op jit(solution)/shard_map/ppermute | solution.py:377
  257.7 6.4 %collective-permute-start.39 = (bf16[64,2048]{1,0:T(8,128)(2,1)S(1)}, bf16[64,2048]{1,0:T(8,128)(2,1)S(1)}, u32[]{:S(2)}, u32[]{:S(2)}) collective-permute-start(bf16[64,2048]{1,0:T(8,128)(2,1)S(1)} %slice_add_fusion.14), channel_id=1, source_target_pairs={{0,4},{1,5},{2,6},{3,7},{4,0},{5,1},{6,2},{7,3},{8,12},{9,13},{10,... | collective-permute-start | bytes 786440 | tf_op jit(solution)/shard_map/ppermute | solution.py:377
  264.1 6.4 %collective-permute-start.42 = (bf16[64,2048]{1,0:T(8,128)(2,1)S(1)}, bf16[64,2048]{1,0:T(8,128)(2,1)S(1)}, u32[]{:S(2)}, u32[]{:S(2)}) collective-permute-start(bf16[64,2048]{1,0:T(8,128)(2,1)S(1)} %slice_add_fusion.12), channel_id=1, source_target_pairs={{0,1},{1,0},{2,3},{3,2},{4,5},{5,4},{6,7},{7,6},{8,9},{9,8},{10,11... | collective-permute-start | bytes 786440 | tf_op jit(solution)/shard_map/ppermute | solution.py:377
  270.5 6.4 %collective-permute-start.53 = (bf16[16,2048]{1,0:T(8,128)(2,1)S(1)}, bf16[16,2048]{1,0:T(8,128)(2,1)S(1)}, u32[]{:S(2)}, u32[]{:S(2)}) collective-permute-start(bf16[16,2048]{1,0:T(8,128)(2,1)S(1)} %get-tuple-element.141), channel_id=1, source_target_pairs={{0,16},{1,17},{2,18},{3,19},{4,20},{5,21},{6,22},{7,23},{8,24},{9,... | collective-permute-start | bytes 196616 | tf_op jit(solution)/shard_map/ppermute | solution.py:377
  270.5 7.2 %collective-permute-start.63 = (bf16[16,2176]{1,0:T(8,128)(2,1)S(1)}, bf16[16,2176]{1,0:T(8,128)(2,1)S(1)}, u32[]{:S(2)}, u32[]{:S(2)}) collective-permute-start(bf16[16,2176]{1,0:T(8,128)(2,1)S(1)} %get-tuple-element.134), channel_id=1, source_target_pairs={{0,24},{1,25},{2,26},{3,27},{4,28},{5,29},{6,30},{7,31},{8,16},{9,... | collective-permute-start | bytes 208904 | tf_op jit(solution)/shard_map/ppermute | solution.py:377
  272.4 10.1 %collective-permute-start.61 = (bf16[16,2176]{1,0:T(8,128)(2,1)S(1)}, bf16[16,2176]{1,0:T(8,128)(2,1)S(1)}, u32[]{:S(2)}, u32[]{:S(2)}) collective-permute-start(bf16[16,2176]{1,0:T(8,128)(2,1)S(1)} %get-tuple-element.136), channel_id=1, source_target_pairs={{0,8},{1,9},{2,10},{3,11},{4,12},{5,13},{6,14},{7,15},{8,0},{9,1},... | collective-permute-start | bytes 208904 | tf_op jit(solution)/shard_map/ppermute | solution.py:377
  274.2 8.3 %collective-permute-start.62 = (bf16[16,2176]{1,0:T(8,128)(2,1)S(1)}, bf16[16,2176]{1,0:T(8,128)(2,1)S(1)}, u32[]{:S(2)}, u32[]{:S(2)}) collective-permute-start(bf16[16,2176]{1,0:T(8,128)(2,1)S(1)} %get-tuple-element.137), channel_id=1, source_target_pairs={{0,16},{1,17},{2,18},{3,19},{4,20},{5,21},{6,22},{7,23},{8,24},{9,... | collective-permute-start | bytes 208904 | tf_op jit(solution)/shard_map/ppermute | solution.py:377
  275.1 7.4 %collective-permute-start.45 = (bf16[16,4096]{1,0:T(8,128)(2,1)S(1)}, bf16[16,4096]{1,0:T(8,128)(2,1)S(1)}, u32[]{:S(2)}, u32[]{:S(2)}) collective-permute-start(bf16[16,4096]{1,0:T(8,128)(2,1)S(1)} %get-tuple-element.126), channel_id=1, source_target_pairs={{0,24},{1,25},{2,26},{3,27},{4,28},{5,29},{6,30},{7,31},{8,16},{9,... | collective-permute-start | bytes 393224 | tf_op jit(solution)/shard_map/ppermute | solution.py:377
  276.9 7.0 %collective-permute-start.43 = (bf16[16,4096]{1,0:T(8,128)(2,1)S(1)}, bf16[16,4096]{1,0:T(8,128)(2,1)S(1)}, u32[]{:S(2)}, u32[]{:S(2)}) collective-permute-start(bf16[16,4096]{1,0:T(8,128)(2,1)S(1)} %get-tuple-element.128), channel_id=1, source_target_pairs={{0,8},{1,9},{2,10},{3,11},{4,12},{5,13},{6,14},{7,15},{8,0},{9,1},... | collective-permute-start | bytes 393224 | tf_op jit(solution)/shard_map/ppermute | solution.py:377
  277.7 7.8 %collective-permute-start.44 = (bf16[16,4096]{1,0:T(8,128)(2,1)S(1)}, bf16[16,4096]{1,0:T(8,128)(2,1)S(1)}, u32[]{:S(2)}, u32[]{:S(2)}) collective-permute-start(bf16[16,4096]{1,0:T(8,128)(2,1)S(1)} %get-tuple-element.129), channel_id=1, source_target_pairs={{0,16},{1,17},{2,18},{3,19},{4,20},{5,21},{6,22},{7,23},{8,24},{9,... | collective-permute-start | bytes 393224 | tf_op jit(solution)/shard_map/ppermute | solution.py:377
  (22 other events, 178.3 us)

commit v3 on v2

--- a/solution.py
+++ b/solution.py
@@ -377,57 +377,62 @@
     return lax.ppermute(value, AXES, [(device, device ^ flip) for device in range(32)])
 
 
-def gather_pair(both, width):
-    both = jnp.concatenate([both] + [exchange(both, FLIP_Z * i) for i in (1, 2, 3)], 0)
+def exchange_side(value, step):
+    flips = (FLIP_X, FLIP_Y) if step == 0 else (FLIP_Y, FLIP_X)
+    return lax.ppermute(value, AXES, [(device, device ^ flips[device >> 1 & 1]) for device in range(32)])
+
+
+def tied(values, *others):
+    return lax.optimization_barrier((values, others))[0]
+
+
+def along_z(block):
+    return [exchange(block, FLIP_Z * i) for i in Z_ORDER]
+
+
+Z_ORDER = (1, 2, 3)
+
+
+def join(*parts):
+    return jnp.concatenate(parts, 0)
+
+
+def both_cores(halves):
+    return halves + [exchange(half, FLIP_CORE) for half in halves]
+
+
+def add_halves(kept, came):
+    half = kept.shape[0] // 2
+    return kept[half:] + came[half:], kept[:half] + came[:half]
+
+
+def z_blocks(both):
+    blocks = [both[BLOCK * i : BLOCK * (i + 1)] for i in range(4)]
+    return [blocks[0]] + [exchange(block, FLIP_Z * i) for i, block in zip(Z_ORDER, blocks[1:])]
+
+
+def block_places(me):
     out = []
-    for value, first, second in (
-        (both[:, :width], FLIP_X, FLIP_Y), (both[:, width:], FLIP_Y, FLIP_X)
-    ):
-        value = jnp.concatenate([value, exchange(value, first)], 0)
-        other = exchange(value, second)
-        out.append([value, other, exchange(value, FLIP_CORE), exchange(other, FLIP_CORE)])
-    return out[0] + out[1]
-
-
-def scatter_steps(kept, sent, first, second):
-    came = exchange(sent, FLIP_CORE)
-    for flip in (first, second):
-        half = kept.shape[0] // 2
-        sent = kept[half:] + came[half:]
-        kept = kept[:half] + came[:half]
-        came = exchange(sent, flip)
-    return kept + came
-
-
-def scatter_pair(left, right):
-    left = scatter_steps(left[0], left[1], FLIP_Y, FLIP_X)
-    right = scatter_steps(right[0], right[1], FLIP_X, FLIP_Y)
-    both = jnp.concatenate([left, right], 1)
-    return [both[:BLOCK]] + [
-        exchange(both[BLOCK * i : BLOCK * (i + 1)], FLIP_Z * i) for i in (1, 2, 3)
-    ]
-
-
-def block_flips(first, second):
-    return [
-        (core * 2 + b, (a * 4 + z) * BLOCK, core * FLIP_CORE + b * second + a * first + z * FLIP_Z)
-        for core in (0, 1) for b in (0, 1) for a in (0, 1) for z in range(4)
-    ]
-
-
-LEFT_FLIPS, RIGHT_FLIPS = block_flips(FLIP_X, FLIP_Y), block_flips(FLIP_Y, FLIP_X)
+    for other in (0, 1):
+        core = (me >> 1 & 1) ^ other
+        first, second = FLIP_X - 3 * core, FLIP_Y + 3 * core
+        for b in (0, 1):
+            for a in (0, 1):
+                for i, z in enumerate((0,) + Z_ORDER):
+                    owner = me ^ (other * FLIP_CORE + b * second + a * first + z * FLIP_Z)
+                    out.append((other * 2 + b, (a * 4 + i) * BLOCK, owner))
+    return out
 
 
 def nn(left, right):
     return jnp.dot(left, right, preferred_element_type=F32)
 
 
-def load_blocks(me, flips, pieces, columns, target, target_columns, semaphore):
-    for piece, row, flip in flips:
-        place = pl.multiple_of((me ^ flip) * BLOCK, BLOCK)
+def load_blocks(me, pieces, columns, target, target_columns, semaphore):
+    for piece, row, owner in block_places(me):
         pltpu.make_async_copy(
             pieces[piece].at[pl.ds(row, BLOCK), columns],
-            target.at[pl.ds(place, BLOCK), target_columns],
+            target.at[pl.ds(pl.multiple_of(owner * BLOCK, BLOCK), BLOCK), target_columns],
             semaphore,
         ).start()
 
@@ -436,11 +441,10 @@
     pltpu.make_async_copy(target, target, semaphore).wait()
 
 
-def store_blocks(me, flips, source, columns, targets, target_columns, semaphore):
-    for piece, row, flip in flips:
-        place = pl.multiple_of((me ^ flip) * BLOCK, BLOCK)
+def store_blocks(me, source, columns, targets, target_columns, semaphore):
+    for piece, row, owner in block_places(me):
         pltpu.make_async_copy(
-            source.at[pl.ds(place, BLOCK), columns],
+            source.at[pl.ds(pl.multiple_of(owner * BLOCK, BLOCK), BLOCK), columns],
             targets[piece // 2].at[pl.ds((piece % 2) * 128 + row, BLOCK), target_columns],
             semaphore,
         ).start()
@@ -524,7 +528,7 @@
 
 
 def attend_back(
-    queries, upstream, keys, values, log_rows, dot_rows, query_row, key_seg, query_grad, pair_grad
+    queries, upstream, keys, values, log_rows, dot_rows, query_row, key_seg, query_grad, pair_grad, pairs
 ):
     (key_ref, key_at), (value_ref, value_at) = keys, values
     query_grad[...] = jnp.zeros_like(query_grad)
@@ -533,8 +537,8 @@
         rows = pl.ds(pl.multiple_of(index * TILE, TILE), TILE)
         same = jnp.concatenate([key_seg[rows, :]] * (OWN // TILE), 1) == query_row
         bias = jnp.where(same, 0.0, MASKED)
-        for pair in range(HEADS // 2):
-            at = pair * TILE
+        for pair in pairs:
+            at, to = pair * TILE, (pair - pairs[0]) * TILE
             query = queries[:, at : at + TILE]
             grad = upstream[:, at : at + TILE]
             key = key_ref[rows, key_at + at : key_at + at + TILE]
@@ -552,24 +556,39 @@
                 value_parts.append(nn(weights.astype(BF16), grad))
                 key_parts.append(nn(score_grad, query))
                 total = total + transposed(score_grad, one_key)
-            query_grad[:, at : at + TILE] += total
+            query_grad[:, to : to + TILE] += total
             keep = lane_half(key_parts[0].shape, 0)
-            pair_grad[rows, at : at + TILE] = jnp.where(keep, *key_parts).astype(BF16)
-            pair_grad[rows, MODEL + at : MODEL + at + TILE] = jnp.where(keep, *value_parts).astype(BF16)
+            pair_grad[rows, to : to + TILE] = jnp.where(keep, *key_parts).astype(BF16)
+            to = to + len(pairs) * TILE
+            pair_grad[rows, to : to + TILE] = jnp.where(keep, *value_parts).astype(BF16)
         return unused
 
     lax.fori_loop(0, key_seg.shape[0] // TILE, block, 0)
 
 
 def pack_body(
-    place, vectors, project, output, query, keyval, crossout, up, down, states,
-    one, two, three, window, semaphore
+    place, vectors, project, output, query, keyval, crossout, up, down, states, source,
+    one, two, three, near, own_source, block, semaphores
 ):
     me, side = place[0], place[1]
-    send = pltpu.make_async_copy(
-        states.at[pl.ds(pl.multiple_of((1 - side) * WINDOW, WINDOW), WINDOW), :], window, semaphore
-    )
-    send.start()
+    copies = [
+        (project, one.at[:, :1536]),
+        (output, two.at[:, :512]),
+        (query, two.at[:, 512:1024]),
+        (keyval, two.at[:, 1024:2048]),
+        (crossout, two.at[:, 2048:]),
+        (up, three.at[:, :FEED]),
+    ] + [
+        (down.at[part * BLOCK : (part + 1) * BLOCK, :], three.at[:, FEED + part * 512 : FEED + (part + 1) * 512])
+        for part in range(4)
+    ] + [
+        (states.at[pl.ds(pl.multiple_of((1 - side) * WINDOW, WINDOW), WINDOW), :], near)
+    ]
+    copies = [pltpu.make_async_copy(*copy, semaphores.at[i]) for i, copy in enumerate(copies)]
+    for copy in copies:
+        copy.start()
+    gap = jnp.zeros((HALF_SOURCE - source.shape[0], MODEL), F32)
+    own_source[...] = jnp.concatenate([source[...].astype(F32), gap], 0).astype(BF16)
     values = jnp.broadcast_to(vectors[...].astype(F32), (8, 256))
     lanes = lax.broadcasted_iota(jnp.int32, (8, TILE), 1)
     rows = lax.broadcasted_iota(jnp.int32, (8, TILE), 0)
@@ -582,27 +601,19 @@
     moved = pltpu.roll(values, wide + 256 - 112, 1)[:, :TILE]
     inside = jnp.logical_and(lanes >= wide, lanes < wide + 64)
     packed = jnp.where(jnp.logical_and(rows == 7, inside), moved, packed)
-    one[:, :1536] = project[...]
-    one[:, 1536:] = jnp.concatenate([packed, jnp.zeros((8, TILE), F32)], 0).astype(BF16)
-    two[:, :512] = output[...]
-    two[:, 512:1024] = query[...]
-    two[:, 1024:2048] = keyval[...]
-    two[:, 2048:] = crossout[...]
-    three[:, :FEED] = up[...]
-    for part in range(4):
-        three[:, FEED + part * 512 : FEED + (part + 1) * 512] = down[part * BLOCK : (part + 1) * BLOCK, :]
-    send.wait()
-
-
-def self_body(place, segments, states, window, *refs):
-    pieces, refs = refs[:8], refs[8:]
-    queries, pair, mixed, log_rows, lowered, vectors, up_bias, weight, packed, query_seg, sems = refs
-    me, side = place[0], place[1]
-    load_blocks(me, RIGHT_FLIPS, pieces[4:], slice(768, 896), packed, slice(0, 128), sems.at[0])
-    load_blocks(me, LEFT_FLIPS, pieces[:4], slice(0, 768), weight, slice(0, 768), sems.at[1])
-    load_blocks(me, RIGHT_FLIPS, pieces[4:], slice(0, 768), weight, slice(768, 1536), sems.at[2])
-    query_seg[...] = spread(own_segments_of(side, segments[...]))
-    key_row = key_segments_of(side, segments[...])
+    block[...] = jnp.concatenate([packed, jnp.zeros((8, TILE), F32)], 0).astype(BF16)
+    last = pltpu.make_async_copy(block, one.at[:, 1536:], semaphores.at[len(copies)])
+    last.start()
+    for copy in copies + [last]:
+        copy.wait()
+
+
+def self_body(place, states, window, *refs):
+    pieces, refs = refs[:4], refs[4:]
+    queries, pair, lowered, vectors, up_bias, weight, packed, sems = refs
+    me = place[0]
+    load_blocks(me, pieces, slice(1536, 1664), packed, slice(0, 128), sems.at[0])
+    load_blocks(me, pieces, slice(0, 1536), weight, slice(0, 1536), sems.at[1])
     wait_all(packed, sems.at[0])
     for tile in range(4):
         total = jnp.zeros((8, TILE), F32)
@@ -620,29 +631,29 @@
         rows = slice(i * TILE, (i + 1) * TILE)
         value = states[rows, :] if i < 4 else window[(i - 4) * TILE : (i - 3) * TILE, :]
         lowered[rows, :] = (normed_rows(value.astype(F32))[0] * gain + shift).astype(BF16)
-    wait_all(weight.at[:, :768], sems.at[1])
-    wait_all(weight.at[:, 768:], sems.at[2])
+    wait_all(weight, sems.at[1])
     for i in range(KEYS // 256):
         rows = slice(i * 256, (i + 1) * 256)
         if i < 2:
             queries[rows, :] = (nn(lowered[rows, :], weight[:, :512]) .astype(BF16) * SCALE).astype(BF16)
         pair[rows, :] = nn(lowered[rows, :], weight[:, 512:]).astype(BF16)
+
+
+def self_mix_body(place, segments, queries, pair, mixed, log_rows, query_seg):
+    query_seg[...] = spread(own_segments_of(place[1], segments[...]))
+    key_row = key_segments_of(place[1], segments[...])
     attend(queries, (pair, 0), (pair, MODEL), mixed, log_rows, query_seg, key_row)
 
 
-def cross_body(place, segments, source_segments, states, own_source, other_source, self_mixed, vectors, *refs):
-    pieces, refs = refs[:8], refs[8:]
-    after_self, lowered, queries, pair, mixed, log_rows, after_cross, source, weight, query_seg, sems = refs
+def cross_body(place, states, own_source, other_source, self_mixed, vectors, *refs):
+    pieces, refs = refs[:4], refs[4:]
+    after_self, lowered, queries, pair, weight, source, sems = refs
     me, side = place[0], place[1]
-    load_blocks(me, LEFT_FLIPS, pieces[:4], slice(0, 1280), weight, slice(0, 1280), sems.at[0])
-    load_blocks(me, RIGHT_FLIPS, pieces[4:], slice(0, 1280), weight, slice(1280, 2560), sems.at[1])
-    query_seg[...] = spread(own_segments_of(side, segments[...]))
-    key_row = source_segments[...].astype(F32)
+    load_blocks(me, pieces, slice(0, 2560), weight, slice(0, 2560), sems.at[0])
     source[:HALF_SOURCE, :] = jnp.where(side == 0, own_source[...], other_source[...])
     source[HALF_SOURCE:, :] = jnp.where(side == 0, other_source[...], own_source[...])
     gain, shift = vectors[3:4, :], vectors[4:5, :]
-    wait_all(weight.at[:, :1280], sems.at[0])
-    wait_all(weight.at[:, 1280:], sems.at[1])
+    wait_all(weight, sems.at[0])
     pair[...] = nn(source[...], weight[:, 1024:2048]).astype(BF16)
     for i in range(2):
         rows = slice(i * 256, (i + 1) * 256)
@@ -650,7 +661,13 @@
         after_self[rows, :] = value
         lowered[rows, :] = (normed_rows(value)[0] * gain + shift).astype(BF16)
         queries[rows, :] = (nn(lowered[rows, :], weight[:, 512:1024]).astype(BF16) * SCALE).astype(BF16)
-    attend(queries, (pair, 0), (pair, MODEL), mixed, log_rows, query_seg, key_row)
+
+
+def cross_mix_body(
+    place, segments, source_segments, queries, pair, after_self, weight, mixed, log_rows, after_cross, query_seg
+):
+    query_seg[...] = spread(own_segments_of(place[1], segments[...]))
+    attend(queries, (pair, 0), (pair, MODEL), mixed, log_rows, query_seg, source_segments[...].astype(F32))
     for i in range(2):
         rows = slice(i * 256, (i + 1) * 256)
         after_cross[rows, :] = after_self[rows, :] + nn(mixed[rows, :], weight[:, 2048:])
@@ -660,18 +677,18 @@
 
 
 def feed_body(place, after_cross, output_grad, vectors, up_bias, *refs):
-    pieces, refs = refs[:8], refs[8:]
+    pieces, refs = refs[:4], refs[4:]
     (
-        layer_out, after_grad, up_keep, up_send, down_keep, down_send, sums, bias_sums,
+        layer_out, after_grad, kept, sent, sums, bias_sums,
         up, down, lowered, flipped, total, back, up_grad, down_grad, sems,
     ) = refs
     me = place[0]
-    load_blocks(me, LEFT_FLIPS, pieces[:4], slice(0, FEED), up, slice(0, FEED), sems.at[0])
+    load_blocks(me, pieces, slice(0, FEED), up, slice(0, FEED), sems.at[0])
     for part in range(4):
-        for piece, row, flip in RIGHT_FLIPS:
-            spot = pl.multiple_of((me ^ flip) * 64 + part * BLOCK, BLOCK)
+        for piece, row, owner in block_places(me):
+            spot = pl.multiple_of(owner * 64 + part * BLOCK, BLOCK)
             pltpu.make_async_copy(
-                pieces[4 + piece].at[pl.ds(row, BLOCK), slice(part * 512, (part + 1) * 512)],
+                pieces[piece].at[pl.ds(row, BLOCK), slice(FEED + part * 512, FEED + (part + 1) * 512)],
                 down.at[pl.ds(spot, BLOCK), :],
                 sems.at[1],
             ).start()
@@ -706,14 +723,14 @@
         return unused
 
     lax.fori_loop(0, FEED // CHUNK, chunk, 0)
-    store_blocks(me, LEFT_FLIPS, up_grad, slice(0, FEED), (up_keep, up_send), slice(0, FEED), sems.at[2])
+    store_blocks(me, up_grad, slice(0, FEED), (kept, sent), slice(0, FEED), sems.at[2])
     for part in range(4):
-        for piece, row, flip in RIGHT_FLIPS:
-            spot = pl.multiple_of((me ^ flip) * 64 + part * BLOCK, BLOCK)
+        for piece, row, owner in block_places(me):
+            spot = pl.multiple_of(owner * 64 + part * BLOCK, BLOCK)
             pltpu.make_async_copy(
                 down_grad.at[pl.ds(spot, BLOCK), :],
-                (down_keep, down_send)[piece // 2].at[
-                    pl.ds((piece % 2) * 128 + row, BLOCK), slice(part * 512, (part + 1) * 512)
+                (kept, sent)[piece // 2].at[
+                    pl.ds((piece % 2) * 128 + row, BLOCK), slice(FEED + part * 512, FEED + (part + 1) * 512)
                 ],
                 sems.at[3],
             ).start()
@@ -734,40 +751,36 @@
 
 
 def cross_back_body(
-    place, segments, source_segments, own_source, other_source, after_self, lowered, queries, pair,
-    mixed, log_rows, after_grad, vectors, sums, *refs
+    place, segments, source_segments, own_source, other_source, queries, pair, mixed, log_rows, after_grad, weight,
+    asked, source_own, source_send, grads, upstream, query_grad, pair_grad, source, key_seg,
 ):
-    pieces, refs = refs[:8], refs[8:]
-    (
-        self_grad, source_own, source_send, left_keep, left_send, right_keep, right_send, new_sums,
-        source, weight, upstream, query_grad, pair_grad, left_grad, right_grad, key_seg, sems,
-    ) = refs
-    me, side = place[0], place[1]
-    load_blocks(me, RIGHT_FLIPS, pieces[4:], slice(0, 1280), weight, slice(1280, 2560), sems.at[1])
-    load_blocks(me, LEFT_FLIPS, pieces[:4], slice(0, 1280), weight, slice(0, 1280), sems.at[0])
+    side = place[1]
     key_seg[...] = spread(source_segments[...].astype(F32))
     query_row = own_segments_of(side, segments[...])
     source[:HALF_SOURCE, :] = jnp.where(side == 0, own_source[...], other_source[...])
     source[HALF_SOURCE:, :] = jnp.where(side == 0, other_source[...], own_source[...])
-    wait_all(weight.at[:, 1280:], sems.at[1])
-    wait_all(weight.at[:, :1280], sems.at[0])
     grad_low = after_grad[...].astype(BF16)
     upstream[...] = against(grad_low, weight[:, 2048:]).astype(BF16)
-    left_grad[:, :512] = transposed(mixed[...], grad_low).astype(BF16)
     dot_rows = head_dots(upstream[...], mixed[...])
+    grads[:, :512] = transposed(mixed[...], grad_low).astype(BF16)
     attend_back(
         queries, upstream, (pair, 0), (pair, MODEL), log_rows, dot_rows, query_row, key_seg,
-        query_grad, pair_grad,
-    )
-    asked = (query_grad[...] * SCALE).astype(BF16)
-    left_grad[:, 512:] = transposed(lowered[...], asked).astype(BF16)
-    right_grad[...] = transposed(source[...], pair_grad[...]).astype(BF16)
-    store_blocks(me, LEFT_FLIPS, left_grad, slice(0, 1024), (left_keep, left_send), slice(0, 1024), sems.at[2])
-    store_blocks(me, RIGHT_FLIPS, right_grad, slice(0, 1024), (right_keep, right_send), slice(0, 1024), sems.at[3])
+        query_grad, pair_grad, (0, 1, 2, 3),
+    )
+    asked[...] = (query_grad[...] * SCALE).astype(BF16)
+    grads[:, 512:] = transposed(source[...], pair_grad[...]).astype(BF16)
     back = against(pair_grad[...], weight[:, 1024:2048])
     first, second = back[:HALF_SOURCE], back[HALF_SOURCE:]
     source_own[...] = jnp.where(side == 0, first, second)
     source_send[...] = jnp.where(side == 0, second, first).astype(BF16)
+
+
+def cross_weight_body(
+    place, after_self, lowered, self_mixed, after_grad, asked, vectors, sums, weight, some_grads, *refs
+):
+    self_grad, upstream, dot_rows, kept, sent, new_sums, grads, sems = refs
+    me = place[0]
+    store_blocks(me, some_grads, slice(0, 1536), (kept, sent), slice(0, 1536), sems.at[0])
     gain = vectors[3:4, :]
     gain_sum, shift_sum = jnp.zeros((1, MODEL), F32), jnp.zeros((1, MODEL), F32)
     for i in range(2):
@@ -776,71 +789,90 @@
         up = against(asked[rows, :], weight[:, 512:1024])
         self_grad[rows, :] = after_grad[rows, :] + norm_back_rows(up, normed, inverse, gain)
         gain_sum, shift_sum = gain_sum + column_sum(up * normed), shift_sum + column_sum(up)
+    grads[:, :512] = transposed(lowered[...], asked[...]).astype(BF16)
+    grad_low = self_grad[...].astype(BF16)
+    grads[:, 512:] = transposed(self_mixed[...], grad_low).astype(BF16)
+    store_blocks(me, grads, slice(0, 1024), (kept, sent), slice(1536, 2560), sems.at[1])
+    upstream[...] = against(grad_low, weight[:, :512]).astype(BF16)
+    dot_rows[...] = head_dots(upstream[...], self_mixed[...])
     zero = jnp.zeros((1, MODEL), F32)
     new_sums[...] = sums[...] + jnp.concatenate(
         [zero, zero, zero, gain_sum, shift_sum, zero, zero, zero], 0
     )
-    wait_all(left_grad, sems.at[2])
-    wait_all(right_grad, sems.at[3])
+    wait_all(some_grads, sems.at[0])
+    wait_all(grads, sems.at[1])
+
+
+def project_grads(lowered, asked, pair_grad, weight, at, grads, back):
+    grads[:, :256] = transposed(lowered[:OWN, :], asked).astype(BF16)
+    grads[:, 256:512] = transposed(lowered[...], pair_grad[:, :256]).astype(BF16)
+    grads[:, 512:768] = transposed(lowered[...], pair_grad[:, 256:]).astype(BF16)
+    for i in range(3):
+        rows = slice(i * 256, (i + 1) * 256)
+        part = against(pair_grad[rows, :256], weight[:, 512 + at : 768 + at]) + against(
+            pair_grad[rows, 256:], weight[:, 1024 + at : 1280 + at]
+        )
+        if i < 2:
+            part = part + against(asked[rows, :], weight[:, at : at + 256])
+        back(rows, part)
 
 
 def self_back_body(
-    place, segments, states, window, lowered, queries, pair, mixed, log_rows, self_grad, vectors,
+    place, segments, lowered, queries, pair, log_rows, upstream, dot_rows, weight,
+    part_back, left_keep, left_send, query_grad, pair_grad, left_grad, key_seg, sems,
+):
+    key_seg[...] = spread(key_segments_of(place[1], segments[...]))
+    query_row = own_segments_of(place[1], segments[...])
+    attend_back(
+        queries, upstream, (pair, 0), (pair, MODEL), log_rows, dot_rows, query_row, key_seg,
+        query_grad, pair_grad, (0, 1),
+    )
+
+    def keep(rows, part):
+        part_back[rows, :] = part
+
+    project_grads(lowered, (query_grad[...] * SCALE).astype(BF16), pair_grad, weight, 0, left_grad, keep)
+    store_blocks(place[0], left_grad, slice(0, 768), (left_keep, left_send), slice(0, 768), sems.at[0])
+    wait_all(left_grad, sems.at[0])
+
+
+def self_last_body(
+    place, segments, states, window, lowered, queries, pair, log_rows, upstream, dot_rows, weight, part_back,
     sums, bias_sums, *refs
 ):
-    pieces, more, refs = refs[:8], refs[8:12], refs[12:]
-    (
-        own_back, send_back, left_keep, left_send, right_keep, right_send,
-        weight, output, upstream, query_grad, pair_grad, left_grad, right_grad, key_seg, sems,
-    ) = refs
-    me, side = place[0], place[1]
-    load_blocks(me, LEFT_FLIPS, more, slice(0, 512), output, slice(0, 512), sems.at[4])
-    load_blocks(me, LEFT_FLIPS, pieces[:4], slice(0, 768), weight, slice(0, 768), sems.at[0])
-    load_blocks(me, RIGHT_FLIPS, pieces[4:], slice(0, 768), weight, slice(768, 1536), sems.at[1])
-    key_seg[...] = spread(key_segments_of(side, segments[...]))
-    query_row = own_segments_of(side, segments[...])
-    wait_all(output, sems.at[4])
-    grad_low = self_grad[...].astype(BF16)
-    upstream[...] = against(grad_low, output[...]).astype(BF16)
-    right_grad[:, 512:1024] = transposed(mixed[...], grad_low).astype(BF16)
-    dot_rows = head_dots(upstream[...], mixed[...])
+    own_back, send_back, right_keep, right_send, query_grad, pair_grad, right_grad, key_seg, sems = refs
+    key_seg[...] = spread(key_segments_of(place[1], segments[...]))
+    query_row = own_segments_of(place[1], segments[...])
     attend_back(
         queries, upstream, (pair, 0), (pair, MODEL), log_rows, dot_rows, query_row, key_seg,
-        query_grad, pair_grad,
-    )
-    wait_all(weight.at[:, :768], sems.at[0])
-    wait_all(weight.at[:, 768:], sems.at[1])
-    asked = (query_grad[...] * SCALE).astype(BF16)
-    left_grad[:, :512] = transposed(lowered[:OWN, :], asked).astype(BF16)
-    left_grad[:, 512:] = transposed(lowered[...], pair_grad[:, :512]).astype(BF16)
-    right_grad[:, :512] = transposed(lowered[...], pair_grad[:, 512:]).astype(BF16)
-    store_blocks(me, LEFT_FLIPS, left_grad, slice(0, 1024), (left_keep, left_send), slice(0, 1024), sems.at[2])
-    gain_sum, shift_sum = jnp.zeros((1, MODEL), F32), jnp.zeros((1, MODEL), F32)
-    for i in range(3):
-        rows = slice(i * 256, (i + 1) * 256)
-        back = against(pair_grad[rows, :], weight[:, 512:])
-        if i < 2:
-            back = back + against(asked[rows, :], weight[:, :512])
-            own_back[rows, :] = back
+        query_grad, pair_grad, (2, 3),
+    )
+    gain_sum, shift_sum = [jnp.zeros((1, MODEL), F32)], [jnp.zeros((1, MODEL), F32)]
+
+    def finish(rows, part):
+        part = part + part_back[rows, :]
+        if rows.start < OWN:
+            own_back[rows, :] = part
             value = states[rows, :]
         else:
-            send_back[...] = back.astype(BF16)
+            send_back[...] = part.astype(BF16)
             value = window[...]
         normed = normed_rows(value.astype(F32))[0]
-        gain_sum, shift_sum = gain_sum + column_sum(back * normed), shift_sum + column_sum(back)
+        gain_sum[0], shift_sum[0] = gain_sum[0] + column_sum(part * normed), shift_sum[0] + column_sum(part)
+
+    project_grads(lowered, (query_grad[...] * SCALE).astype(BF16), pair_grad, weight, 256, right_grad, finish)
     zero = jnp.zeros((1, MODEL), F32)
-    sums = sums[...] + jnp.concatenate([zero, gain_sum, shift_sum, zero, zero, zero, zero, zero], 0)
+    sums = sums[...] + jnp.concatenate([zero, gain_sum[0], shift_sum[0], zero, zero, zero, zero, zero], 0)
     last = lax.broadcasted_iota(jnp.int32, (8, TILE), 0) == 7
     for device in range(32):
         tile, wide = device // 8 * TILE, device // 2 * TILE
         value = jnp.where(last, bias_sums[:, wide : wide + TILE], sums[:, tile : tile + TILE])
         high = value.astype(BF16).astype(F32)
-        right_grad[device * BLOCK : (device + 1) * BLOCK, 1024:] = jnp.concatenate(
+        right_grad[device * BLOCK : (device + 1) * BLOCK, 768:] = jnp.concatenate(
             [high, value - high], 0
         ).astype(BF16)
-    store_blocks(me, RIGHT_FLIPS, right_grad, slice(0, 1152), (right_keep, right_send), slice(0, 1152), sems.at[3])
-    wait_all(left_grad, sems.at[2])
-    wait_all(right_grad, sems.at[3])
+    store_blocks(place[0], right_grad, slice(0, 896), (right_keep, right_send), slice(0, 896), sems.at[0])
+    wait_all(right_grad, sems.at[0])
 
 
 def target_body(place, back, came, states, self_grad, vectors, out):
@@ -856,7 +888,7 @@
 
 def finish_body(place, *refs):
     feed, cross, last, outs = refs[:4], refs[4:8], refs[8:12], refs[12:]
-    project, output, query, keyval, crossout, up, down, small = outs
+    project, output, query, keyval, crossout, up, down, *small = outs
     me = place[0]
 
     def total(parts, begin, end):
@@ -869,16 +901,20 @@
     for part in range(4):
         down[part * BLOCK : (part + 1) * BLOCK, :] = total(feed, FEED + part * 512, FEED + (part + 1) * 512)
     crossout[...] = total(cross, 0, 512)
-    query[...] = total(cross, 512, 1024)
-    keyval[...] = total(cross, 1024, 2048)
-    project[...] = total(last, 0, 1536)
-    output[...] = total(last, 1536, 2048)
-    value = total(last, 2048, 2176)
+    keyval[...] = total(cross, 512, 1536)
+    query[...] = total(cross, 1536, 2048)
+    output[...] = total(cross, 2048, 2560)
+    for part in range(6):
+        to = part // 2 * 512 + part % 2 * 256
+        at = part // 2 * 256 + part % 2 * 768
+        project[:, to : to + 256] = total(last, at, at + 256)
+    value = total(last, 1536, 1664)
     value = value[:8] + value[8:]
     narrow = pltpu.roll(value, (TILE - (me & 7) * 16) & 127, 1)
     wide = pltpu.roll(value, (TILE - (me & 1) * 64) & 127, 1)
-    last_row = lax.broadcasted_iota(jnp.int32, (8, TILE), 0) == 7
-    small[...] = jnp.where(last_row, wide, narrow)
+    for row in range(7):
+        small[row][...] = narrow[row : row + 1, :16]
+    small[7][...] = wide[7:8, :64]
 
 
 def shape_of(*shape, dtype=BF16):
@@ -887,20 +923,21 @@
 
 VMEM_SPEC = pl.BlockSpec(memory_space=pltpu.VMEM)
 ANY_SPEC = pl.BlockSpec(memory_space=pl.ANY)
+HBM_SPEC = pl.BlockSpec(memory_space=pltpu.HBM)
 SMEM_SPEC = pl.BlockSpec(memory_space=pltpu.SMEM)
 
 
-def call(body, name, place, inputs, pieces, outs, scratch, flops, any_outs=(), any_ins=()):
+def call(body, name, place, inputs, pieces, outs, scratch, flops, any_outs=(), any_ins=(), vmem=40):
     return pl.pallas_call(
         body,
         name=name,
         out_shape=outs,
         in_specs=[SMEM_SPEC]
-        + [ANY_SPEC if i in any_ins else VMEM_SPEC for i in range(len(inputs))]
+        + [HBM_SPEC if i in any_ins else VMEM_SPEC for i in range(len(inputs))]
         + [ANY_SPEC] * len(pieces),
         out_specs=[ANY_SPEC if i in any_outs else VMEM_SPEC for i in range(len(outs))],
         scratch_shapes=scratch,
-        compiler_params=pltpu.CompilerParams(vmem_limit_bytes=40 * 2**20),
+        compiler_params=pltpu.CompilerParams(vmem_limit_bytes=vmem * 2**20),
         cost_estimate=pl.CostEstimate(flops=flops, bytes_accessed=4 * 2**20, transcendentals=0),
     )(place, *inputs, *pieces)
 
@@ -914,108 +951,194 @@
     side = lax.axis_index("seq")
     place = jnp.stack([lax.axis_index("rows") * 2 + side, side]).astype(jnp.int32)
     states, grad = target_states[0], output_grad[0]
-    small = jnp.concatenate([
-        output_bias, first_gain, first_shift, second_gain, second_shift, third_gain, third_shift,
-        hidden_bias, jnp.zeros((80,), BF16),
-    ]).reshape(1, 256)
-    one, two, three, near = call(
+    small = jnp.pad(hidden_bias, (112, 80))
+    for i, vector in enumerate(
+        (output_bias, first_gain, first_shift, second_gain, second_shift, third_gain, third_shift)
+    ):
+        small = small + jnp.pad(vector, (16 * i, 240 - 16 * i))
+    small = small.reshape(1, 256)
+    one, two, three, near, own_source = call(
         pack_body, "pack", place,
-        [small, self_project, self_output, cross_query, cross_keyval, cross_output, hidden_up, hidden_down, states],
-        [], [shape_of(16, 1664), shape_of(16, 2560), shape_of(16, 4096), shape_of(WINDOW, MODEL)],
-        [dma], 1000000, any_outs=(3,), any_ins=(8,),
-    )
+        [
+            small, self_project, self_output, cross_query, cross_keyval, cross_output, hidden_up, hidden_down, states,
+            source_states[0],
+        ],
+        [],
+        [
+            shape_of(16, 1664), shape_of(16, 2560), shape_of(16, 4096), shape_of(WINDOW, MODEL),
+            shape_of(HALF_SOURCE, MODEL),
+        ],
+        [vmem((BLOCK, TILE), BF16), dma((12,))], 1000000, any_ins=range(1, 9), vmem=60,
+    )
+    parts_one = along_z(one)
     window = exchange(near, FLIP_Y)
-    pieces_one = gather_pair(one, 768)
-    pieces_two = gather_pair(two, 1280)
-    pieces_three = gather_pair(three, FEED)
+    one = join(one, *parts_one)
+    came = exchange_side(one, 0)
+    two, window = tied((two, window), came)
+    parts_two = along_z(two)
+    one = tied(join(one, came), window)
+    other = exchange_side(one, 1)
+    parts_two = tied(parts_two, other)
+    pieces_one = both_cores([one, other])
+    two = join(two, *parts_two)
+    came = exchange_side(two, 0)
     half = source_states.shape[1]
-    own_source = jnp.pad(source_states[0], ((0, HALF_SOURCE - half), (0, 0)))
-    other_source = exchange(own_source, FLIP_Y)
     gap = jnp.full((1, HALF_SOURCE - half), -1, jnp.int32)
     source_seg = jnp.concatenate([source_segments[:, :half], gap, source_segments[:, half:], gap], 1)
 
-    queries, pair, mixed, logs, lowered, vectors, up_bias = call(
-        self_body, "self_forward", place, [target_segments, states, window], pieces_one,
+    queries, pair, lowered, vectors, up_bias, weight_one = call(
+        self_body, "self_lower", place, [states, window], pieces_one,
         [
-            shape_of(OWN, MODEL), shape_of(KEYS, 2 * MODEL), shape_of(OWN, MODEL), shape_of(HEADS, OWN, dtype=F32),
-            shape_of(KEYS, MODEL), shape_of(8, MODEL, dtype=F32), shape_of(1, FEED, dtype=F32),
+            shape_of(OWN, MODEL), shape_of(KEYS, 2 * MODEL), shape_of(KEYS, MODEL), shape_of(8, MODEL, dtype=F32),
+            shape_of(1, FEED, dtype=F32), shape_of(MODEL, 1536),
         ],
-        [vmem((MODEL, 1536), BF16), vmem((MODEL, TILE), BF16), vmem((OWN, TILE), F32), dma((3,))],
-        5000000000,
-    )
-    after_self, lowered_two, queries_two, pair_two, mixed_two, logs_two, after_cross = call(
-        cross_body, "cross_forward", place,
-        [target_segments, source_seg, states, own_source, other_source, mixed, vectors], pieces_two,
+        [vmem((MODEL, TILE), BF16), dma((3,))], 3000000000,
+    )
+    came, two, three, sent_source = tied((came, two, three, own_source), queries)
+    parts_three = along_z(three)
+    other_source = exchange(sent_source, FLIP_Y)
+    two = join(two, came)
+    two_core = exchange(two, FLIP_CORE)
+    other = exchange_side(two, 1)
+    mixed, logs = call(
+        self_mix_body, "self_mix", place, [target_segments, queries, pair], [],
+        [shape_of(OWN, MODEL), shape_of(HEADS, OWN, dtype=F32)], [vmem((OWN, TILE), F32)], 8000000000,
+    )
+    other, two_core, parts_three, three, other_source = tied(
+        (other, two_core, parts_three, three, other_source), mixed
+    )
+    pieces_two = [two, other, two_core, exchange(other, FLIP_CORE)]
+    three = join(three, *parts_three)
+    came = exchange_side(three, 0)
+    after_self, lowered_two, queries_two, pair_two, weight_two = call(
+        cross_body, "cross_lower", place, [states, own_source, other_source, mixed, vectors], pieces_two,
         [
             shape_of(OWN, MODEL, dtype=F32), shape_of(OWN, MODEL), shape_of(OWN, MODEL), shape_of(SOURCES, 2 * MODEL),
-            shape_of(OWN, MODEL), shape_of(HEADS, OWN, dtype=F32), shape_of(OWN, MODEL, dtype=F32),
+            shape_of(MODEL, 2560),
         ],
-        [vmem((SOURCES, MODEL), BF16), vmem((MODEL, 2560), BF16), vmem((OWN, TILE), F32), dma((2,))],
-        5000000000,
-    )
-    layer_out, after_grad, up_keep, up_send, down_keep, down_send, sums, bias_sums = call(
+        [vmem((SOURCES, MODEL), BF16), dma((2,))], 3000000000,
+    )
+    came, three = tied((came, three), queries_two)
+    three = join(three, came)
+    three_core = exchange(three, FLIP_CORE)
+    other = exchange_side(three, 1)
+    mixed_two, logs_two, after_cross = call(
+        cross_mix_body, "cross_mix", place,
+        [target_segments, source_seg, queries_two, pair_two, after_self, weight_two], [],
+        [shape_of(OWN, MODEL), shape_of(HEADS, OWN, dtype=F32), shape_of(OWN, MODEL, dtype=F32)],
+        [vmem((OWN, TILE), F32)], 8000000000,
+    )
+    three_core, other = tied((three_core, other), after_cross)
+    pieces_three = [three, other, three_core, exchange(other, FLIP_CORE)]
+    layer_out, after_grad, feed_kept, feed_sent, sums, bias_sums = call(
         feed_body, "feed", place, [after_cross, grad, vectors, up_bias], pieces_three,
-        [shape_of(OWN, MODEL), shape_of(OWN, MODEL, dtype=F32)] + [shape_of(256, FEED)] * 4
+        [shape_of(OWN, MODEL), shape_of(OWN, MODEL, dtype=F32)] + [shape_of(256, 2 * FEED)] * 2
         + [shape_of(8, MODEL, dtype=F32), shape_of(1, FEED, dtype=F32)],
         [
             vmem((MODEL, FEED), BF16), vmem((FEED, MODEL), BF16), vmem((OWN, MODEL), BF16), vmem((MODEL, OWN), BF16),
             vmem((OWN, MODEL), F32), vmem((OWN, MODEL), F32), vmem((MODEL, FEED), BF16), vmem((FEED, MODEL), BF16),
             dma((4,)),
         ],
-        10000000000, any_outs=(2, 3, 4, 5),
-    )
-    feed = scatter_pair((up_keep, up_send), (down_keep, down_send))
-    self_grad, source_own, source_send, *cross_sends, sums = call(
+        10000000000, any_outs=(2, 3),
+    )
+    feed_sent, feed_kept = add_halves(feed_kept, exchange(feed_sent, FLIP_CORE))
+    after_grad = tied(after_grad, feed_sent)
+    feed_came = exchange_side(feed_sent, 1)
+    asked, source_own, source_send, some_grads = call(
         cross_back_body, "cross_backward", place,
         [
-            target_segments, source_seg, own_source, other_source, after_self, lowered_two, queries_two, pair_two,
-            mixed_two, logs_two, after_grad, vectors, sums,
+            target_segments, source_seg, own_source, other_source, queries_two, pair_two, mixed_two, logs_two,
+            after_grad, weight_two,
         ],
-        pieces_two,
-        [shape_of(OWN, MODEL, dtype=F32), shape_of(HALF_SOURCE, MODEL, dtype=F32), shape_of(HALF_SOURCE, MODEL)]
-        + [shape_of(256, 1024)] * 4 + [shape_of(8, MODEL, dtype=F32)],
+        [],
         [
-            vmem((SOURCES, MODEL), BF16), vmem((MODEL, 2560), BF16), vmem((OWN, MODEL), BF16), vmem((OWN, MODEL), F32),
-            vmem((SOURCES, 2 * MODEL), BF16), vmem((MODEL, 1024), BF16), vmem((MODEL, 1024), BF16),
-            vmem((SOURCES, TILE), F32), dma((4,)),
+            shape_of(OWN, MODEL), shape_of(HALF_SOURCE, MODEL, dtype=F32), shape_of(HALF_SOURCE, MODEL),
+            shape_of(MODEL, 1536),
         ],
-        8000000000, any_outs=(3, 4, 5, 6),
-    )
-    cross = scatter_pair(cross_sends[:2], cross_sends[2:])
+        [
+            vmem((OWN, MODEL), BF16), vmem((OWN, MODEL), F32), vmem((SOURCES, 2 * MODEL), BF16),
+            vmem((SOURCES, MODEL), BF16), vmem((SOURCES, TILE), F32),
+        ],
+        10000000000,
+    )
+    feed_came = tied(feed_came, asked)
+    feed_sent, feed_kept = add_halves(feed_kept, feed_came)
+    asked = tied(asked, feed_sent)
+    feed_came = exchange_side(feed_sent, 0)
+    self_grad, upstream, dot_rows, cross_kept, cross_sent, sums = call(
+        cross_weight_body, "cross_weights", place,
+        [after_self, lowered_two, mixed, after_grad, asked, vectors, sums, weight_two, some_grads], [],
+        [shape_of(OWN, MODEL, dtype=F32), shape_of(OWN, MODEL), shape_of(HEADS, OWN, dtype=F32)]
+        + [shape_of(256, 2560)] * 2 + [shape_of(8, MODEL, dtype=F32)],
+        [vmem((MODEL, 1024), BF16), dma((2,))],
+        6000000000, any_outs=(3, 4),
+    )
+    feed_came = tied(feed_came, upstream)
+    cross_kept, cross_sent, source_send = tied((cross_kept, cross_sent, source_send), feed_came)
+    feed = z_blocks(feed_kept + feed_came)
+    cross_sent, cross_kept = add_halves(cross_kept, exchange(cross_sent, FLIP_CORE))
     source_came = exchange(source_send, FLIP_Y)
+    cross_came = exchange_side(cross_sent, 1)
+    upstream = tied(upstream, feed[0], cross_sent)
+    part_back, *left_sends = call(
+        self_back_body, "self_backward", place,
+        [target_segments, lowered, queries, pair, logs, upstream, dot_rows, weight_one], [],
+        [shape_of(KEYS, MODEL, dtype=F32)] + [shape_of(256, 768)] * 2,
+        [
+            vmem((OWN, 256), F32), vmem((KEYS, 512), BF16), vmem((MODEL, 768), BF16), vmem((KEYS, TILE), F32), dma((1,)),
+        ],
+        8000000000, any_outs=(1, 2),
+    )
+    cross_came, feed, source_own, source_came = tied((cross_came, feed, source_own, source_came), part_back)
+    left_sends = tied(left_sends, cross_came, feed, source_came)
+    cross_sent, cross_kept = add_halves(cross_kept, cross_came)
+    left_sent, left_kept = add_halves(left_sends[0], exchange(left_sends[1], FLIP_CORE))
+    cross_came, left_came = exchange_side(cross_sent, 0), exchange_side(left_sent, 1)
+    part_back = tied(part_back, cross_sent, left_sent)
+    own_back, send_back, *right_sends = call(
+        self_last_body, "self_last", place,
+        [
+            target_segments, states, window, lowered, queries, pair, logs, upstream, dot_rows, weight_one, part_back,
+            sums, bias_sums,
+        ],
+        [],
+        [shape_of(OWN, MODEL, dtype=F32), shape_of(WINDOW, MODEL)] + [shape_of(256, 896)] * 2,
+        [
+            vmem((OWN, 256), F32), vmem((KEYS, 512), BF16), vmem((MODEL, 896), BF16), vmem((KEYS, TILE), F32), dma((1,)),
+        ],
+        8000000000, any_outs=(2, 3),
+    )
+    cross_came, left_came, source_own = tied((cross_came, left_came, source_own), own_back)
+    right_sends, send_back = tied((right_sends, send_back), cross_came, left_came)
+    right_sent, right_kept = add_halves(right_sends[0], exchange(right_sends[1], FLIP_CORE))
+    cross_kept, left_kept = tied((cross_kept, left_kept), right_sent)
+    right_came, came = exchange_side(right_sent, 1), exchange(send_back, FLIP_Y)
+    left_sent, left_kept = add_halves(left_kept, left_came)
+    left_came = exchange_side(left_sent, 0)
+    cross = z_blocks(cross_kept + cross_came)
+    right_sent, right_kept = add_halves(right_kept, right_came)
+    right_came = exchange_side(right_sent, 0)
+    came, source_own = tied((came, source_own), right_sent)
     grad_source = source_own[:half] + source_came[:half].astype(F32)
-    own_back, send_back, *last_sends = call(
-        self_back_body, "self_backward", place,
-        [target_segments, states, window, lowered, queries, pair, mixed, logs, self_grad, vectors, sums, bias_sums],
-        pieces_one + pieces_two[:4],
-        [shape_of(OWN, MODEL, dtype=F32), shape_of(WINDOW, MODEL)] + [shape_of(256, 1024)] * 2
-        + [shape_of(256, 1152)] * 2,
-        [
-            vmem((MODEL, 1536), BF16), vmem((MODEL, MODEL), BF16), vmem((OWN, MODEL), BF16), vmem((OWN, MODEL), F32),
-            vmem((KEYS, 2 * MODEL), BF16), vmem((MODEL, 1024), BF16), vmem((MODEL, 1152), BF16),
-            vmem((KEYS, TILE), F32), dma((5,)),
-        ],
-        12000000000, any_outs=(2, 3, 4, 5),
-    )
-    last = scatter_pair(last_sends[:2], last_sends[2:])
     (grad_target,) = call(
-        target_body, "target_grad", place, [own_back, exchange(send_back, FLIP_Y), states, self_grad, vectors], [],
+        target_body, "target_grad", place, [own_back, came, states, self_grad, vectors], [],
         [shape_of(OWN, MODEL, dtype=F32)], [], 1000000,
     )
-    *grads, small = call(
+    last = z_blocks(jnp.concatenate([left_kept + left_came, right_kept + right_came], 1))
+    project, output, query, keyval, crossout, up, down, *small = call(
         finish_body, "finish", place, feed + cross + last, [],
         [
             shape_of(16, 1536, dtype=F32), shape_of(16, 512, dtype=F32), shape_of(16, 512, dtype=F32),
             shape_of(16, 1024, dtype=F32), shape_of(16, 512, dtype=F32), shape_of(16, 2048, dtype=F32),
-            shape_of(64, 512, dtype=F32), shape_of(8, TILE, dtype=F32),
-        ],
+            shape_of(64, 512, dtype=F32),
+        ]
+        + [shape_of(1, 16, dtype=F32)] * 7 + [shape_of(1, 64, dtype=F32)],
         [], 1000000,
     )
-    project, output, query, keyval, crossout, up, down = grads
-    rows = [small[i, :16] for i in range(7)]
+    *rows, up_sum = [row[0] for row in small]
     return (
         layer_out[None], grad_target[None], grad_source[None], project, output, query, keyval, crossout, up,
-        small[7, :64], down, *rows,
+        up_sum, down, *rows,
     )
 
 

time: 289 us -> 202 us (0.70)
  waiting for transfers between devices: 103 us -> 47.2 us
  local copies, waits for them, and re-layouts: 20.9 us -> 2.84 us
  starting transfers between devices: 65.1 us -> 50.1 us
    ppermute x64 -> x32, waiting for transfers between devices: 103 us -> 19.4 us  [exchange(): lax.ppermute(value, AXES, [(device, device ^ flip) for device in range(32)])]
    ppermute x64 -> x32, starting transfers between devices: 65.1 us -> 35 us  [exchange(): lax.ppermute(value, AXES, [(device, device ^ flip) for device in range(32)])]
    ppermute x0 -> x14, waiting for transfers between devices: none -> 27.8 us  [exchange_side(): lax.ppermute(value, AXES, [(device, device ^ flips[device >> 1 & 1]) for...]
    ppermute x0 -> x14, starting transfers between devices: none -> 15.1 us  [exchange_side(): lax.ppermute(value, AXES, [(device, device ^ flips[device >> 1 & 1]) for...]
    unnamed x53 -> x42, local copies, waits for them, and re-layouts: 13.3 us -> 2.04 us
    concatenate x4 -> x5, local copies, waits for them, and re-layouts: 5.47 us -> 0.1 us  [join(): return jnp.concatenate(parts, 0)]
    pallas_call x8 -> x12, Pallas kernels: 95.4 us -> 96 us  [call(): pl.pallas_call(body, name=name, out_shape=outs, in_specs=[SMEM_SPEC] + [H...]
  transfers between devices with their start and end apart: 64 -> 46, of which waited for: 26 -> 20; matrix products, arithmetic and copies ran while one was open for 1% -> 2% of each run, Pallas kernels for 11% -> 36%
where the time goes in v3:
time: 202 us
  Pallas kernels  96 us (48%)
  starting transfers between devices  50.1 us (25%)
  waiting for transfers between devices  47.2 us (23%)
  other arithmetic  4.02 us (2%)
  local copies, waits for them, and re-layouts  2.84 us (1%)
    pallas_call x12, Pallas kernels, call(): pl.pallas_call(body, name=name, out_shape=outs, in_specs=[SMEM_SPEC] + [H...  96 us
    ppermute x32, starting transfers between devices, exchange(): lax.ppermute(value, AXES, [(device, device ^ flip) for device in range(32)])  35 us
    ppermute x14, waiting for transfers between devices, exchange_side(): lax.ppermute(value, AXES, [(device, device ^ flips[device >> 1 & 1]) for...  27.8 us
    ppermute x32, waiting for transfers between devices, exchange(): lax.ppermute(value, AXES, [(device, device ^ flip) for device in range(32)])  19.4 us
    ppermute x14, starting transfers between devices, exchange_side(): lax.ppermute(value, AXES, [(device, device ^ flips[device >> 1 & 1]) for...  15.1 us
  transfers between devices with their start and end apart: 46, of which 20 were waited for; matrix products, arithmetic and copies ran while one was open for 2% of the time, Pallas kernels for 36%

profile of v3, /device:TPU:0, one launch (start us, length us, event | category | flops | bytes accessed | tf_op | source)
XLA Modules:
  0.0 201.5 jit_solution(15374701497382070515)
XLA Ops:
  0.7 0.9 pad_add_fusion.2
  2.7 3.1 %pack.1 = (bf16[16,1664]{1,0:T(8,128)(2,1)}, bf16[16,2560]{1,0:T(8,128)(2,1)}, bf16[16,4096]{1,0:T(8,128)(2,1)}, bf16[256,512]{1,0:T(8,128)(2,1)}, bf16[192,512]{1,0:T(8,128)(2,1)}) custom-call(s32[2]{0:T(128)} %pad_add_fusion.1.place, bf16[1,256]{1,0:T(2,128)(2,1)} %reshape.39.vectors, bf16[16,1536]{1,0:T(8,128)(2,1)} %project.1, bf16[16,512]{1,0:T(8,128)(2,1)} %output.1, ...), custom_call_target="tpu_custom_call" | custom-call | flops 1000000 | bytes 4194304 | tf_op jit(solution)/shard_map/pack/pallas_call | solution.py:931
  5.8 5.1 %collective-permute-start.3 = (bf16[16,1664]{1,0:T(8,128)(2,1)}, bf16[16,1664]{1,0:T(8,128)(2,1)S(1)}, u32[]{:S(2)}, u32[]{:S(2)}) collective-permute-start(bf16[16,1664]{1,0:T(8,128)(2,1)} %get-tuple-element.129), channel_id=1, source_target_pairs={{0,24},{1,25},{2,26},{3,27},{4,28},{5,29},{6,30},{7,31},{8,16},{9,... | collective-permute-start | bytes 159752 | tf_op jit(solution)/shard_map/ppermute | solution.py:377
  10.9 0.6 collective-permute-start.1
  11.6 1.7 collective-permute-start
  13.2 0.8 constant_dynamic-update-slice_fusion.4
  14.0 2.1 %collective-permute-done.2 = bf16[16,1664]{1,0:T(8,128)(2,1)S(1)} collective-permute-done((bf16[16,1664]{1,0:T(8,128)(2,1)}, bf16[16,1664]{1,0:T(8,128)(2,1)S(1)}, u32[]{:S(2)}, u32[]{:S(2)}) %collective-permute-start.2) | collective-permute-done | bytes 53280 | tf_op jit(solution)/shard_map/ppermute | solution.py:377
  16.2 0.8 pad_maximum_fusion
  17.0 1.6 collective-permute-start.4
  18.6 1.2 collective-permute-done.window
  19.8 3.1 %collective-permute-done.4 = bf16[64,1664]{1,0:T(8,128)(2,1)S(1)} collective-permute-done((bf16[64,1664]{1,0:T(8,128)(2,1)S(1)}, bf16[64,1664]{1,0:T(8,128)(2,1)S(1)}, u32[]{:S(2)}, u32[]{:S(2)}) %collective-permute-start.4) | collective-permute-done | bytes 213024 | tf_op jit(solution)/shard_map/ppermute | solution.py:382
  22.9 1.6 collective-permute-start.8
  24.5 2.4 %collective-permute-start.7 = (bf16[16,2560]{1,0:T(8,128)(2,1)}, bf16[16,2560]{1,0:T(8,128)(2,1)S(1)}, u32[]{:S(2)}, u32[]{:S(2)}) collective-permute-start(bf16[16,2560]{1,0:T(8,128)(2,1)} %get-tuple-element.130), channel_id=1, source_target_pairs={{0,24},{1,25},{2,26},{3,27},{4,28},{5,29},{6,30},{7,31},{8,16},{9,... | collective-permute-start | bytes 245768 | tf_op jit(solution)/shard_map/ppermute | solution.py:377
  26.9 2.0 %collective-permute-start.5 = (bf16[16,2560]{1,0:T(8,128)(2,1)}, bf16[16,2560]{1,0:T(8,128)(2,1)S(1)}, u32[]{:S(2)}, u32[]{:S(2)}) collective-permute-start(bf16[16,2560]{1,0:T(8,128)(2,1)} %get-tuple-element.130), channel_id=1, source_target_pairs={{0,8},{1,9},{2,10},{3,11},{4,12},{5,13},{6,14},{7,15},{8,0},{9,1},... | collective-permute-start | bytes 245768 | tf_op jit(solution)/shard_map/ppermute | solution.py:377
  28.9 0.9 constant_dynamic-update-slice_fusion.8
  29.8 1.2 collective-permute-done.7
  31.0 2.9 %collective-permute-done.6 = bf16[16,2560]{1,0:T(8,128)(2,1)S(1)} collective-permute-done((bf16[16,2560]{1,0:T(8,128)(2,1)}, bf16[16,2560]{1,0:T(8,128)(2,1)S(1)}, u32[]{:S(2)}, u32[]{:S(2)}) %collective-permute-start.6) | collective-permute-done | bytes 81952 | tf_op jit(solution)/shard_map/ppermute | solution.py:377
  34.0 1.2 collective-permute-start.9
  35.7 3.8 %self_lower.1 = (bf16[512,512]{1,0:T(8,128)(2,1)S(1)}, bf16[768,1024]{1,0:T(8,128)(2,1)S(1)}, bf16[768,512]{1,0:T(8,128)(2,1)S(1)}, f32[8,512]{1,0:T(8,128)S(1)}...) custom-call(s32[2]{0:T(128)S(1)} %copy-done.1, bf16[512,512]{1,0:T(8,128)(2,1)S(1)} %bitcast.18, ...), custom_call_target="tpu_custom_call" | custom-call | flops 3000000000 | bytes 4194304 | tf_op jit(solution)/shard_map/self_lower/pallas_call | solution.py:931
  39.6 1.6 collective-permute-done.9
  41.2 2.5 %collective-permute-start.16 = (bf16[16,4096]{1,0:T(8,128)(2,1)S(1)}, bf16[16,4096]{1,0:T(8,128)(2,1)S(1)}, u32[]{:S(2)}, u32[]{:S(2)}) collective-permute-start(bf16[16,4096]{1,0:T(8,128)(2,1)S(1)} %copy-done.13), channel_id=1, source_target_pairs={{0,24},{1,25},{2,26},{3,27},{4,28},{5,29},{6,30},{7,31},{8,16},{9,... | collective-permute-start | bytes 393224 | tf_op jit(solution)/shard_map/ppermute | solution.py:377
  43.7 1.9 collective-permute-start.14
  45.7 1.4 collective-permute-start.12
  47.1 2.3 %collective-permute-done.16 = bf16[16,4096]{1,0:T(8,128)(2,1)S(1)} collective-permute-done((bf16[16,4096]{1,0:T(8,128)(2,1)S(1)}, bf16[16,4096]{1,0:T(8,128)(2,1)S(1)}, u32[]{:S(2)}, u32[]{:S(2)}) %collective-permute-start.16) | collective-permute-done | bytes 131104 | tf_op jit(solution)/shard_map/ppermute | solution.py:377
  49.4 1.4 collective-permute-start.17
  50.8 11.6 %self_mix.1 = (bf16[512,512]{1,0:T(8,128)(2,1)S(1)}, f32[8,512]{1,0:T(8,128)S(1)}) custom-call(s32[2]{0:T(128)S(1)} %copy-done.1, s32[1,1024]{1,0:T(1,128)S(1)} %copy-done.4, bf16[512,512]{1,0:T(8,128)(2,1)S(1)} %get-tuple-element.137.queries, bf16[768,1024]{1,0:T(8,128)(2,1)S(1)} %get-tuple-element.142.pair), custom_call_target="tpu_custom_call" | custom-call | flops 8000000000 | bytes 4194304 | tf_op jit(solution)/shard_map/self_mix/pallas_call | solution.py:931
  62.6 0.7 collective-permute-start.19
  63.3 1.3 collective-permute-done.18.refs_3_
  64.7 6.1 %cross_lower.1 = (f32[512,512]{1,0:T(8,128)S(1)}, bf16[512,512]{1,0:T(8,128)(2,1)S(1)}, bf16[512,512]{1,0:T(8,128)(2,1)S(1)}, bf16[384,1024]{1,0:T(8,128)(2,1)S(1)}, bf16[512,2560]{1,0:T(8,128)(2,1)S(1)}) custom-call(s32[2]{0:T(128)S(1)} %copy-done.1, bf16[512,512]{1,0:T(8,128)(2,1)S(1)} %bitcast.19, bf16[192,512]{1,0:T(8,128)(2,1)S(1)} %copy-done.3, ...), custom_call_target="tpu_custom_call" | custom-call | flops 3000000000 | bytes 4194304 | tf_op jit(solution)/shard_map/cross_lower/pallas_call | solution.py:931
  70.8 1.0 collective-permute-done.19
  72.0 0.7 collective-permute-start.21
  72.9 10.1 %cross_mix.1 = (bf16[512,512]{1,0:T(8,128)(2,1)S(1)}, f32[8,512]{1,0:T(8,128)S(1)}, f32[512,512]{1,0:T(8,128)S(1)}) custom-call(s32[2]{0:T(128)S(1)} %copy-done.1, s32[1,1024]{1,0:T(1,128)S(1)} %copy-done.4, s32[1,384]{1,0:T(1,128)S(1)} %pad_add_fusion.source_segments, bf16[512,512]{1,0:T(8,128)(2,1)S(1)} %get-tuple-element.148.queries, ...), custom_call_target="tpu_custom_call" | custom-call | flops 8000000000 | bytes 4194304 | tf_op jit(solution)/shard_map/cross_mix/pallas_call | solution.py:931
  82.9 3.9 %collective-permute-done.21.refs_1_ = bf16[128,4096]{1,0:T(8,128)(2,1)S(1)} collective-permute-done((bf16[128,4096]{1,0:T(8,128)(2,1)S(1)}, bf16[128,4096]{1,0:T(8,128)(2,1)S(1)}, u32[]{:S(2)}, u32[]{:S(2)}) %collective-permute-start.21) | collective-permute-done | bytes 1048608 | tf_op jit(solution)/shard_map/ppermute | solution.py:382
  86.8 2.7 %collective-permute-done.22.refs_3_ = bf16[128,4096]{1,0:T(8,128)(2,1)S(1)} collective-permute-done((bf16[128,4096]{1,0:T(8,128)(2,1)S(1)}, bf16[128,4096]{1,0:T(8,128)(2,1)S(1)}, u32[]{:S(2)}, u32[]{:S(2)}) %collective-permute-start.22) | collective-permute-done | bytes 1048608 | tf_op jit(solution)/shard_map/ppermute | solution.py:377
  89.5 19.0 %feed.1 = (bf16[512,512]{1,0:T(8,128)(2,1)}, f32[512,512]{1,0:T(8,128)S(1)}, bf16[256,4096]{1,0:T(8,128)(2,1)S(1)}, bf16[256,4096]{1,0:T(8,128)(2,1)S(1)}, f32[8,512]{1,0:T(8,128)S(1)}, /*index=5*/f32[1,2048]{1,0:T(1,128)S(1)}) custom-call(s32[2]{0:T(128)S(1)} %copy-done.1, f32[512,512]{1,0:T(8,128)S(1)} %get-tuple-element.152.after_cross, ...), custom_call_target="tpu_custom_call" | custom-call | flops 10000000000 | bytes 4194304 | tf_op jit(solution)/shard_map/feed/pallas_call | solution.py:931
  108.7 4.0 %collective-permute-done.23 = bf16[256,4096]{1,0:T(8,128)(2,1)S(1)} collective-permute-done((bf16[256,4096]{1,0:T(8,128)(2,1)S(1)}, bf16[256,4096]{1,0:T(8,128)(2,1)S(1)}, u32[]{:S(2)}, u32[]{:S(2)}) %collective-permute-start.23) | collective-permute-done | bytes 2097184 | tf_op jit(solution)/shard_map/ppermute | solution.py:377
  112.9 0.7 collective-permute-start.24
  113.8 10.3 %cross_backward.1 = (bf16[512,512]{1,0:T(8,128)(2,1)S(1)}, f32[192,512]{1,0:T(8,128)S(1)}, bf16[192,512]{1,0:T(8,128)(2,1)S(1)}, bf16[512,1536]{1,0:T(8,128)(2,1)S(1)}) custom-call(s32[2]{0:T(128)S(1)} %copy-done.1, s32[1,1024]{1,0:T(1,128)S(1)} %copy-done.4, s32[1,384]{1,0:T(1,128)S(1)} %pad_add_fusion.source_segments, bf16[192,512]{1,0:T(8,128)(2,1)S(1)} %copy-done.3, ...), custom_call_target="tpu_custom_call" | custom-call | flops 10000000000 | bytes 4194304 | tf_op jit(solution)/shard_map/cross_backward/pallas_call | solution.py:931
  124.1 3.7 %collective-permute-done.24 = bf16[128,4096]{1,0:T(8,128)(2,1)S(1)} collective-permute-done((bf16[128,4096]{1,0:T(8,128)(2,1)S(1)}, bf16[128,4096]{1,0:T(8,128)(2,1)S(1)}, u32[]{:S(2)}, u32[]{:S(2)}) %collective-permute-start.24) | collective-permute-done | bytes 1048608 | tf_op jit(solution)/shard_map/ppermute | solution.py:382
  127.9 0.7 collective-permute-start.25
  128.6 5.5 %cross_weights.1 = (f32[512,512]{1,0:T(8,128)S(1)}, bf16[512,512]{1,0:T(8,128)(2,1)S(1)}, f32[8,512]{1,0:T(8,128)S(1)}, bf16[256,2560]{1,0:T(8,128)(2,1)S(1)}, b...) custom-call(s32[2]{0:T(128)S(1)} %copy-done.1, f32[512,512]{1,0:T(8,128)S(1)} %get-tuple-element.150.after_self, ...), custom_call_target="tpu_custom_call" | custom-call | flops 6000000000 | bytes 4194304 | tf_op jit(solution)/shard_map/cross_weights/pallas_call | solution.py:931
  134.0 3.1 %collective-permute-done.25 = bf16[64,4096]{1,0:T(8,128)(2,1)S(1)} collective-permute-done((bf16[64,4096]{1,0:T(8,128)(2,1)S(1)}, bf16[64,4096]{1,0:T(8,128)(2,1)S(1)}, u32[]{:S(2)}, u32[]{:S(2)}) %collective-permute-start.25) | collective-permute-done | bytes 524320 | tf_op jit(solution)/shard_map/ppermute | solution.py:382
  137.3 2.7 %collective-permute-start.30 = (bf16[16,4096]{1,0:T(8,128)(2,1)S(1)}, bf16[16,4096]{1,0:T(8,128)(2,1)S(1)}, u32[]{:S(2)}, u32[]{:S(2)}) collective-permute-start(bf16[16,4096]{1,0:T(8,128)(2,1)S(1)} %get-tuple-element.244), channel_id=1, source_target_pairs={{0,24},{1,25},{2,26},{3,27},{4,28},{5,29},{6,30},{7,31},{8,16},{9,... | collective-permute-start | bytes 393224 | tf_op jit(solution)/shard_map/ppermute | solution.py:377
  140.0 3.2 %collective-permute-start.29 = (bf16[16,4096]{1,0:T(8,128)(2,1)S(1)}, bf16[16,4096]{1,0:T(8,128)(2,1)S(1)}, u32[]{:S(2)}, u32[]{:S(2)}) collective-permute-start(bf16[16,4096]{1,0:T(8,128)(2,1)S(1)} %get-tuple-element.245), channel_id=1, source_target_pairs={{0,16},{1,17},{2,18},{3,19},{4,20},{5,21},{6,22},{7,23},{8,24},{9,... | collective-permute-start | bytes 393224 | tf_op jit(solution)/shard_map/ppermute | solution.py:377
  143.6 1.8 collective-permute-start.27
  145.4 11.3 %self_backward.1 = (f32[768,512]{1,0:T(8,128)S(1)}, bf16[256,768]{1,0:T(8,128)(2,1)S(1)}, bf16[256,768]{1,0:T(8,128)(2,1)S(1)}) custom-call(s32[2]{0:T(128)S(1)} %copy-done.1, s32[1,1024]{1,0:T(1,128)S(1)} %copy-done.4, bf16[768,512]{1,0:T(8,128)(2,1)S(1)} %copy-done.8, bf16[512,512]{1,0:T(8,128)(2,1)S(1)} %copy-done.10, ...), custom_call_target="tpu_custom_call" | custom-call | flops 8000000000 | bytes 4194304 | tf_op jit(solution)/shard_map/self_backward/pallas_call | solution.py:931
  157.5 1.1 collective-permute-done.32
  159.1 11.5 %self_last.1 = (f32[512,512]{1,0:T(8,128)S(1)}, bf16[256,512]{1,0:T(8,128)(2,1)S(1)}, bf16[256,896]{1,0:T(8,128)(2,1)S(1)}, bf16[256,896]{1,0:T(8,128)(2,1)S(1)}) custom-call(s32[2]{0:T(128)S(1)} %copy-done.1, s32[1,1024]{1,0:T(1,128)S(1)} %copy-done.4, bf16[512,512]{1,0:T(8,128)(2,1)S(1)} %bitcast.20, bf16[256,512]{1,0:T(8,128)(2,1)S(1)} %collective-permute-done.window, ...), custom_call_target="tpu_custom_call" | custom-call | flops 8000000000 | bytes 4194304 | tf_op jit(solution)/shard_map/self_last/pallas_call | solution.py:931
  170.7 1.8 collective-permute-start.35
  172.5 1.8 collective-permute-start.37
  174.5 1.5 collective-permute-start.40
  176.0 1.9 collective-permute-start.39
  177.9 1.0 collective-permute-start.38
  178.9 4.0 %collective-permute-done.37 = bf16[128,896]{1,0:T(8,128)(2,1)S(1)} collective-permute-done((bf16[128,896]{1,0:T(8,128)(2,1)S(1)}, bf16[128,896]{1,0:T(8,128)(2,1)S(1)}, u32[]{:S(2)}, u32[]{:S(2)}) %collective-permute-start.37) | collective-permute-done | bytes 229408 | tf_op jit(solution)/shard_map/ppermute | solution.py:382
  182.9 1.0 collective-permute-start.41
  184.0 3.6 %collective-permute-done.41 = bf16[64,768]{1,0:T(8,128)(2,1)S(1)} collective-permute-done((bf16[64,768]{1,0:T(8,128)(2,1)S(1)}, bf16[64,768]{1,0:T(8,128)(2,1)S(1)}, u32[]{:S(2)}, u32[]{:S(2)}) %collective-permute-start.41) | collective-permute-done | bytes 98336 | tf_op jit(solution)/shard_map/ppermute | solution.py:382
  187.5 1.0 collective-permute-start.42
  188.6 3.7 %collective-permute-done.42 = bf16[64,896]{1,0:T(8,128)(2,1)S(1)} collective-permute-done((bf16[64,896]{1,0:T(8,128)(2,1)S(1)}, bf16[64,896]{1,0:T(8,128)(2,1)S(1)}, u32[]{:S(2)}, u32[]{:S(2)}) %collective-permute-start.42) | collective-permute-done | bytes 114720 | tf_op jit(solution)/shard_map/ppermute | solution.py:382
  192.4 1.5 collective-permute-start.45
  193.9 0.8 collective-permute-start.43
  194.7 2.2 %collective-permute-start.44 = (bf16[16,1664]{1,0:T(8,128)(2,1)S(1)}, bf16[16,1664]{1,0:T(8,128)(2,1)S(1)}, u32[]{:S(2)}, u32[]{:S(2)}) collective-permute-start(bf16[16,1664]{1,0:T(8,128)(2,1)S(1)} %get-tuple-element.255), channel_id=1, source_target_pairs={{0,16},{1,17},{2,18},{3,19},{4,20},{5,21},{6,22},{7,23},{8,24},{9,... | collective-permute-start | bytes 159752 | tf_op jit(solution)/shard_map/ppermute | solution.py:377
  196.8 0.8 add_bitcast_fusion
  197.6 2.3 %target_grad.1 = f32[512,512]{1,0:T(8,128)} custom-call(s32[2]{0:T(128)S(1)} %copy-done.1, f32[512,512]{1,0:T(8,128)S(1)} %get-tuple-element.203.back, bf16[256,512]{1,0:T(8,128)(2,1)S(1)} %collective-permute-done.35.came, bf16[512,512]{1,0:T(8,128)(2,1)S(1)} %bitcast.21, f32[512,512]{1,0:T(8,128)S(1)} %get-tuple-element.215.self_grad, ...), custom_call_target="tpu_custom_call" | custom-call | flops 1000000 | bytes 4194304 | tf_op jit(solution)/shard_map/target_grad/pallas_call | solution.py:931
  199.9 1.4 finish.1
  (110 shorter events, 5.1 us)
Async XLA Ops:
  0.7 35.0 %copy-start = (bf16[1,512,512]{2,1,0:T(8,128)(2,1)S(1)}, bf16[1,512,512]{2,1,0:T(8,128)(2,1)}, u32[]{:S(2)}) copy-start(bf16[1,512,512]{2,1,0:T(8,128)(2,1)} %param.20) | copy-start | bytes 1572868
  2.7 33.0 %copy-start.1 = (s32[2]{0:T(128)S(1)}, s32[2]{0:T(128)}, u32[]{:S(2)}) copy-start(s32[2]{0:T(128)} %pad_add_fusion.1.place) | copy-start | bytes 28
  5.8 8.2 %collective-permute-start.3 = (bf16[16,1664]{1,0:T(8,128)(2,1)}, bf16[16,1664]{1,0:T(8,128)(2,1)S(1)}, u32[]{:S(2)}, u32[]{:S(2)}) collective-permute-start(bf16[16,1664]{1,0:T(8,128)(2,1)} %get-tuple-element.129), channel_id=1, source_target_pairs={{0,24},{1,25},{2,26},{3,27},{4,28},{5,29},{6,30},{7,31},{8,16},{9,... | collective-permute-start | bytes 159752 | tf_op jit(solution)/shard_map/ppermute | solution.py:377
  10.9 5.2 %collective-permute-start.2 = (bf16[16,1664]{1,0:T(8,128)(2,1)}, bf16[16,1664]{1,0:T(8,128)(2,1)S(1)}, u32[]{:S(2)}, u32[]{:S(2)}) collective-permute-start(bf16[16,1664]{1,0:T(8,128)(2,1)} %get-tuple-element.129), channel_id=1, source_target_pairs={{0,16},{1,17},{2,18},{3,19},{4,20},{5,21},{6,22},{7,23},{8,24},{9,... | collective-permute-start | bytes 159752 | tf_op jit(solution)/shard_map/ppermute | solution.py:377
  10.9 5.2 %collective-permute-start.1 = (bf16[16,1664]{1,0:T(8,128)(2,1)}, bf16[16,1664]{1,0:T(8,128)(2,1)S(1)}, u32[]{:S(2)}, u32[]{:S(2)}) collective-permute-start(bf16[16,1664]{1,0:T(8,128)(2,1)} %get-tuple-element.129), channel_id=1, source_target_pairs={{0,8},{1,9},{2,10},{3,11},{4,12},{5,13},{6,14},{7,15},{8,0},{9,1},... | collective-permute-start | bytes 159752 | tf_op jit(solution)/shard_map/ppermute | solution.py:377
  11.6 8.2 %collective-permute-start = (bf16[256,512]{1,0:T(8,128)(2,1)}, bf16[256,512]{1,0:T(8,128)(2,1)S(1)}, u32[]{:S(2)}, u32[]{:S(2)}) collective-permute-start(bf16[256,512]{1,0:T(8,128)(2,1)} %get-tuple-element.128), channel_id=1, source_target_pairs={{0,1},{1,0},{2,3},{3,2},{4,5},{5,4},{6,7},{7,6},{8,9},{9,8},{10,11... | collective-permute-start | bytes 786440 | tf_op jit(solution)/shard_map/ppermute | solution.py:377
  17.0 5.9 %collective-permute-start.4 = (bf16[64,1664]{1,0:T(8,128)(2,1)S(1)}, bf16[64,1664]{1,0:T(8,128)(2,1)S(1)}, u32[]{:S(2)}, u32[]{:S(2)}) collective-permute-start(bf16[64,1664]{1,0:T(8,128)(2,1)S(1)} %pad_maximum_fusion), channel_id=1, source_target_pairs={{0,4},{1,5},{2,3},{3,2},{4,0},{5,1},{6,7},{7,6},{8,12},{9,13},{10,... | collective-permute-start | bytes 638984 | tf_op jit(solution)/shard_map/ppermute | solution.py:382
  22.9 10.9 %collective-permute-start.8 = (bf16[128,1664]{1,0:T(8,128)(2,1)S(1)}, bf16[128,1664]{1,0:T(8,128)(2,1)S(1)}, u32[]{:S(2)}, u32[]{:S(2)}) collective-permute-start(bf16[128,1664]{1,0:T(8,128)(2,1)S(1)} %constant_dynamic-update-slice_fusion.refs_0_), channel_id=1, source_target_pairs={{0,1},{1,0},{2,6},{3,7},{4,5},{5,4},{6,2},{7,3},{8,9},{9,8},{10,14... | collective-permute-start | bytes 1277960 | tf_op jit(solution)/shard_map/ppermute | solution.py:382
  24.5 6.5 %collective-permute-start.7 = (bf16[16,2560]{1,0:T(8,128)(2,1)}, bf16[16,2560]{1,0:T(8,128)(2,1)S(1)}, u32[]{:S(2)}, u32[]{:S(2)}) collective-permute-start(bf16[16,2560]{1,0:T(8,128)(2,1)} %get-tuple-element.130), channel_id=1, source_target_pairs={{0,24},{1,25},{2,26},{3,27},{4,28},{5,29},{6,30},{7,31},{8,16},{9,... | collective-permute-start | bytes 245768 | tf_op jit(solution)/shard_map/ppermute | solution.py:377
  26.9 7.0 %collective-permute-start.6 = (bf16[16,2560]{1,0:T(8,128)(2,1)}, bf16[16,2560]{1,0:T(8,128)(2,1)S(1)}, u32[]{:S(2)}, u32[]{:S(2)}) collective-permute-start(bf16[16,2560]{1,0:T(8,128)(2,1)} %get-tuple-element.130), channel_id=1, source_target_pairs={{0,16},{1,17},{2,18},{3,19},{4,20},{5,21},{6,22},{7,23},{8,24},{9,... | collective-permute-start | bytes 245768 | tf_op jit(solution)/shard_map/ppermute | solution.py:377
  26.9 7.0 %collective-permute-start.5 = (bf16[16,2560]{1,0:T(8,128)(2,1)}, bf16[16,2560]{1,0:T(8,128)(2,1)S(1)}, u32[]{:S(2)}, u32[]{:S(2)}) collective-permute-start(bf16[16,2560]{1,0:T(8,128)(2,1)} %get-tuple-element.130), channel_id=1, source_target_pairs={{0,8},{1,9},{2,10},{3,11},{4,12},{5,13},{6,14},{7,15},{8,0},{9,1},... | collective-permute-start | bytes 245768 | tf_op jit(solution)/shard_map/ppermute | solution.py:377
  29.8 5.3 %collective-permute-start.10 = (bf16[128,1664]{1,0:T(8,128)(2,1)S(1)}, bf16[128,1664]{1,0:T(8,128)(2,1)S(1)}, u32[]{:S(2)}, u32[]{:S(2)}) collective-permute-start(bf16[128,1664]{1,0:T(8,128)(2,1)S(1)} %constant_dynamic-update-slice_fusion.refs_0_), channel_id=1, source_target_pairs={{0,2},{1,3},{2,0},{3,1},{4,6},{5,7},{6,4},{7,5},{8,10},{9,11},{10,... | collective-permute-start | bytes 1277960 | tf_op jit(solution)/shard_map/ppermute | solution.py:377
  33.9 1.8 collective-permute-start.11
  34.0 7.2 %copy-start.13 = (bf16[16,4096]{1,0:T(8,128)(2,1)S(1)}, bf16[16,4096]{1,0:T(8,128)(2,1)}, u32[]{:S(2)}) copy-start(bf16[16,4096]{1,0:T(8,128)(2,1)} %get-tuple-element.154) | copy-start | bytes 393220
  34.0 15.4 %copy-start.3 = (bf16[192,512]{1,0:T(8,128)(2,1)S(1)}, bf16[192,512]{1,0:T(8,128)(2,1)}, u32[]{:S(2)}) copy-start(bf16[192,512]{1,0:T(8,128)(2,1)} %get-tuple-element.141.own_source) | copy-start | bytes 589828
  34.0 16.8 %copy-start.4 = (s32[1,1024]{1,0:T(1,128)S(1)}, s32[1,1024]{1,0:T(1,128)}, u32[]{:S(2)}) copy-start(s32[1,1024]{1,0:T(1,128)} %segments.9) | copy-start | bytes 12292
  34.0 7.1 %collective-permute-start.9 = (bf16[64,2560]{1,0:T(8,128)(2,1)S(1)}, bf16[64,2560]{1,0:T(8,128)(2,1)S(1)}, u32[]{:S(2)}, u32[]{:S(2)}) collective-permute-start(bf16[64,2560]{1,0:T(8,128)(2,1)S(1)} %constant_dynamic-update-slice_fusion.5), channel_id=1, source_target_pairs={{0,4},{1,5},{2,3},{3,2},{4,0},{5,1},{6,7},{7,6},{8,12},{9,13},{10,... | collective-permute-start | bytes 983048 | tf_op jit(solution)/shard_map/ppermute | solution.py:382
  39.5 22.9 %copy-start.7 = (bf16[768,512]{1,0:T(8,128)(2,1)}, bf16[768,512]{1,0:T(8,128)(2,1)S(1)}, u32[]{:S(2)}) copy-start(bf16[768,512]{1,0:T(8,128)(2,1)S(1)} %get-tuple-element.163.lowered) | copy-start | bytes 2359300
  39.6 22.9 %copy-start.9 = (bf16[512,512]{1,0:T(8,128)(2,1)}, bf16[512,512]{1,0:T(8,128)(2,1)S(1)}, u32[]{:S(2)}) copy-start(bf16[512,512]{1,0:T(8,128)(2,1)S(1)} %get-tuple-element.137.queries) | copy-start | bytes 1572868
  41.2 8.3 %collective-permute-start.16 = (bf16[16,4096]{1,0:T(8,128)(2,1)S(1)}, bf16[16,4096]{1,0:T(8,128)(2,1)S(1)}, u32[]{:S(2)}, u32[]{:S(2)}) collective-permute-start(bf16[16,4096]{1,0:T(8,128)(2,1)S(1)} %copy-done.13), channel_id=1, source_target_pairs={{0,24},{1,25},{2,26},{3,27},{4,28},{5,29},{6,30},{7,31},{8,16},{9,... | collective-permute-start | bytes 393224 | tf_op jit(solution)/shard_map/ppermute | solution.py:377
  43.6 18.8 %collective-permute-start.15 = (bf16[16,4096]{1,0:T(8,128)(2,1)S(1)}, bf16[16,4096]{1,0:T(8,128)(2,1)S(1)}, u32[]{:S(2)}, u32[]{:S(2)}) collective-permute-start(bf16[16,4096]{1,0:T(8,128)(2,1)S(1)} %copy-done.13), channel_id=1, source_target_pairs={{0,16},{1,17},{2,18},{3,19},{4,20},{5,21},{6,22},{7,23},{8,24},{9,... | collective-permute-start | bytes 393224 | tf_op jit(solution)/shard_map/ppermute | solution.py:377
  43.7 18.8 %collective-permute-start.14 = (bf16[16,4096]{1,0:T(8,128)(2,1)S(1)}, bf16[16,4096]{1,0:T(8,128)(2,1)S(1)}, u32[]{:S(2)}, u32[]{:S(2)}) collective-permute-start(bf16[16,4096]{1,0:T(8,128)(2,1)S(1)} %copy-done.13), channel_id=1, source_target_pairs={{0,8},{1,9},{2,10},{3,11},{4,12},{5,13},{6,14},{7,15},{8,0},{9,1},... | collective-permute-start | bytes 393224 | tf_op jit(solution)/shard_map/ppermute | solution.py:377
  45.6 16.9 %collective-permute-start.13 = (bf16[128,2560]{1,0:T(8,128)(2,1)S(1)}, bf16[128,2560]{1,0:T(8,128)(2,1)S(1)}, u32[]{:S(2)}, u32[]{:S(2)}) collective-permute-start(bf16[128,2560]{1,0:T(8,128)(2,1)S(1)} %constant_dynamic-update-slice_fusion.9.refs_0_), channel_id=1, source_target_pairs={{0,2},{1,3},{2,0},{3,1},{4,6},{5,7},{6,4},{7,5},{8,10},{9,11},{10,... | collective-permute-start | bytes 1966088 | tf_op jit(solution)/shard_map/ppermute | solution.py:377
  45.7 16.8 %collective-permute-start.12 = (bf16[128,2560]{1,0:T(8,128)(2,1)S(1)}, bf16[128,2560]{1,0:T(8,128)(2,1)S(1)}, u32[]{:S(2)}, u32[]{:S(2)}) collective-permute-start(bf16[128,2560]{1,0:T(8,128)(2,1)S(1)} %constant_dynamic-update-slice_fusion.9.refs_0_), channel_id=1, source_target_pairs={{0,1},{1,0},{2,6},{3,7},{4,5},{5,4},{6,2},{7,3},{8,9},{9,8},{10,14... | collective-permute-start | bytes 1966088 | tf_op jit(solution)/shard_map/ppermute | solution.py:382
  49.4 13.0 %collective-permute-start.17 = (bf16[192,512]{1,0:T(8,128)(2,1)S(1)}, bf16[192,512]{1,0:T(8,128)(2,1)S(1)}, u32[]{:S(2)}, u32[]{:S(2)}) collective-permute-start(bf16[192,512]{1,0:T(8,128)(2,1)S(1)} %copy-done.3), channel_id=1, source_target_pairs={{0,1},{1,0},{2,3},{3,2},{4,5},{5,4},{6,7},{7,6},{8,9},{9,8},{10,11... | collective-permute-start | bytes 589832 | tf_op jit(solution)/shard_map/ppermute | solution.py:377
  62.5 2.2 %collective-permute-start.18 = (bf16[128,2560]{1,0:T(8,128)(2,1)S(1)}, bf16[128,2560]{1,0:T(8,128)(2,1)S(1)}, u32[]{:S(2)}, u32[]{:S(2)}) collective-permute-start(bf16[128,2560]{1,0:T(8,128)(2,1)S(1)} %collective-permute-done.12.refs_1_), channel_id=1, source_target_pairs={{0,2},{1,3},{2,0},{3,1},{4,6},{5,7},{6,4},{7,5},{8,10},{9,11},{10,... | collective-permute-start | bytes 1966088 | tf_op jit(solution)/shard_map/ppermute | solution.py:377
  62.6 9.2 %collective-permute-start.19 = (bf16[64,4096]{1,0:T(8,128)(2,1)S(1)}, bf16[64,4096]{1,0:T(8,128)(2,1)S(1)}, u32[]{:S(2)}, u32[]{:S(2)}) collective-permute-start(bf16[64,4096]{1,0:T(8,128)(2,1)S(1)} %constant_dynamic-update-slice_fusion.11), channel_id=1, source_target_pairs={{0,4},{1,5},{2,3},{3,2},{4,0},{5,1},{6,7},{7,6},{8,12},{9,13},{10,... | collective-permute-start | bytes 1572872 | tf_op jit(solution)/shard_map/ppermute | solution.py:382
  70.8 12.1 %copy-start.5 = (bf16[512,512]{1,0:T(8,128)(2,1)}, bf16[512,512]{1,0:T(8,128)(2,1)S(1)}, u32[]{:S(2)}) copy-start(bf16[512,512]{1,0:T(8,128)(2,1)S(1)} %get-tuple-element.148.queries) | copy-start | bytes 1572868
  70.8 1.9 copy-start.14
  72.0 14.9 %collective-permute-start.21 = (bf16[128,4096]{1,0:T(8,128)(2,1)S(1)}, bf16[128,4096]{1,0:T(8,128)(2,1)S(1)}, u32[]{:S(2)}, u32[]{:S(2)}) collective-permute-start(bf16[128,4096]{1,0:T(8,128)(2,1)S(1)} %constant_dynamic-update-slice_fusion.15.refs_0_), channel_id=1, source_target_pairs={{0,1},{1,0},{2,6},{3,7},{4,5},{5,4},{6,2},{7,3},{8,9},{9,8},{10,14... | collective-permute-start | bytes 3145736 | tf_op jit(solution)/shard_map/ppermute | solution.py:382
  72.7 14.1 %collective-permute-start.20 = (bf16[128,4096]{1,0:T(8,128)(2,1)S(1)}, bf16[128,4096]{1,0:T(8,128)(2,1)S(1)}, u32[]{:S(2)}, u32[]{:S(2)}) collective-permute-start(bf16[128,4096]{1,0:T(8,128)(2,1)S(1)} %constant_dynamic-update-slice_fusion.15.refs_0_), channel_id=1, source_target_pairs={{0,2},{1,3},{2,0},{3,1},{4,6},{5,7},{6,4},{7,5},{8,10},{9,11},{10,... | collective-permute-start | bytes 3145736 | tf_op jit(solution)/shard_map/ppermute | solution.py:377
  72.9 16.6 %copy-start.2 = (bf16[1,512,512]{2,1,0:T(8,128)(2,1)S(1)}, bf16[1,512,512]{2,1,0:T(8,128)(2,1)}, u32[]{:S(2)}) copy-start(bf16[1,512,512]{2,1,0:T(8,128)(2,1)} %param.24) | copy-start | bytes 1572868
  86.8 2.7 %collective-permute-start.22 = (bf16[128,4096]{1,0:T(8,128)(2,1)S(1)}, bf16[128,4096]{1,0:T(8,128)(2,1)S(1)}, u32[]{:S(2)}, u32[]{:S(2)}) collective-permute-start(bf16[128,4096]{1,0:T(8,128)(2,1)S(1)} %collective-permute-done.21.refs_1_), channel_id=1, source_target_pairs={{0,2},{1,3},{2,0},{3,1},{4,6},{5,7},{6,4},{7,5},{8,10},{9,11},{10,... | collective-permute-start | bytes 3145736 | tf_op jit(solution)/shard_map/ppermute | solution.py:377
  108.5 5.2 %copy-start.11 = (f32[512,512]{1,0:T(8,128)}, f32[512,512]{1,0:T(8,128)S(1)}, u32[]{:S(2)}) copy-start(f32[512,512]{1,0:T(8,128)S(1)} %get-tuple-element.169.after_grad) | copy-start | bytes 3145732
  108.5 4.2 %collective-permute-start.23 = (bf16[256,4096]{1,0:T(8,128)(2,1)S(1)}, bf16[256,4096]{1,0:T(8,128)(2,1)S(1)}, u32[]{:S(2)}, u32[]{:S(2)}) collective-permute-start(bf16[256,4096]{1,0:T(8,128)(2,1)S(1)} %get-tuple-element.168), channel_id=1, source_target_pairs={{0,2},{1,3},{2,0},{3,1},{4,6},{5,7},{6,4},{7,5},{8,10},{9,11},{10,... | collective-permute-start | bytes 6291464 | tf_op jit(solution)/shard_map/ppermute | solution.py:377
  112.7 1.0 copy-start.6
  112.9 14.9 %collective-permute-start.24 = (bf16[128,4096]{1,0:T(8,128)(2,1)S(1)}, bf16[128,4096]{1,0:T(8,128)(2,1)S(1)}, u32[]{:S(2)}, u32[]{:S(2)}) collective-permute-start(bf16[128,4096]{1,0:T(8,128)(2,1)S(1)} %get-tuple-element.235), channel_id=1, source_target_pairs={{0,1},{1,0},{2,6},{3,7},{4,5},{5,4},{6,2},{7,3},{8,9},{9,8},{10,14... | collective-permute-start | bytes 3145736 | tf_op jit(solution)/shard_map/ppermute | solution.py:382
  124.1 4.4 %copy-start.12 = (f32[512,512]{1,0:T(8,128)S(1)}, f32[512,512]{1,0:T(8,128)}, u32[]{:S(2)}) copy-start(f32[512,512]{1,0:T(8,128)} %copy-done.11) | copy-start | bytes 3145732
  127.9 9.2 %collective-permute-start.25 = (bf16[64,4096]{1,0:T(8,128)(2,1)S(1)}, bf16[64,4096]{1,0:T(8,128)(2,1)S(1)}, u32[]{:S(2)}, u32[]{:S(2)}) collective-permute-start(bf16[64,4096]{1,0:T(8,128)(2,1)S(1)} %slice_add_fusion.5), channel_id=1, source_target_pairs={{0,4},{1,5},{2,3},{3,2},{4,0},{5,1},{6,7},{7,6},{8,12},{9,13},{10,... | collective-permute-start | bytes 1572872 | tf_op jit(solution)/shard_map/ppermute | solution.py:382
  137.1 6.4 %collective-permute-start.26 = (bf16[256,2560]{1,0:T(8,128)(2,1)S(1)}, bf16[256,2560]{1,0:T(8,128)(2,1)S(1)}, u32[]{:S(2)}, u32[]{:S(2)}) collective-permute-start(bf16[256,2560]{1,0:T(8,128)(2,1)S(1)} %get-tuple-element.183), channel_id=1, source_target_pairs={{0,2},{1,3},{2,0},{3,1},{4,6},{5,7},{6,4},{7,5},{8,10},{9,11},{10,... | collective-permute-start | bytes 3932168 | tf_op jit(solution)/shard_map/ppermute | solution.py:377
  137.3 19.5 %collective-permute-start.30 = (bf16[16,4096]{1,0:T(8,128)(2,1)S(1)}, bf16[16,4096]{1,0:T(8,128)(2,1)S(1)}, u32[]{:S(2)}, u32[]{:S(2)}) collective-permute-start(bf16[16,4096]{1,0:T(8,128)(2,1)S(1)} %get-tuple-element.244), channel_id=1, source_target_pairs={{0,24},{1,25},{2,26},{3,27},{4,28},{5,29},{6,30},{7,31},{8,16},{9,... | collective-permute-start | bytes 393224 | tf_op jit(solution)/shard_map/ppermute | solution.py:377
  140.0 16.8 %collective-permute-start.29 = (bf16[16,4096]{1,0:T(8,128)(2,1)S(1)}, bf16[16,4096]{1,0:T(8,128)(2,1)S(1)}, u32[]{:S(2)}, u32[]{:S(2)}) collective-permute-start(bf16[16,4096]{1,0:T(8,128)(2,1)S(1)} %get-tuple-element.245), channel_id=1, source_target_pairs={{0,16},{1,17},{2,18},{3,19},{4,20},{5,21},{6,22},{7,23},{8,24},{9,... | collective-permute-start | bytes 393224 | tf_op jit(solution)/shard_map/ppermute | solution.py:377
  143.2 2.2 %copy-start.8 = (bf16[768,512]{1,0:T(8,128)(2,1)S(1)}, bf16[768,512]{1,0:T(8,128)(2,1)}, u32[]{:S(2)}) copy-start(bf16[768,512]{1,0:T(8,128)(2,1)} %copy-done.7) | copy-start | bytes 2359300
  143.2 2.2 %copy-start.10 = (bf16[512,512]{1,0:T(8,128)(2,1)S(1)}, bf16[512,512]{1,0:T(8,128)(2,1)}, u32[]{:S(2)}) copy-start(bf16[512,512]{1,0:T(8,128)(2,1)} %copy-done.9) | copy-start | bytes 1572868
  143.2 13.6 %collective-permute-start.28 = (bf16[16,4096]{1,0:T(8,128)(2,1)S(1)}, bf16[16,4096]{1,0:T(8,128)(2,1)S(1)}, u32[]{:S(2)}, u32[]{:S(2)}) collective-permute-start(bf16[16,4096]{1,0:T(8,128)(2,1)S(1)} %get-tuple-element.246), channel_id=1, source_target_pairs={{0,8},{1,9},{2,10},{3,11},{4,12},{5,13},{6,14},{7,15},{8,0},{9,1},... | collective-permute-start | bytes 393224 | tf_op jit(solution)/shard_map/ppermute | solution.py:377
  143.2 13.6 %collective-permute-start.31 = (bf16[192,512]{1,0:T(8,128)(2,1)S(1)}, bf16[192,512]{1,0:T(8,128)(2,1)S(1)}, u32[]{:S(2)}, u32[]{:S(2)}) collective-permute-start(bf16[192,512]{1,0:T(8,128)(2,1)S(1)} %get-tuple-element.189), channel_id=1, source_target_pairs={{0,1},{1,0},{2,3},{3,2},{4,5},{5,4},{6,7},{7,6},{8,9},{9,8},{10,11... | collective-permute-start | bytes 589832 | tf_op jit(solution)/shard_map/ppermute | solution.py:377
  143.6 13.3 %collective-permute-start.27 = (bf16[128,2560]{1,0:T(8,128)(2,1)S(1)}, bf16[128,2560]{1,0:T(8,128)(2,1)S(1)}, u32[]{:S(2)}, u32[]{:S(2)}) collective-permute-start(bf16[128,2560]{1,0:T(8,128)(2,1)S(1)} %get-tuple-element.237), channel_id=1, source_target_pairs={{0,1},{1,0},{2,6},{3,7},{4,5},{5,4},{6,2},{7,3},{8,9},{9,8},{10,14... | collective-permute-start | bytes 1966088 | tf_op jit(solution)/shard_map/ppermute | solution.py:382
  157.0 1.7 collective-permute-start.32
  157.0 13.5 %collective-permute-start.33 = (bf16[64,2560]{1,0:T(8,128)(2,1)S(1)}, bf16[64,2560]{1,0:T(8,128)(2,1)S(1)}, u32[]{:S(2)}, u32[]{:S(2)}) collective-permute-start(bf16[64,2560]{1,0:T(8,128)(2,1)S(1)} %get-tuple-element.239), channel_id=1, source_target_pairs={{0,4},{1,5},{2,3},{3,2},{4,0},{5,1},{6,7},{7,6},{8,12},{9,13},{10,... | collective-permute-start | bytes 983048 | tf_op jit(solution)/shard_map/ppermute | solution.py:382
  158.7 11.9 %collective-permute-start.34 = (bf16[128,768]{1,0:T(8,128)(2,1)S(1)}, bf16[128,768]{1,0:T(8,128)(2,1)S(1)}, u32[]{:S(2)}, u32[]{:S(2)}) collective-permute-start(bf16[128,768]{1,0:T(8,128)(2,1)S(1)} %get-tuple-element.243), channel_id=1, source_target_pairs={{0,1},{1,0},{2,6},{3,7},{4,5},{5,4},{6,2},{7,3},{8,9},{9,8},{10,14... | collective-permute-start | bytes 589832 | tf_op jit(solution)/shard_map/ppermute | solution.py:382
  170.6 1.9 collective-permute-start.36
  170.7 17.9 %collective-permute-start.35 = (bf16[256,512]{1,0:T(8,128)(2,1)S(1)}, bf16[256,512]{1,0:T(8,128)(2,1)S(1)}, u32[]{:S(2)}, u32[]{:S(2)}) collective-permute-start(bf16[256,512]{1,0:T(8,128)(2,1)S(1)} %get-tuple-element.210), channel_id=1, source_target_pairs={{0,1},{1,0},{2,3},{3,2},{4,5},{5,4},{6,7},{7,6},{8,9},{9,8},{10,11... | collective-permute-start | bytes 786440 | tf_op jit(solution)/shard_map/ppermute | solution.py:377
  172.5 10.4 %collective-permute-start.37 = (bf16[128,896]{1,0:T(8,128)(2,1)S(1)}, bf16[128,896]{1,0:T(8,128)(2,1)S(1)}, u32[]{:S(2)}, u32[]{:S(2)}) collective-permute-start(bf16[128,896]{1,0:T(8,128)(2,1)S(1)} %get-tuple-element.241), channel_id=1, source_target_pairs={{0,1},{1,0},{2,6},{3,7},{4,5},{5,4},{6,2},{7,3},{8,9},{9,8},{10,14... | collective-permute-start | bytes 688136 | tf_op jit(solution)/shard_map/ppermute | solution.py:382
  174.5 20.2 %collective-permute-start.40 = (bf16[16,2560]{1,0:T(8,128)(2,1)S(1)}, bf16[16,2560]{1,0:T(8,128)(2,1)S(1)}, u32[]{:S(2)}, u32[]{:S(2)}) collective-permute-start(bf16[16,2560]{1,0:T(8,128)(2,1)S(1)} %get-tuple-element.248), channel_id=1, source_target_pairs={{0,24},{1,25},{2,26},{3,27},{4,28},{5,29},{6,30},{7,31},{8,16},{9,... | collective-permute-start | bytes 245768 | tf_op jit(solution)/shard_map/ppermute | solution.py:377
  176.0 23.9 %collective-permute-start.39 = (bf16[16,2560]{1,0:T(8,128)(2,1)S(1)}, bf16[16,2560]{1,0:T(8,128)(2,1)S(1)}, u32[]{:S(2)}, u32[]{:S(2)}) collective-permute-start(bf16[16,2560]{1,0:T(8,128)(2,1)S(1)} %get-tuple-element.249), channel_id=1, source_target_pairs={{0,16},{1,17},{2,18},{3,19},{4,20},{5,21},{6,22},{7,23},{8,24},{9,... | collective-permute-start | bytes 245768 | tf_op jit(solution)/shard_map/ppermute | solution.py:377
  177.9 22.0 %collective-permute-start.38 = (bf16[16,2560]{1,0:T(8,128)(2,1)S(1)}, bf16[16,2560]{1,0:T(8,128)(2,1)S(1)}, u32[]{:S(2)}, u32[]{:S(2)}) collective-permute-start(bf16[16,2560]{1,0:T(8,128)(2,1)S(1)} %get-tuple-element.250), channel_id=1, source_target_pairs={{0,8},{1,9},{2,10},{3,11},{4,12},{5,13},{6,14},{7,15},{8,0},{9,1},... | collective-permute-start | bytes 245768 | tf_op jit(solution)/shard_map/ppermute | solution.py:377
  182.9 4.6 %collective-permute-start.41 = (bf16[64,768]{1,0:T(8,128)(2,1)S(1)}, bf16[64,768]{1,0:T(8,128)(2,1)S(1)}, u32[]{:S(2)}, u32[]{:S(2)}) collective-permute-start(bf16[64,768]{1,0:T(8,128)(2,1)S(1)} %slice_add_fusion.14), channel_id=1, source_target_pairs={{0,4},{1,5},{2,3},{3,2},{4,0},{5,1},{6,7},{7,6},{8,12},{9,13},{10,... | collective-permute-start | bytes 294920 | tf_op jit(solution)/shard_map/ppermute | solution.py:382
  187.5 4.8 %collective-permute-start.42 = (bf16[64,896]{1,0:T(8,128)(2,1)S(1)}, bf16[64,896]{1,0:T(8,128)(2,1)S(1)}, u32[]{:S(2)}, u32[]{:S(2)}) collective-permute-start(bf16[64,896]{1,0:T(8,128)(2,1)S(1)} %slice_add_fusion.13), channel_id=1, source_target_pairs={{0,4},{1,5},{2,3},{3,2},{4,0},{5,1},{6,7},{7,6},{8,12},{9,13},{10,... | collective-permute-start | bytes 344072 | tf_op jit(solution)/shard_map/ppermute | solution.py:382
  192.4 7.5 %collective-permute-start.45 = (bf16[16,1664]{1,0:T(8,128)(2,1)S(1)}, bf16[16,1664]{1,0:T(8,128)(2,1)S(1)}, u32[]{:S(2)}, u32[]{:S(2)}) collective-permute-start(bf16[16,1664]{1,0:T(8,128)(2,1)S(1)} %get-tuple-element.252), channel_id=1, source_target_pairs={{0,24},{1,25},{2,26},{3,27},{4,28},{5,29},{6,30},{7,31},{8,16},{9,... | collective-permute-start | bytes 159752 | tf_op jit(solution)/shard_map/ppermute | solution.py:377
  193.9 6.0 %collective-permute-start.43 = (bf16[16,1664]{1,0:T(8,128)(2,1)S(1)}, bf16[16,1664]{1,0:T(8,128)(2,1)S(1)}, u32[]{:S(2)}, u32[]{:S(2)}) collective-permute-start(bf16[16,1664]{1,0:T(8,128)(2,1)S(1)} %get-tuple-element.254), channel_id=1, source_target_pairs={{0,8},{1,9},{2,10},{3,11},{4,12},{5,13},{6,14},{7,15},{8,0},{9,1},... | collective-permute-start | bytes 159752 | tf_op jit(solution)/shard_map/ppermute | solution.py:377
  194.7 5.2 %collective-permute-start.44 = (bf16[16,1664]{1,0:T(8,128)(2,1)S(1)}, bf16[16,1664]{1,0:T(8,128)(2,1)S(1)}, u32[]{:S(2)}, u32[]{:S(2)}) collective-permute-start(bf16[16,1664]{1,0:T(8,128)(2,1)S(1)} %get-tuple-element.255), channel_id=1, source_target_pairs={{0,16},{1,17},{2,18},{3,19},{4,20},{5,21},{6,22},{7,23},{8,24},{9,... | collective-permute-start | bytes 159752 | tf_op jit(solution)/shard_map/ppermute | solution.py:377
